TPU v7x, 32 devices: a whole 2x2x4 slice. The times are simulated.
32 devices in a mesh: grp: 2 (over y), hid: 4 (over z), ex: 2 (over x), sub: 2 (over core).
Axes of the slice: x: 2, y: 2, z: 4, core: 2. Of those that a mesh axis runs over, the one named last changes fastest.
Arguments:
- cand_grad: bfloat16 [512, 11008], P(('grp', 'ex'), 'hid'), parts along dimension 0, may hold values from -6 to 6
- query_grad: bfloat16 [512, 11008], P(('grp', 'ex'), 'hid'), parts along dimension 0, may hold values from -6 to 6
- cand_act: bfloat16 [512, 4096], P(('grp', 'ex'), 'sub'), parts along dimension 0, may hold values from -6 to 6
- query_act: bfloat16 [512, 4096], P(('grp', 'ex'), 'sub'), parts along dimension 0, may hold values from -6 to 6
- cand_ids: int32 [512], P(('grp', 'ex')), parts along dimension 0, may hold values from 1 to 50279, as said below
- query_ids: int32 [512], P(('grp', 'ex')), parts along dimension 0, may hold values from 1 to 50279, as said below
- cand_offsets: int32 [8], P('grp'), parts along dimension 0, may hold values from 0 to 255, as said below
- basis_g: bfloat16 [11008, 11008], P('hid', ('ex', 'sub')), may hold values from -0.0546875 to 0.0546875
- basis_a: bfloat16 [4096, 4096], P('sub', 'hid'), may hold values from -0.09375 to 0.09375
- eigvals: float32 [11008, 4096], P('ex', 'hid'), may hold values from 0.25 to 4
Outputs:
- scores: float32 [8, 16], P('grp', 'sub'), parts along dimension 0
There are 2 independent parts, one for each index of `grp`. A program takes and returns all parts, laid end to end along the dimension named above; an argument that names none is the same for every part. Nothing has to cross between parts.
Inputs may be any that keep to these rules, and one draw needn't show every extreme that they name: `cand_ids`: token id 1 is padding; all other ids are real tokens. `query_ids`: token id 1 is padding; all other ids are real tokens. cand_offsets[0] is 0 and the offsets rise strictly, so every example holds one or more tokens.
All inputs are finite; a program needn't handle non-finite values.
Results may differ from a plain program's by a relative error of at most 0.0056.
Values may be sent and summed in bfloat16 or wider, within the bound.
No kernel may reach another device: no remote copies, remote signals or barrier semaphores. Data moves between devices by JAX's collectives and lax.ppermute only.
A program may use at most 192 MiB of HBM per device.

v0:
```python
import math

import jax
import jax.numpy as jnp
from jax import lax
from jax.sharding import PartitionSpec as P

D = 4096
FF = 11008
TC_DEV = 128
EX_DEV = 2
QUERIES_HALF = 8
QLEN = 16


pad_token = 1


def per_device(
    cand_grad,
    query_grad,
    cand_act,
    query_act,
    cand_ids,
    query_ids,
    cand_offsets,
    basis_g,
    basis_a,
    eigvals,
):
    cand_rows = cand_grad.shape[0]
    query_rows = query_grad.shape[0]
    local_rows = cand_rows + query_rows
    groups = lax.axis_size("ex")
    keep_rows = (jnp.concatenate([cand_ids, query_ids]) != pad_token).astype(jnp.bfloat16)
    all_grads = jnp.concatenate([cand_grad, query_grad], 0) * keep_rows[:, None]
    all_acts = jnp.concatenate([cand_act, query_act], 0)
    basis_term = jnp.dot(
        lax.all_gather(all_grads, "ex", axis=0, tiled=True),
        basis_g,
        preferred_element_type=jnp.float32,
    )
    summed_grads = lax.psum(basis_term, "hid").astype(jnp.bfloat16)
    eigen_grads = lax.all_gather(summed_grads, "sub", axis=1, tiled=True)
    full_basis, full_acts = (
        lax.all_gather(basis_a, "sub", axis=0, tiled=True),
        lax.all_gather(all_acts, "sub", axis=1, tiled=True),
    )
    eigen_local = jnp.dot(full_acts, full_basis, preferred_element_type=jnp.float32).astype(
        jnp.bfloat16
    )
    eigen_acts = lax.all_gather(eigen_local, "ex", axis=0, tiled=True)
    grad_blocks = eigen_grads.reshape(groups, local_rows, eigen_grads.shape[1])
    act_blocks = eigen_acts.reshape(groups, local_rows, eigen_acts.shape[1])
    cand_eigen_grad = grad_blocks[:, :cand_rows].reshape(groups * cand_rows, eigen_grads.shape[1])
    query_eigen_grad = grad_blocks[:, cand_rows:].reshape(groups * query_rows, eigen_grads.shape[1])
    cand_eigen_act = act_blocks[:, :cand_rows].reshape(groups * cand_rows, eigen_acts.shape[1])
    query_eigen_act = act_blocks[:, cand_rows:].reshape(groups * query_rows, eigen_acts.shape[1])
    half_tokens = groups * query_rows // lax.axis_size("sub")
    first_token = lax.axis_index("sub") * half_tokens
    query_grad_half = lax.dynamic_slice_in_dim(query_eigen_grad, first_token, half_tokens, 0)
    query_act_half = lax.dynamic_slice_in_dim(query_eigen_act, first_token, half_tokens, 0)
    query_grad_half = query_grad_half.reshape(QUERIES_HALF, QLEN, eigen_grads.shape[1])
    query_act_half = query_act_half.reshape(QUERIES_HALF, QLEN, eigen_acts.shape[1])
    cand_wide = cand_eigen_act.astype(jnp.float32)

    def one_query(query_pair):
        grad_block, act_block = query_pair
        outer_sum = jnp.dot(grad_block.T, act_block, preferred_element_type=jnp.float32)
        precond = (outer_sum / eigvals).astype(jnp.bfloat16)
        image_rows = jnp.dot(cand_eigen_grad, precond, preferred_element_type=jnp.float32)
        return jnp.sum(image_rows * cand_wide, axis=1)

    token_scores = lax.map(one_query, (query_grad_half, query_act_half))
    total_cand = groups * cand_rows
    positions = jnp.arange(total_cand, dtype=jnp.int32)
    example_ends = jnp.concatenate([cand_offsets[1:], jnp.full((1,), total_cand, jnp.int32)])
    member = (
        (positions[None, :] >= cand_offsets[:, None]) & (positions[None, :] < example_ends[:, None])
    ).astype(jnp.float32)
    partial_value = jnp.dot(member, token_scores.T, precision=lax.Precision.HIGHEST)
    factor = 1.0 / math.sqrt(FF * D * QLEN * (TC_DEV // EX_DEV))
    return lax.psum(partial_value, ("hid", "ex")) * factor


def solution(mesh):
    return jax.shard_map(
        per_device,
        mesh=mesh,
        in_specs=(
            P(("grp", "ex"), "hid"),
            P(("grp", "ex"), "hid"),
            P(("grp", "ex"), "sub"),
            P(("grp", "ex"), "sub"),
            P(("grp", "ex")),
            P(("grp", "ex")),
            P("grp"),
            P("hid", ("ex", "sub")),
            P("sub", "hid"),
            P("ex", "hid"),
        ),
        out_specs=P("grp", "sub"),
        check_vma=False,
    )
```

profile of v0, /device:TPU:0, one launch (start us, length us, event | category | flops | bytes accessed | tf_op | source)
XLA Modules:
  0.0 461.6 jit_solution(9645096532736747845)
XLA Ops:
  6.5 0.0 copy-start
  6.5 0.0 copy-start.1
  6.5 0.0 all-gather.6.cloned.1.call-start
  6.5 0.8 compare_convert_fusion
  7.3 2.8 maximum_multiply_fusion
  10.1 0.0 all-gather.6.cloned.1.call-update
  10.1 0.0 all-gather.10.cloned.1.call-start
  10.2 0.0 copy-done
  10.2 0.0 copy-done.1
  10.2 1.0 pad_maximum_fusion
  11.3 0.0 all-gather.10.cloned.1.call-update
  11.3 0.0 all-gather.12.cloned.1.call-start
  11.3 0.7 all-gather.12.cloned.1.call-update
  12.0 0.0 all-gather.8.cloned.1.call-start
  12.1 42.1 %all-gather.6.cloned.1.call-done = bf16[512,2752]{0,1:T(8,128)(2,1)} async-done(((bf16[256,2752]{0,1:T(8,128)(2,1)}), bf16[512,2752]{0,1:T(8,128)(2,1)}) %all-gather.6.cloned.1.call-update) | async-done | bytes 2818064 | tf_op jit(solution)/shard_map/all_gather | solution.py:39
  54.2 14.3 %fusion.23 = f32[512,2752]{0,1:T(8,128)} fusion(bf16[512,2752]{0,1:T(8,128)(2,1)} %all-gather.6.cloned.1.call-done, bf16[2752,2752]{1,0:T(8,128)(2,1)} %param.19), kind=kOutput, calls=%fused_computation.28 | convolution fusion | flops 7755268096 | bytes 23601152 | tf_op jit(solution)/shard_map/dot_general | solution.py:38
  68.5 196.2 %all-reduce.1 = bf16[512,2752]{0,1:T(8,128)(2,1)} all-reduce(f32[512,2752]{0,1:T(8,128)} %fusion.23), channel_id=1, replica_groups=mesh['grp'=2,'hid'=4,'ex'=2,'sub'=2] {'hid'}, use_global_device_ids=true, to_apply=%region_0.0 | all-reduce | flops 1409024 | bytes 8454144 | tf_op jit(solution)/shard_map/psum | solution.py:43
  264.7 0.0 copy-start.2
  264.7 0.0 all-gather.8.cloned.1.call-update
  264.7 0.2 all-gather.14.cloned.1.call-start
  264.9 0.4 copy-done.2
  265.3 0.1 slice.15
  265.4 0.1 pad_add_fusion
  265.5 7.9 %convolution_convert_fusion = bf16[256,1024]{1,0:T(8,128)(2,1)} fusion(bf16[256,4096]{1,0:T(8,128)(2,1)} %all-gather.10.cloned.1.call-done, bf16[4096,1024]{1,0:T(8,128)(2,1)} %all-gather.12.cloned.1.call-done), kind=kOutput, calls=%fused_computation.12 | convolution fusion | flops 2147745792 | bytes 11010048 | tf_op jit(solution)/shard_map/dot_general | solution.py:49
  273.4 0.0 all-gather.14.cloned.1.call-update
  273.4 4.5 all-gather.8.cloned.1.call-done
  277.9 12.5 %reshape.42 = bf16[2,256,5504]{1,0,2:T(2,128)(2,1)} reshape(bf16[512,5504]{0,1:T(8,128)(2,1)} %all-gather.8.cloned.1.call-done) | data formatting | bytes 11272192 | tf_op jit(solution)/shard_map/reshape | solution.py:53
  290.3 7.5 %fusion.21 = (bf16[2,128,5504]{1,0,2:T(2,128)(2,1)}, bf16[2,128,5504]{1,0,2:T(2,128)(2,1)S(1)}) fusion(bf16[2,256,5504]{1,0,2:T(2,128)(2,1)} %reshape.42), kind=kLoop, calls=%fused_computation.26 | loop fusion | bytes 11272192 | tf_op jit(solution)/shard_map/slice | solution.py:55
  297.8 8.0 %copy.12 = bf16[2,128,5504]{2,1,0:T(8,128)(2,1)} copy(bf16[2,128,5504]{1,0,2:T(2,128)(2,1)} %get-tuple-element.57) | data formatting | bytes 5636096 | tf_op jit(solution)/shard_map/slice | solution.py:55
  305.8 5.6 %copy.14 = bf16[2,128,5504]{2,1,0:T(8,128)(2,1)} copy(bf16[2,128,5504]{1,0,2:T(2,128)(2,1)S(1)} %get-tuple-element.58) | data formatting | bytes 5636096 | tf_op jit(solution)/shard_map/reshape | solution.py:56
  311.5 1.4 constant_dynamic-slice_fusion.1
  312.9 0.0 all-gather.14.cloned.1.call-done
  312.9 1.3 fusion.22
  314.2 0.7 constant_dynamic-slice_fusion
  315.0 0.1 bitcast_convert_fusion
  315.1 0.3 copy.15
  315.4 117.3 %while.10 = (s32[]{:T(128)}, f32[8,256]{1,0:T(8,128)S(1)}, bf16[8,16,5504]{2,1,0:T(8,128)(2,1)S(1)}, bf16[8,16,1024]{2,1,0:T(8,128)(2,1)}, f32[5504,1024]{1,0:T(...) while((s32[]{:T(128)}, f32[8,256]{1,0:T(8,128)S(1)}, ...), condition=%wide.region_3.4_spmd, body=%wide.region_1.3_spmd.sunk | while | flops 3077832448 | bytes 26624104 | solution.py:74
  315.5 14.6 %fusion.37 = f32[256]{0:T(256)S(1)} fusion(f32[256,1024]{0,1:T(8,128)S(1)} %get-tuple-element.128, bf16[256,5504]{1,0:T(8,128)(2,1)} %get-tuple-element.127, f32[5504,1024]{1,0:T(8,128)} %get-tuple-element.126, bf16[8,16,5504]{2,1,0:T(8,128)(2,1)S(1)} %get-tuple-element.124, s32[]{:T(128)S(6)} %copy.20, bf16[8,16,1024]{2,1,0:T(8,128)(2,1)} %get-tuple-element.125), kind=kOutput, calls=%fused_computation.5.clone.1 | convolution fusion | flops 3077832448 | bytes 26621952 | tf_op jit(solution)/shard_map/while/body/eval_jaxpr/dot_general | solution.py:71
  330.1 14.6 %fusion.37 = f32[256]{0:T(256)S(1)} fusion(f32[256,1024]{0,1:T(8,128)S(1)} %get-tuple-element.128, bf16[256,5504]{1,0:T(8,128)(2,1)} %get-tuple-element.127, f32[5504,1024]{1,0:T(8,128)} %get-tuple-element.126, bf16[8,16,5504]{2,1,0:T(8,128)(2,1)S(1)} %get-tuple-element.124, s32[]{:T(128)S(6)} %copy.20, bf16[8,16,1024]{2,1,0:T(8,128)(2,1)} %get-tuple-element.125), kind=kOutput, calls=%fused_computation.5.clone.1 | convolution fusion | flops 3077832448 | bytes 26621952 | tf_op jit(solution)/shard_map/while/body/eval_jaxpr/dot_general | solution.py:71
  344.8 14.6 %fusion.37 = f32[256]{0:T(256)S(1)} fusion(f32[256,1024]{0,1:T(8,128)S(1)} %get-tuple-element.128, bf16[256,5504]{1,0:T(8,128)(2,1)} %get-tuple-element.127, f32[5504,1024]{1,0:T(8,128)} %get-tuple-element.126, bf16[8,16,5504]{2,1,0:T(8,128)(2,1)S(1)} %get-tuple-element.124, s32[]{:T(128)S(6)} %copy.20, bf16[8,16,1024]{2,1,0:T(8,128)(2,1)} %get-tuple-element.125), kind=kOutput, calls=%fused_computation.5.clone.1 | convolution fusion | flops 3077832448 | bytes 26621952 | tf_op jit(solution)/shard_map/while/body/eval_jaxpr/dot_general | solution.py:71
  359.4 14.6 %fusion.37 = f32[256]{0:T(256)S(1)} fusion(f32[256,1024]{0,1:T(8,128)S(1)} %get-tuple-element.128, bf16[256,5504]{1,0:T(8,128)(2,1)} %get-tuple-element.127, f32[5504,1024]{1,0:T(8,128)} %get-tuple-element.126, bf16[8,16,5504]{2,1,0:T(8,128)(2,1)S(1)} %get-tuple-element.124, s32[]{:T(128)S(6)} %copy.20, bf16[8,16,1024]{2,1,0:T(8,128)(2,1)} %get-tuple-element.125), kind=kOutput, calls=%fused_computation.5.clone.1 | convolution fusion | flops 3077832448 | bytes 26621952 | tf_op jit(solution)/shard_map/while/body/eval_jaxpr/dot_general | solution.py:71
  374.1 14.6 %fusion.37 = f32[256]{0:T(256)S(1)} fusion(f32[256,1024]{0,1:T(8,128)S(1)} %get-tuple-element.128, bf16[256,5504]{1,0:T(8,128)(2,1)} %get-tuple-element.127, f32[5504,1024]{1,0:T(8,128)} %get-tuple-element.126, bf16[8,16,5504]{2,1,0:T(8,128)(2,1)S(1)} %get-tuple-element.124, s32[]{:T(128)S(6)} %copy.20, bf16[8,16,1024]{2,1,0:T(8,128)(2,1)} %get-tuple-element.125), kind=kOutput, calls=%fused_computation.5.clone.1 | convolution fusion | flops 3077832448 | bytes 26621952 | tf_op jit(solution)/shard_map/while/body/eval_jaxpr/dot_general | solution.py:71
  388.8 14.6 %fusion.37 = f32[256]{0:T(256)S(1)} fusion(f32[256,1024]{0,1:T(8,128)S(1)} %get-tuple-element.128, bf16[256,5504]{1,0:T(8,128)(2,1)} %get-tuple-element.127, f32[5504,1024]{1,0:T(8,128)} %get-tuple-element.126, bf16[8,16,5504]{2,1,0:T(8,128)(2,1)S(1)} %get-tuple-element.124, s32[]{:T(128)S(6)} %copy.20, bf16[8,16,1024]{2,1,0:T(8,128)(2,1)} %get-tuple-element.125), kind=kOutput, calls=%fused_computation.5.clone.1 | convolution fusion | flops 3077832448 | bytes 26621952 | tf_op jit(solution)/shard_map/while/body/eval_jaxpr/dot_general | solution.py:71
  403.4 14.6 %fusion.37 = f32[256]{0:T(256)S(1)} fusion(f32[256,1024]{0,1:T(8,128)S(1)} %get-tuple-element.128, bf16[256,5504]{1,0:T(8,128)(2,1)} %get-tuple-element.127, f32[5504,1024]{1,0:T(8,128)} %get-tuple-element.126, bf16[8,16,5504]{2,1,0:T(8,128)(2,1)S(1)} %get-tuple-element.124, s32[]{:T(128)S(6)} %copy.20, bf16[8,16,1024]{2,1,0:T(8,128)(2,1)} %get-tuple-element.125), kind=kOutput, calls=%fused_computation.5.clone.1 | convolution fusion | flops 3077832448 | bytes 26621952 | tf_op jit(solution)/shard_map/while/body/eval_jaxpr/dot_general | solution.py:71
  418.1 14.6 %fusion.37 = f32[256]{0:T(256)S(1)} fusion(f32[256,1024]{0,1:T(8,128)S(1)} %get-tuple-element.128, bf16[256,5504]{1,0:T(8,128)(2,1)} %get-tuple-element.127, f32[5504,1024]{1,0:T(8,128)} %get-tuple-element.126, bf16[8,16,5504]{2,1,0:T(8,128)(2,1)S(1)} %get-tuple-element.124, s32[]{:T(128)S(6)} %copy.20, bf16[8,16,1024]{2,1,0:T(8,128)(2,1)} %get-tuple-element.125), kind=kOutput, calls=%fused_computation.5.clone.1 | convolution fusion | flops 3077832448 | bytes 26621952 | tf_op jit(solution)/shard_map/while/body/eval_jaxpr/dot_general | solution.py:71
  432.7 0.2 fusion.17
  432.9 21.6 %psum.15 = f32[4,8]{1,0:T(4,128)S(1)} all-reduce(f32[4,8]{1,0:T(4,128)S(1)} %fusion.17), channel_id=1, replica_groups=mesh['grp'=2,'hid'=4,'ex'=2,'sub'=2] {'hid','ex'}, use_global_device_ids=true, to_apply=%region_4.5 | all-reduce | flops 32 | bytes 256 | tf_op jit(solution)/shard_map/psum | solution.py:83
  454.5 0.6 broadcast_multiply_fusion
  (11 shorter events, 0.3 us)
Async XLA Ops:
  6.5 3.7 copy-start
  6.5 3.7 copy-start.1
  6.5 47.7 %all-gather.6.cloned.1.call-start = ((), (), s32[]{:S(2)}) async-start(), calls=%async_computation | async-start | bytes 4227072 | tf_op jit(solution)/shard_map/all_gather | solution.py:39
  10.1 255.3 %all-gather.10.cloned.1.call-start = ((), (), s32[]{:S(2)}) async-start(), calls=%async_computation.2 | async-start | bytes 3145728 | tf_op jit(solution)/shard_map/all_gather | solution.py:47
  11.3 254.2 %all-gather.12.cloned.1.call-start = ((), (), s32[]{:S(2)}) async-start(), calls=%async_computation.3 | async-start | bytes 12582912 | tf_op jit(solution)/shard_map/all_gather | solution.py:46
  12.0 265.9 %all-gather.8.cloned.1.call-start = ((), (), s32[]{:S(2)}) async-start(), calls=%async_computation.1 | async-start | bytes 8454144 | tf_op jit(solution)/shard_map/all_gather | solution.py:44
  264.7 0.7 copy-start.2
  264.7 48.2 %all-gather.14.cloned.1.call-start = ((), (), s32[]{:S(2)}) async-start(), calls=%async_computation.4 | async-start | bytes 1572864 | tf_op jit(solution)/shard_map/all_gather | solution.py:52
Sparse Core Ops, SparseCore 0:
  10.3 43.8 all-gather.5
  55.7 10.5 all-gather.9
  67.9 21.0 all-gather.11
  264.8 13.0 all-gather.7
  279.3 22.4 all-gather.13
where the time goes:
time: 462 us
  blocking collectives  218 us (47%)
  matrix products  139 us (30%)
  waiting for transfers between devices  47.4 us (10%)
  local copies, waits for them, and re-layouts  38.2 us (8%)
  between operations  13.2 us (3%)
  other arithmetic  5.42 us (1%)
    psum x1, blocking collectives, per_device(): summed_grads = lax.psum(basis_term, 'hid').astype(jnp.bfloat16)  196 us
    dot_general x8, matrix products, one_query(): jnp.dot(cand_eigen_grad, precond, preferred_element_type=jnp.float32)  117 us
    all_gather x1, waiting for transfers between devices, per_device(): lax.all_gather(all_grads, 'ex', axis=0, tiled=True)  42.1 us
    psum x1, blocking collectives, per_device(): return lax.psum(partial_value, ('hid', 'ex')) * factor  21.6 us
    slice x2, local copies, waits for them, and re-layouts, per_device(): grad_blocks[:, :cand_rows].reshape(groups * cand_rows, eigen_grads.shape[1])  15.5 us
    dot_general x1, matrix products, per_device(): jnp.dot(lax.all_gather(all_grads, 'ex', axis=0, tiled=True), basis_g, pre...  14.3 us
    reshape x1, local copies, waits for them, and re-layouts, per_device(): grad_blocks = eigen_grads.reshape(groups, local_rows, eigen_grads.shape[1])  12.5 us
  transfers between devices with their start and end apart: 5, of which 2 were waited for; matrix products, arithmetic and copies ran while one was open for 13% of the time, Pallas kernels for 0%

commit v1 on v0

v1 whole, which is shorter than its diff:
```python
import functools
import math

import jax
import jax.numpy as jnp
from jax import lax
from jax.experimental import pallas as pl
from jax.experimental.pallas import tpu as pltpu
from jax.sharding import PartitionSpec as P

D = 4096
FF = 11008
TC_DEV = 128
EX_DEV = 2
QLEN = 16
PAD = 1
VMEM_BYTES = 48 * 1024 * 1024
CHUNKS = (256, 640, 640, 640, 384)


def chunk_bounds(total):
    bounds = []
    start = 0
    for width in CHUNKS:
        if start + width < total:
            bounds.append((start, width))
            start += width
    bounds.append((start, total - start))
    return bounds


def project_kernel(n_first, n_second, *refs):
    firsts = refs[:n_first]
    seconds = refs[n_first : n_first + n_second]
    basis_ref, out_ref, rows_ref = refs[n_first + n_second :]
    split = firsts[0].shape[0]

    @pl.when(pl.program_id(0) == 0)
    def _():
        rows_ref[:split] = functools.reduce(lambda a, b: a + b, [r[...] for r in firsts])
        rows_ref[split:] = functools.reduce(lambda a, b: a + b, [r[...] for r in seconds])

    out_ref[...] = jnp.dot(
        rows_ref[...], basis_ref[...], preferred_element_type=jnp.float32
    ).astype(out_ref.dtype)


def project(firsts, seconds, basis, start, width, out_type):
    rows = firsts[0].shape[0] + seconds[0].shape[0]
    depth = basis.shape[0]
    tile = 256 if width % 256 == 0 and start % 256 == 0 else 128
    tiles = pl.cdiv(width, tile)
    first_tile = start // tile
    whole = lambda a: pl.BlockSpec(a.shape, lambda i: (0, 0))
    return pl.pallas_call(
        functools.partial(project_kernel, len(firsts), len(seconds)),
        grid=(tiles,),
        in_specs=[whole(a) for a in firsts]
        + [whole(a) for a in seconds]
        + [pl.BlockSpec((depth, tile), lambda i: (0, first_tile + i))],
        out_specs=pl.BlockSpec((rows, tile), lambda i: (0, i)),
        out_shape=jax.ShapeDtypeStruct((rows, width), out_type),
        scratch_shapes=[pltpu.VMEM((rows, depth), basis.dtype)],
        compiler_params=pltpu.CompilerParams(vmem_limit_bytes=VMEM_BYTES),
        cost_estimate=pl.CostEstimate(
            flops=2 * rows * depth * width,
            bytes_accessed=2 * (rows * depth + depth * width + rows * width),
            transcendentals=0,
        ),
        name="project",
    )(*firsts, *seconds, basis)


def score_kernel(blocks, cand_rows, examples, at_ref, *refs):
    del at_ref
    sums = []
    place = 0
    for terms in blocks:
        parts = [r[...].astype(jnp.float32) for r in refs[place : place + terms]]
        sums.append(functools.reduce(lambda a, b: a + b, parts))
        place += terms
    eig_ref, cand_act_ref, query_act_ref, out_ref = refs[place:]
    cand = jnp.concatenate([b[:cand_rows] for b in sums], 0).T.astype(jnp.bfloat16)
    query = (
        jnp.concatenate([b[cand_rows:] for b in sums], 0)
        .astype(jnp.bfloat16)
        .astype(jnp.float32)
        .T
    )
    inverse = 1.0 / eig_ref[...]
    features = inverse.shape[1]
    for k in range(examples):
        outer = jnp.dot(
            cand,
            cand_act_ref[:, k * features : (k + 1) * features],
            preferred_element_type=jnp.float32,
        )
        weights = (outer * inverse).astype(jnp.bfloat16)
        image = lax.dot_general(
            weights,
            query_act_ref[...],
            (((1,), (1,)), ((), ())),
            preferred_element_type=jnp.float32,
        )
        out_ref[k : k + 1, :] = jnp.sum(image * query, axis=0, keepdims=True)


def score_chunk(blocks, cand_rows, eigvals, first_row, width, cand_acts, query_acts, examples):
    flat = [a for block in blocks for a in block]
    tokens = query_acts.shape[0]
    features = eigvals.shape[1]
    whole = lambda a: pl.BlockSpec(a.shape, lambda i, at: (0, 0))
    return pl.pallas_call(
        functools.partial(score_kernel, tuple(len(b) for b in blocks), cand_rows, examples),
        grid_spec=pltpu.PrefetchScalarGridSpec(
            num_scalar_prefetch=1,
            grid=(1,),
            in_specs=[whole(a) for a in flat]
            + [
                pl.BlockSpec(
                    (pl.Element(width), pl.Element(features)), lambda i, at: (pl.multiple_of(at[0], 8), 0)
                ),
                whole(cand_acts),
                whole(query_acts),
            ],
            out_specs=pl.BlockSpec((examples, tokens), lambda i, at: (0, 0)),
        ),
        out_shape=jax.ShapeDtypeStruct((examples, tokens), jnp.float32),
        compiler_params=pltpu.CompilerParams(vmem_limit_bytes=VMEM_BYTES),
        cost_estimate=pl.CostEstimate(
            flops=4 * width * features * tokens * examples,
            bytes_accessed=4 * width * features + 2 * cand_acts.size + 2 * query_acts.size,
            transcendentals=0,
        ),
        name="score",
    )(jnp.reshape(first_row, (1,)).astype(jnp.int32), *flat, eigvals, cand_acts, query_acts)


def line_sum_terms(own, axis, link_type):
    size = lax.axis_size(axis)
    terms = [own]
    last = None
    for hop in range(1, size):
        send = own if last is None else own.astype(jnp.float32) + last.astype(jnp.float32)
        pairs = [(hop - 1, hop), (size - hop, size - hop - 1)]
        last = lax.ppermute(send.astype(link_type), axis, pairs)
        terms.append(last)
    return terms


def small_sum(value, axes):
    size = lax.axis_size(axes)
    if size > 4:
        return lax.psum(value, axes)
    terms = [value]
    for other in range(1, size):
        terms.append(lax.ppermute(value, axes, [(i, i ^ other) for i in range(size)]))
    while len(terms) > 1:
        terms = [a + b for a, b in zip(terms[::2], terms[1::2])]
    return terms[0]


def per_device(
    cand_grad,
    query_grad,
    cand_act,
    query_act,
    cand_ids,
    query_ids,
    cand_offsets,
    basis_g,
    basis_a,
    eigvals,
):
    cand_rows = cand_grad.shape[0]
    query_rows = query_grad.shape[0]
    groups = lax.axis_size("ex")
    halves = lax.axis_size("sub")
    ex = lax.axis_index("ex")
    sub = lax.axis_index("sub")
    directions = basis_g.shape[1]
    features = basis_a.shape[1]
    examples = cand_offsets.shape[0]
    link_type = jnp.bfloat16 if lax.axis_size("hid") <= 4 else jnp.float32
    paired = groups == 2 and halves == 2 and cand_rows == query_rows
    both = ("ex", "sub")

    if paired:
        cand_over = lax.ppermute(cand_grad, both, [(0, 2), (2, 0)])
        query_over = lax.ppermute(query_grad, both, [(1, 3), (3, 1)])
        cand_across = lax.ppermute(cand_over, both, [(0, 1), (2, 3)])
        query_across = lax.ppermute(query_over, both, [(1, 0), (3, 2)])
        sources = [
            ([cand_grad], [query_grad]),
            ([cand_over, cand_across], [query_over, query_across]),
        ]
        block_cand = cand_rows
    else:
        gather = lambda a: lax.all_gather(a, "ex", axis=0, tiled=True)
        sources = [([gather(cand_grad)], [gather(query_grad)])]
        block_cand = cand_rows * groups

    bounds = chunk_bounds(directions)
    block_terms = []
    for firsts, seconds in sources:
        block_terms.append(
            [
                line_sum_terms(
                    project(firsts, seconds, basis_g, start, width, link_type), "hid", link_type
                )
                for start, width in bounds
            ]
        )

    keep = (jnp.concatenate([cand_ids, query_ids]) != PAD).astype(jnp.bfloat16)
    act_share = project([cand_act], [query_act], basis_a, 0, features, jnp.float32)
    if paired:
        to_other = jnp.where(sub == 0, act_share[cand_rows:], act_share[:cand_rows])
        mine = jnp.where(sub == 0, act_share[:cand_rows], act_share[cand_rows:])
        keep_mine = jnp.where(sub == 0, keep[:cand_rows], keep[cand_rows:])
        came = lax.ppermute(to_other, "sub", [(0, 1), (1, 0)])
        half_own = (mine + came).astype(jnp.bfloat16) * keep_mine[:, None]
        half_over = lax.ppermute(half_own, "ex", [(0, 1), (1, 0)])
        kept = jnp.concatenate([half_own, half_over], 0)
        swapped = lax.ppermute(kept, "sub", [(0, 1), (1, 0)])
        cand_eigen_act = jnp.where(sub == 0, kept, swapped)
        query_eigen_act = jnp.where(sub == 0, swapped, kept)
        span = jnp.arange(cand_rows, dtype=jnp.int32)
        positions = jnp.concatenate([ex * cand_rows + span, (1 - ex) * cand_rows + span])
    else:
        eigen = lax.psum(act_share, "sub").astype(jnp.bfloat16) * keep[:, None]
        cand_eigen_act = lax.all_gather(eigen[:cand_rows], "ex", axis=0, tiled=True)
        query_eigen_act = lax.all_gather(eigen[cand_rows:], "ex", axis=0, tiled=True)
        positions = jnp.arange(groups * cand_rows, dtype=jnp.int32)

    total_cand = groups * cand_rows
    example_ends = jnp.concatenate([cand_offsets[1:], jnp.full((1,), total_cand, jnp.int32)])
    member = (positions[:, None] >= cand_offsets[None, :]) & (
        positions[:, None] < example_ends[None, :]
    )
    split_acts = (
        member.astype(jnp.bfloat16)[:, :, None] * cand_eigen_act[:, None, :]
    ).reshape(total_cand, examples * features)

    token_scores = 0.0
    for c, (start, width) in enumerate(bounds):
        token_scores += score_chunk(
            [terms[c] for terms in block_terms],
            block_cand,
            eigvals,
            sub * directions + start,
            width,
            split_acts,
            query_eigen_act,
            examples,
        )
    queries = groups * query_rows // QLEN
    partial_value = token_scores.reshape(examples, queries, QLEN).sum(2)
    if paired:
        turned = jnp.roll(partial_value, queries // 2, axis=1)
        partial_value = jnp.where(ex == 0, partial_value, turned)
    total = small_sum(small_sum(partial_value, both), "hid")
    mine = lax.dynamic_slice_in_dim(total, sub * (queries // halves), queries // halves, 1)
    factor = 1.0 / math.sqrt(FF * D * QLEN * (TC_DEV // EX_DEV))
    return mine * factor


def solution(mesh):
    return jax.shard_map(
        per_device,
        mesh=mesh,
        in_specs=(
            P(("grp", "ex"), "hid"),
            P(("grp", "ex"), "hid"),
            P(("grp", "ex"), "sub"),
            P(("grp", "ex"), "sub"),
            P(("grp", "ex")),
            P(("grp", "ex")),
            P("grp"),
            P("hid", ("ex", "sub")),
            P("sub", "hid"),
            P("ex", "hid"),
        ),
        out_specs=P("grp", "sub"),
        check_vma=False,
    )
```

time: 462 us -> 278 us (0.60)
  blocking collectives: 218 us -> 0 us
  matrix products: 139 us -> 0 us
  starting transfers between devices: 0.35 us -> 94.4 us
  Pallas kernels: 0 us -> 75.1 us
  waiting for transfers between devices: 47.4 us -> 73.7 us
  local copies, waits for them, and re-layouts: 38.2 us -> 17 us
  between operations: 13.2 us -> 1.3 us
  other arithmetic: 5.42 us -> 14 us
    psum x2 -> x0, blocking collectives: 218 us -> none  [the longest x1 196 us: per_device(): summed_grads = lax.psum(basis_term, 'hid').astype(jnp.bfloat16)]
    dot_general x11 -> x0, matrix products: 139 us -> none  [the longest x8 117 us: one_query(): jnp.dot(cand_eigen_grad, precond, preferred_element_type=jnp.float32)]
    ppermute x0 -> x49, starting transfers between devices: none -> 94.4 us  [the longest x36 76.4 us: line_sum_terms(): last = lax.ppermute(send.astype(link_type), axis, pairs)]
    pallas_call x0 -> x19, Pallas kernels: none -> 75.1 us  [the longest x13 50.6 us: project(): pl.pallas_call(functools.partial(project_kernel, len(firsts), len(seconds...]
    ppermute x0 -> x49, waiting for transfers between devices: none -> 73.7 us  [the longest x36 63.7 us: line_sum_terms(): last = lax.ppermute(send.astype(link_type), axis, pairs)]
    all_gather x5 -> x0, waiting for transfers between devices: 46.6 us -> none  [the longest x1 42.1 us: per_device(): lax.all_gather(all_grads, 'ex', axis=0, tiled=True)]
    reshape x2 -> x1, local copies, waits for them, and re-layouts: 18.1 us -> 0.08 us  [per_device(): partial_value = token_scores.reshape(examples, queries, QLEN).sum(2)]
    slice x3 -> x1, local copies, waits for them, and re-layouts: 16.8 us -> 0.07 us  [per_device(): turned = jnp.roll(partial_value, queries // 2, axis=1)]
  transfers between devices with their start and end apart: 5 -> 49, of which waited for: 2 -> 16; matrix products, arithmetic and copies ran while one was open for 13% -> 9% of each run, Pallas kernels for 0% -> 24%
where the time goes in v1:
time: 278 us; the launch traced here: 276 us
  starting transfers between devices  94.4 us (34%)
  Pallas kernels  75.1 us (27%)
  waiting for transfers between devices  73.7 us (27%)
  local copies, waits for them, and re-layouts  17 us (6%)
  other arithmetic  14 us (5%)
    ppermute x36, starting transfers between devices, line_sum_terms(): last = lax.ppermute(send.astype(link_type), axis, pairs)  76.4 us
    ppermute x36, waiting for transfers between devices, line_sum_terms(): last = lax.ppermute(send.astype(link_type), axis, pairs)  63.7 us
    pallas_call x13, Pallas kernels, project(): pl.pallas_call(functools.partial(project_kernel, len(firsts), len(seconds...  50.6 us
    pallas_call x6, Pallas kernels, score_chunk(): pl.pallas_call(functools.partial(score_kernel, tuple((len(b) for b in blo...  24.6 us
    unnamed x89, local copies, waits for them, and re-layouts  8.81 us
    convert_element_type x24, other arithmetic, line_sum_terms(): last = lax.ppermute(send.astype(link_type), axis, pairs)  8.62 us
    ppermute x6, starting transfers between devices, small_sum(): lax.ppermute(value, axes, [(i, i ^ other) for i in range(size)])  6.25 us
    ppermute x6, waiting for transfers between devices, small_sum(): lax.ppermute(value, axes, [(i, i ^ other) for i in range(size)])  5.83 us
  transfers between devices with their start and end apart: 49, of which 16 were waited for; matrix products, arithmetic and copies ran while one was open for 9% of the time, Pallas kernels for 24%

profile of v1, /device:TPU:0, one launch (start us, length us, event | category | flops | bytes accessed | tf_op | source)
XLA Modules:
  0.0 275.6 jit_solution(9651209285437254206)
XLA Ops:
  2.1 4.0 %project.15 = f32[256,1024]{1,0:T(8,128)S(1)} custom-call(bf16[128,2048]{1,0:T(8,128)(2,1)S(1)} %copy-done.33, bf16[128,2048]{1,0:T(8,128)(2,1)S(1)} %copy-done.34, bf16[2048,1024]{1,0:T(8,128)(2,1)} %refs_2_.8), custom_call_target="tpu_custom_call" | custom-call | flops 1073741824 | bytes 5767168 | tf_op jit(solution)/shard_map/project/pallas_call | solution.py:55
  7.4 4.4 %collective-permute-start.3 = (bf16[128,2752]{0,1:T(8,128)(2,1)}, bf16[128,2752]{0,1:T(8,128)(2,1)}, u32[]{:S(2)}, u32[]{:S(2)}) collective-permute-start(bf16[128,2752]{0,1:T(8,128)(2,1)} %param.10), channel_id=1, source_target_pairs={{0,2},{2,0},{4,6},{6,4},{8,10},{10,8},{12,14},{14,12},{16,18},{18,... | collective-permute-start | bytes 2113544 | tf_op jit(solution)/shard_map/ppermute | solution.py:189
  11.8 1.5 collective-permute-start.5
  16.1 5.1 %project.16.refs_0_ = bf16[256,640]{1,0:T(8,128)(2,1)S(1)} custom-call(bf16[128,2752]{1,0:T(8,128)(2,1)S(1)} %copy.61.refs_0_, bf16[128,2752]{1,0:T(8,128)(2,1)S(1)} %copy.62.refs_1_, bf16[2752,2752]{1,0:T(8,128)(2,1)} %refs_4_.11), custom_call_target="tpu_custom_call" | custom-call | flops 901775360 | bytes 5259264 | tf_op jit(solution)/shard_map/project/pallas_call | solution.py:55
  21.1 4.3 %collective-permute-start.13 = (bf16[256,640]{1,0:T(8,128)(2,1)S(1)}, bf16[256,640]{1,0:T(8,128)(2,1)}, u32[]{:S(2)}, u32[]{:S(2)}) collective-permute-start(bf16[256,640]{1,0:T(8,128)(2,1)S(1)} %project.16.refs_0_), channel_id=1, source_target_pairs={{0,4},{12,8},{1,5},{13,9},{2,6},{14,10},{3,7},{15,11},{16,20},{28,... | collective-permute-start | bytes 983048 | tf_op jit(solution)/shard_map/ppermute | solution.py:146
  25.4 2.9 %project.24.refs_0_ = bf16[256,192]{1,0:T(8,128)(2,1)} custom-call(bf16[128,2752]{1,0:T(8,128)(2,1)S(1)} %copy.61.refs_0_, bf16[128,2752]{1,0:T(8,128)(2,1)S(1)} %copy.62.refs_1_, bf16[2752,2752]{1,0:T(8,128)(2,1)} %refs_4_.11), custom_call_target="tpu_custom_call" | custom-call | flops 270532608 | bytes 2564096 | tf_op jit(solution)/shard_map/project/pallas_call | solution.py:55
  28.3 1.9 collective-permute-start.37
  30.3 5.1 %project.18.refs_0_ = bf16[256,640]{1,0:T(8,128)(2,1)S(1)} custom-call(bf16[128,2752]{1,0:T(8,128)(2,1)S(1)} %copy.61.refs_0_, bf16[128,2752]{1,0:T(8,128)(2,1)S(1)} %copy.62.refs_1_, bf16[2752,2752]{1,0:T(8,128)(2,1)} %refs_4_.11), custom_call_target="tpu_custom_call" | custom-call | flops 901775360 | bytes 5259264 | tf_op jit(solution)/shard_map/project/pallas_call | solution.py:55
  35.4 3.5 %project.22.refs_0_ = bf16[256,384]{1,0:T(8,128)(2,1)S(1)} custom-call(bf16[128,2752]{1,0:T(8,128)(2,1)S(1)} %copy.61.refs_0_, bf16[128,2752]{1,0:T(8,128)(2,1)S(1)} %copy.62.refs_1_, bf16[2752,2752]{1,0:T(8,128)(2,1)} %refs_4_.11), custom_call_target="tpu_custom_call" | custom-call | flops 541065216 | bytes 3719168 | tf_op jit(solution)/shard_map/project/pallas_call | solution.py:55
  39.2 1.9 project.13.refs_0_
  41.9 5.0 %project.20.refs_0_ = bf16[256,640]{1,0:T(8,128)(2,1)S(1)} custom-call(bf16[128,2752]{1,0:T(8,128)(2,1)S(1)} %copy.61.refs_0_, bf16[128,2752]{1,0:T(8,128)(2,1)S(1)} %copy.62.refs_1_, bf16[2752,2752]{1,0:T(8,128)(2,1)} %refs_4_.11), custom_call_target="tpu_custom_call" | custom-call | flops 901775360 | bytes 5259264 | tf_op jit(solution)/shard_map/project/pallas_call | solution.py:55
  49.3 2.1 collective-permute-done.refs_1_
  51.4 4.4 %collective-permute-start.31 = (bf16[256,384]{1,0:T(8,128)(2,1)S(1)}, bf16[256,384]{1,0:T(8,128)(2,1)S(1)}, u32[]{:S(2)}, u32[]{:S(2)}) collective-permute-start(bf16[256,384]{1,0:T(8,128)(2,1)S(1)} %project.22.refs_0_), channel_id=1, source_target_pairs={{0,4},{12,8},{1,5},{13,9},{2,6},{14,10},{3,7},{15,11},{16,20},{28,... | collective-permute-start | bytes 589832 | tf_op jit(solution)/shard_map/ppermute | solution.py:146
  55.8 3.6 %collective-permute-done.31.refs_1_ = bf16[256,384]{1,0:T(8,128)(2,1)S(1)} collective-permute-done((bf16[256,384]{1,0:T(8,128)(2,1)S(1)}, bf16[256,384]{1,0:T(8,128)(2,1)S(1)}, u32[]{:S(2)}, u32[]{:S(2)}) %collective-permute-start.31) | collective-permute-done | bytes 196640 | tf_op jit(solution)/shard_map/ppermute | solution.py:146
  60.8 1.6 fusion.21
  62.5 15.1 %collective-permute-start.19 = (bf16[256,640]{1,0:T(8,128)(2,1)S(1)}, bf16[256,640]{1,0:T(8,128)(2,1)S(1)}, u32[]{:S(2)}, u32[]{:S(2)}) collective-permute-start(bf16[256,640]{1,0:T(8,128)(2,1)S(1)} %project.18.refs_0_), channel_id=1, source_target_pairs={{0,4},{12,8},{1,5},{13,9},{2,6},{14,10},{3,7},{15,11},{16,20},{28,... | collective-permute-start | bytes 983048 | tf_op jit(solution)/shard_map/ppermute | solution.py:146
  80.6 3.7 %collective-permute-done.19.refs_1_ = bf16[256,640]{1,0:T(8,128)(2,1)S(1)} collective-permute-done((bf16[256,640]{1,0:T(8,128)(2,1)S(1)}, bf16[256,640]{1,0:T(8,128)(2,1)S(1)}, u32[]{:S(2)}, u32[]{:S(2)}) %collective-permute-start.19) | collective-permute-done | bytes 327712 | tf_op jit(solution)/shard_map/ppermute | solution.py:146
  89.9 4.2 %collective-permute-done.11 = bf16[128,1024]{1,0:T(8,128)(2,1)S(1)} collective-permute-done((bf16[128,1024]{1,0:T(8,128)(2,1)S(1)}, bf16[128,1024]{1,0:T(8,128)(2,1)S(1)}, u32[]{:S(2)}, u32[]{:S(2)}) %collective-permute-start.11) | collective-permute-done | bytes 262176 | tf_op jit(solution)/shard_map/ppermute | solution.py:223
  99.3 3.3 %collective-permute-start.4 = (bf16[128,2752]{0,1:T(8,128)(2,1)}, bf16[128,2752]{0,1:T(8,128)(2,1)}, u32[]{:S(2)}, u32[]{:S(2)}) collective-permute-start(bf16[128,2752]{0,1:T(8,128)(2,1)} %collective-permute-done.3), channel_id=1, source_target_pairs={{0,1},{2,3},{4,5},{6,7},{8,9},{10,11},{12,13},{14,15},{16,17},{18,... | collective-permute-start | bytes 2113544 | tf_op jit(solution)/shard_map/ppermute | solution.py:191
  102.5 1.5 collective-permute-start.6
  111.6 2.2 copy.64.refs_1_
  113.9 2.2 copy.66.refs_3_
  118.3 5.1 %project.17.refs_4_ = bf16[256,640]{1,0:T(8,128)(2,1)S(1)} custom-call(bf16[128,2752]{1,0:T(8,128)(2,1)S(1)} %copy.63.refs_0_, bf16[128,2752]{1,0:T(8,128)(2,1)S(1)} %copy-done, bf16[128,2752]{1,0:T(8,128)(2,1)S(1)} %copy.65.refs_2_, bf16[128,2752]{1,0:T(8,128)(2,1)S(1)} %copy-done.1, bf16[2752,2752]{1,0:T(8,128)(2,1)} %refs_4_.11), custom_call_target="tpu_custom_call" | custom-call | flops 901775360 | bytes 5259264 | tf_op jit(solution)/shard_map/project/pallas_call | solution.py:55
  123.4 5.1 %project.19.refs_4_ = bf16[256,640]{1,0:T(8,128)(2,1)S(1)} custom-call(bf16[128,2752]{1,0:T(8,128)(2,1)S(1)} %copy.63.refs_0_, bf16[128,2752]{1,0:T(8,128)(2,1)S(1)} %copy-done, bf16[128,2752]{1,0:T(8,128)(2,1)S(1)} %copy.65.refs_2_, bf16[128,2752]{1,0:T(8,128)(2,1)S(1)} %copy-done.1, bf16[2752,2752]{1,0:T(8,128)(2,1)} %refs_4_.11), custom_call_target="tpu_custom_call" | custom-call | flops 901775360 | bytes 5259264 | tf_op jit(solution)/shard_map/project/pallas_call | solution.py:55
  128.6 3.5 %project.23.refs_4_ = bf16[256,384]{1,0:T(8,128)(2,1)S(1)} custom-call(bf16[128,2752]{1,0:T(8,128)(2,1)S(1)} %copy.63.refs_0_, bf16[128,2752]{1,0:T(8,128)(2,1)S(1)} %copy-done, bf16[128,2752]{1,0:T(8,128)(2,1)S(1)} %copy.65.refs_2_, bf16[128,2752]{1,0:T(8,128)(2,1)S(1)} %copy-done.1, bf16[2752,2752]{1,0:T(8,128)(2,1)} %refs_4_.11), custom_call_target="tpu_custom_call" | custom-call | flops 541065216 | bytes 3719168 | tf_op jit(solution)/shard_map/project/pallas_call | solution.py:55
  132.0 2.4 project.25.refs_4_
  134.4 14.2 %collective-permute-start.40 = (bf16[256,192]{1,0:T(8,128)(2,1)S(1)}, bf16[256,192]{1,0:T(8,128)(2,1)S(1)}, u32[]{:S(2)}, u32[]{:S(2)}) collective-permute-start(bf16[256,192]{1,0:T(8,128)(2,1)S(1)} %project.25.refs_4_), channel_id=1, source_target_pairs={{0,4},{12,8},{1,5},{13,9},{2,6},{14,10},{3,7},{15,11},{16,20},{28,... | collective-permute-start | bytes 294920 | tf_op jit(solution)/shard_map/ppermute | solution.py:146
  148.6 1.9 project.14.refs_4_
  153.2 5.1 %project.21.refs_4_ = bf16[256,640]{1,0:T(8,128)(2,1)S(1)} custom-call(bf16[128,2752]{1,0:T(8,128)(2,1)S(1)} %copy.63.refs_0_, bf16[128,2752]{1,0:T(8,128)(2,1)S(1)} %copy-done, bf16[128,2752]{1,0:T(8,128)(2,1)S(1)} %copy.65.refs_2_, bf16[128,2752]{1,0:T(8,128)(2,1)S(1)} %copy-done.1, bf16[2752,2752]{1,0:T(8,128)(2,1)} %refs_4_.11), custom_call_target="tpu_custom_call" | custom-call | flops 901775360 | bytes 5259264 | tf_op jit(solution)/shard_map/project/pallas_call | solution.py:55
  159.8 2.1 collective-permute-done.7.refs_5_
  162.0 4.4 %collective-permute-start.34 = (bf16[256,384]{1,0:T(8,128)(2,1)S(1)}, bf16[256,384]{1,0:T(8,128)(2,1)S(1)}, u32[]{:S(2)}, u32[]{:S(2)}) collective-permute-start(bf16[256,384]{1,0:T(8,128)(2,1)S(1)} %project.23.refs_4_), channel_id=1, source_target_pairs={{0,4},{12,8},{1,5},{13,9},{2,6},{14,10},{3,7},{15,11},{16,20},{28,... | collective-permute-start | bytes 589832 | tf_op jit(solution)/shard_map/ppermute | solution.py:146
  166.4 6.8 %collective-permute-done.34.refs_5_ = bf16[256,384]{1,0:T(8,128)(2,1)S(1)} collective-permute-done((bf16[256,384]{1,0:T(8,128)(2,1)S(1)}, bf16[256,384]{1,0:T(8,128)(2,1)S(1)}, u32[]{:S(2)}, u32[]{:S(2)}) %collective-permute-start.34) | collective-permute-done | bytes 196640 | tf_op jit(solution)/shard_map/ppermute | solution.py:146
  177.3 19.1 %collective-permute-done.42.refs_7_ = bf16[256,192]{1,0:T(8,128)(2,1)S(1)} collective-permute-done((bf16[256,192]{1,0:T(8,128)(2,1)S(1)}, bf16[256,192]{1,0:T(8,128)(2,1)S(1)}, u32[]{:S(2)}, u32[]{:S(2)}) %collective-permute-start.42) | collective-permute-done | bytes 98336 | tf_op jit(solution)/shard_map/ppermute | solution.py:146
  196.4 1.5 collective-permute-start.28
  197.9 2.8 %score.11 = f32[4,256]{1,0:T(4,128)S(1)} custom-call(s32[1]{0:T(128)} %bitcast.5.at_ref, bf16[256,192]{1,0:T(8,128)(2,1)} %project.24.refs_0_, bf16[256,192]{1,0:T(8,128)(2,1)} %collective-permute-done.37.refs_1_, bf16[256,192]{1,0:T(8,128)(2,1)S(1)} %copy-done.32, bf16[256,192]{1,0:T(8,128)(2,1)} %collective-permute-done.39.refs_3_, ...), custom_call_target="tpu_custom_call" | custom-call | flops 805306368 | bytes 3407872 | tf_op jit(solution)/shard_map/score/pallas_call | solution.py:113
  206.5 2.0 collective-permute-done.9.refs_7_
  209.8 2.9 %score.6 = f32[4,256]{1,0:T(4,128)S(1)} custom-call(s32[1]{0:T(128)} %bitcast.at_ref, bf16[256,256]{1,0:T(8,128)(2,1)S(1)} %copy-done.12, bf16[256,256]{1,0:T(8,128)(2,1)S(1)} %copy-done.28, bf16[256,256]{1,0:T(8,128)(2,1)S(1)} %copy-done.30, bf16[256,256]{1,0:T(8,128)(2,1)} %collective-permute-done.2.refs_3_, bf16[256,256]{1,0:T(8,128)(2,1)S(1)} %project.14.refs_4_, ...), custom_call_target="tpu_custom_call" | custom-call | flops 1073741824 | bytes 3670016 | tf_op jit(solution)/shard_map/score/pallas_call | solution.py:113
  214.1 4.4 %collective-permute-done.36.refs_7_ = bf16[256,384]{1,0:T(8,128)(2,1)S(1)} collective-permute-done((bf16[256,384]{1,0:T(8,128)(2,1)S(1)}, bf16[256,384]{1,0:T(8,128)(2,1)S(1)}, u32[]{:S(2)}, u32[]{:S(2)}) %collective-permute-start.36) | collective-permute-done | bytes 196640 | tf_op jit(solution)/shard_map/ppermute | solution.py:146
  219.4 3.5 %score.10 = f32[4,256]{1,0:T(4,128)S(1)} custom-call(s32[1]{0:T(128)} %bitcast.4.at_ref, bf16[256,384]{1,0:T(8,128)(2,1)S(1)} %copy-done.10, bf16[256,384]{1,0:T(8,128)(2,1)S(1)} %copy-done.24, bf16[256,384]{1,0:T(8,128)(2,1)S(1)} %copy-done.26, bf16[256,384]{1,0:T(8,128)(2,1)S(1)} %collective-permute-done.33.refs_3_, bf16[256,384]{1,0:T(8,128)(2,1)S(1)} %project.23.refs_4_, ...), custom_call_target="tpu_custom_call" | custom-call | flops 1610612736 | bytes 4194304 | tf_op jit(solution)/shard_map/score/pallas_call | solution.py:113
  228.0 18.6 %collective-permute-done.18.refs_7_ = bf16[256,640]{1,0:T(8,128)(2,1)S(1)} collective-permute-done((bf16[256,640]{1,0:T(8,128)(2,1)S(1)}, bf16[256,640]{1,0:T(8,128)(2,1)S(1)}, u32[]{:S(2)}, u32[]{:S(2)}) %collective-permute-start.18) | collective-permute-done | bytes 327712 | tf_op jit(solution)/shard_map/ppermute | solution.py:146
  246.6 5.2 %score.7 = f32[4,256]{1,0:T(4,128)S(1)} custom-call(s32[1]{0:T(128)} %bitcast.1.at_ref, bf16[256,640]{1,0:T(8,128)(2,1)S(1)} %copy-done.6, bf16[256,640]{1,0:T(8,128)(2,1)} %collective-permute-done.13.refs_1_, bf16[256,640]{1,0:T(8,128)(2,1)S(1)} %copy-done.20, bf16[256,640]{1,0:T(8,128)(2,1)S(1)} %collective-permute-done.15.refs_3_, ...), custom_call_target="tpu_custom_call" | custom-call | flops 2684354560 | bytes 5242880 | tf_op jit(solution)/shard_map/score/pallas_call | solution.py:113
  252.2 5.1 %score.8 = f32[4,256]{1,0:T(4,128)S(1)} custom-call(s32[1]{0:T(128)} %bitcast.2.at_ref, bf16[256,640]{1,0:T(8,128)(2,1)S(1)} %copy-done.4, bf16[256,640]{1,0:T(8,128)(2,1)S(1)} %copy-done.16, bf16[256,640]{1,0:T(8,128)(2,1)S(1)} %copy-done.22, bf16[256,640]{1,0:T(8,128)(2,1)S(1)} %collective-permute-done.21.refs_3_, bf16[256,640]{1,0:T(8,128)(2,1)S(1)} %project.19.refs_4_, ...), custom_call_target="tpu_custom_call" | custom-call | flops 2684354560 | bytes 5242880 | tf_op jit(solution)/shard_map/score/pallas_call | solution.py:113
  257.4 5.0 %score.9 = f32[4,256]{1,0:T(4,128)S(1)} custom-call(s32[1]{0:T(128)} %bitcast.3.at_ref, bf16[256,640]{1,0:T(8,128)(2,1)S(1)} %copy-done.8, bf16[256,640]{1,0:T(8,128)(2,1)S(1)} %copy-done.14, bf16[256,640]{1,0:T(8,128)(2,1)S(1)} %copy-done.18, bf16[256,640]{1,0:T(8,128)(2,1)S(1)} %collective-permute-done.27.refs_3_, bf16[256,640]{1,0:T(8,128)(2,1)S(1)} %project.21.refs_4_, ...), custom_call_target="tpu_custom_call" | custom-call | flops 2684354560 | bytes 5242880 | tf_op jit(solution)/shard_map/score/pallas_call | solution.py:113
  262.8 1.5 collective-permute-start.44
  264.7 1.8 collective-permute-done.44
  267.3 2.2 collective-permute-start.47
  269.5 2.2 collective-permute-start.48
  271.9 3.1 %collective-permute-done.48 = f32[4,16]{1,0:T(4,128)S(1)} collective-permute-done((f32[4,16]{1,0:T(4,128)S(1)}, f32[4,16]{1,0:T(4,128)S(1)}, u32[]{:S(2)}, u32[]{:S(2)}) %collective-permute-start.48) | collective-permute-done | bytes 288 | tf_op jit(solution)/shard_map/ppermute | solution.py:157
  (207 shorter events, 59.4 us)
Async XLA Ops:
  6.9 78.1 %collective-permute-start.10 = (f32[128,1024]{1,0:T(8,128)}, f32[128,1024]{1,0:T(8,128)}, u32[]{:S(2)}, u32[]{:S(2)}) collective-permute-start(f32[128,1024]{1,0:T(8,128)} %slice_select_fusion), channel_id=1, source_target_pairs={{0,1},{1,0},{2,3},{3,2},{4,5},{5,4},{6,7},{7,6},{8,9},{9,8},{10,11... | collective-permute-start | bytes 1572872 | tf_op jit(solution)/shard_map/ppermute | solution.py:221
  7.4 91.9 %collective-permute-start.3 = (bf16[128,2752]{0,1:T(8,128)(2,1)}, bf16[128,2752]{0,1:T(8,128)(2,1)}, u32[]{:S(2)}, u32[]{:S(2)}) collective-permute-start(bf16[128,2752]{0,1:T(8,128)(2,1)} %param.10), channel_id=1, source_target_pairs={{0,2},{2,0},{4,6},{6,4},{8,10},{10,8},{12,14},{14,12},{16,18},{18,... | collective-permute-start | bytes 2113544 | tf_op jit(solution)/shard_map/ppermute | solution.py:189
  11.8 90.8 %collective-permute-start.5 = (bf16[128,2752]{0,1:T(8,128)(2,1)}, bf16[128,2752]{0,1:T(8,128)(2,1)}, u32[]{:S(2)}, u32[]{:S(2)}) collective-permute-start(bf16[128,2752]{0,1:T(8,128)(2,1)} %param.11), channel_id=1, source_target_pairs={{1,3},{3,1},{5,7},{7,5},{9,11},{11,9},{13,15},{15,13},{17,19},{19,... | collective-permute-start | bytes 2113544 | tf_op jit(solution)/shard_map/ppermute | solution.py:190
  21.1 57.1 %collective-permute-start.13 = (bf16[256,640]{1,0:T(8,128)(2,1)S(1)}, bf16[256,640]{1,0:T(8,128)(2,1)}, u32[]{:S(2)}, u32[]{:S(2)}) collective-permute-start(bf16[256,640]{1,0:T(8,128)(2,1)S(1)} %project.16.refs_0_), channel_id=1, source_target_pairs={{0,4},{12,8},{1,5},{13,9},{2,6},{14,10},{3,7},{15,11},{16,20},{28,... | collective-permute-start | bytes 983048 | tf_op jit(solution)/shard_map/ppermute | solution.py:146
  28.3 18.6 %collective-permute-start.37 = (bf16[256,192]{1,0:T(8,128)(2,1)}, bf16[256,192]{1,0:T(8,128)(2,1)}, u32[]{:S(2)}, u32[]{:S(2)}) collective-permute-start(bf16[256,192]{1,0:T(8,128)(2,1)} %project.24.refs_0_), channel_id=1, source_target_pairs={{0,4},{12,8},{1,5},{13,9},{2,6},{14,10},{3,7},{15,11},{16,20},{28,... | collective-permute-start | bytes 294920 | tf_op jit(solution)/shard_map/ppermute | solution.py:146
  47.0 4.4 %collective-permute-start = (bf16[256,256]{1,0:T(8,128)(2,1)S(1)}, bf16[256,256]{1,0:T(8,128)(2,1)S(1)}, u32[]{:S(2)}, u32[]{:S(2)}) collective-permute-start(bf16[256,256]{1,0:T(8,128)(2,1)S(1)} %project.13.refs_0_), channel_id=1, source_target_pairs={{0,4},{12,8},{1,5},{13,9},{2,6},{14,10},{3,7},{15,11},{16,20},{28,... | collective-permute-start | bytes 393224 | tf_op jit(solution)/shard_map/ppermute | solution.py:146
  51.4 8.1 %collective-permute-start.31 = (bf16[256,384]{1,0:T(8,128)(2,1)S(1)}, bf16[256,384]{1,0:T(8,128)(2,1)S(1)}, u32[]{:S(2)}, u32[]{:S(2)}) collective-permute-start(bf16[256,384]{1,0:T(8,128)(2,1)S(1)} %project.22.refs_0_), channel_id=1, source_target_pairs={{0,4},{12,8},{1,5},{13,9},{2,6},{14,10},{3,7},{15,11},{16,20},{28,... | collective-permute-start | bytes 589832 | tf_op jit(solution)/shard_map/ppermute | solution.py:146
  59.4 0.7 collective-permute-start.38
  60.2 2.3 collective-permute-start.1
  62.5 21.8 %collective-permute-start.19 = (bf16[256,640]{1,0:T(8,128)(2,1)S(1)}, bf16[256,640]{1,0:T(8,128)(2,1)S(1)}, u32[]{:S(2)}, u32[]{:S(2)}) collective-permute-start(bf16[256,640]{1,0:T(8,128)(2,1)S(1)} %project.18.refs_0_), channel_id=1, source_target_pairs={{0,4},{12,8},{1,5},{13,9},{2,6},{14,10},{3,7},{15,11},{16,20},{28,... | collective-permute-start | bytes 983048 | tf_op jit(solution)/shard_map/ppermute | solution.py:146
  78.2 9.6 %collective-permute-start.25 = (bf16[256,640]{1,0:T(8,128)(2,1)S(1)}, bf16[256,640]{1,0:T(8,128)(2,1)S(1)}, u32[]{:S(2)}, u32[]{:S(2)}) collective-permute-start(bf16[256,640]{1,0:T(8,128)(2,1)S(1)} %project.20.refs_0_), channel_id=1, source_target_pairs={{0,4},{12,8},{1,5},{13,9},{2,6},{14,10},{3,7},{15,11},{16,20},{28,... | collective-permute-start | bytes 983048 | tf_op jit(solution)/shard_map/ppermute | solution.py:146
  84.3 4.2 %collective-permute-start.32 = (bf16[256,384]{1,0:T(8,128)(2,1)S(1)}, bf16[256,384]{1,0:T(8,128)(2,1)S(1)}, u32[]{:S(2)}, u32[]{:S(2)}) collective-permute-start(bf16[256,384]{1,0:T(8,128)(2,1)S(1)} %fusion.12), channel_id=1, source_target_pairs={{4,8},{8,4},{5,9},{9,5},{6,10},{10,6},{7,11},{11,7},{20,24},{24,20... | collective-permute-start | bytes 589832 | tf_op jit(solution)/shard_map/ppermute | solution.py:146
  85.1 9.8 %collective-permute-start.14 = (bf16[256,640]{1,0:T(8,128)(2,1)S(1)}, bf16[256,640]{1,0:T(8,128)(2,1)S(1)}, u32[]{:S(2)}, u32[]{:S(2)}) collective-permute-start(bf16[256,640]{1,0:T(8,128)(2,1)S(1)} %fusion), channel_id=1, source_target_pairs={{4,8},{8,4},{5,9},{9,5},{6,10},{10,6},{7,11},{11,7},{20,24},{24,20... | collective-permute-start | bytes 983048 | tf_op jit(solution)/shard_map/ppermute | solution.py:146
  87.8 6.4 %collective-permute-start.11 = (bf16[128,1024]{1,0:T(8,128)(2,1)S(1)}, bf16[128,1024]{1,0:T(8,128)(2,1)S(1)}, u32[]{:S(2)}, u32[]{:S(2)}) collective-permute-start(bf16[128,1024]{1,0:T(8,128)(2,1)S(1)} %fusion.24), channel_id=1, source_target_pairs={{0,2},{2,0},{1,3},{3,1},{4,6},{6,4},{5,7},{7,5},{8,10},{10,8},{9,1... | collective-permute-start | bytes 786440 | tf_op jit(solution)/shard_map/ppermute | solution.py:223
  88.5 7.3 %collective-permute-start.20 = (bf16[256,640]{1,0:T(8,128)(2,1)S(1)}, bf16[256,640]{1,0:T(8,128)(2,1)S(1)}, u32[]{:S(2)}, u32[]{:S(2)}) collective-permute-start(bf16[256,640]{1,0:T(8,128)(2,1)S(1)} %fusion.4), channel_id=1, source_target_pairs={{4,8},{8,4},{5,9},{9,5},{6,10},{10,6},{7,11},{11,7},{20,24},{24,20... | collective-permute-start | bytes 983048 | tf_op jit(solution)/shard_map/ppermute | solution.py:146
  94.2 3.8 %collective-permute-start.26 = (bf16[256,640]{1,0:T(8,128)(2,1)S(1)}, bf16[256,640]{1,0:T(8,128)(2,1)S(1)}, u32[]{:S(2)}, u32[]{:S(2)}) collective-permute-start(bf16[256,640]{1,0:T(8,128)(2,1)S(1)} %fusion.8), channel_id=1, source_target_pairs={{4,8},{8,4},{5,9},{9,5},{6,10},{10,6},{7,11},{11,7},{20,24},{24,20... | collective-permute-start | bytes 983048 | tf_op jit(solution)/shard_map/ppermute | solution.py:146
  94.9 13.5 %collective-permute-start.12 = (bf16[256,1024]{1,0:T(8,128)(2,1)S(1)}, bf16[256,1024]{1,0:T(8,128)(2,1)S(1)}, u32[]{:S(2)}, u32[]{:S(2)}) collective-permute-start(bf16[256,1024]{1,0:T(8,128)(2,1)S(1)} %pad_maximum_fusion), channel_id=1, source_target_pairs={{0,1},{1,0},{2,3},{3,2},{4,5},{5,4},{6,7},{7,6},{8,9},{9,8},{10,11... | collective-permute-start | bytes 1572872 | tf_op jit(solution)/shard_map/ppermute | solution.py:225
  95.8 80.2 %collective-permute-start.39 = (bf16[256,192]{1,0:T(8,128)(2,1)}, bf16[256,192]{1,0:T(8,128)(2,1)}, u32[]{:S(2)}, u32[]{:S(2)}) collective-permute-start(bf16[256,192]{1,0:T(8,128)(2,1)} %fusion.21), channel_id=1, source_target_pairs={{8,12},{4,0},{9,13},{5,1},{10,14},{6,2},{11,15},{7,3},{24,28},{20,... | collective-permute-start | bytes 294920 | tf_op jit(solution)/shard_map/ppermute | solution.py:146
  98.0 107.2 %collective-permute-start.2 = (bf16[256,256]{1,0:T(8,128)(2,1)}, bf16[256,256]{1,0:T(8,128)(2,1)}, u32[]{:S(2)}, u32[]{:S(2)}) collective-permute-start(bf16[256,256]{1,0:T(8,128)(2,1)} %fusion.17), channel_id=1, source_target_pairs={{8,12},{4,0},{9,13},{5,1},{10,14},{6,2},{11,15},{7,3},{24,28},{20,... | collective-permute-start | bytes 393224 | tf_op jit(solution)/shard_map/ppermute | solution.py:146
  99.3 12.3 %collective-permute-start.4 = (bf16[128,2752]{0,1:T(8,128)(2,1)}, bf16[128,2752]{0,1:T(8,128)(2,1)}, u32[]{:S(2)}, u32[]{:S(2)}) collective-permute-start(bf16[128,2752]{0,1:T(8,128)(2,1)} %collective-permute-done.3), channel_id=1, source_target_pairs={{0,1},{2,3},{4,5},{6,7},{8,9},{10,11},{12,13},{14,15},{16,17},{18,... | collective-permute-start | bytes 2113544 | tf_op jit(solution)/shard_map/ppermute | solution.py:191
  102.5 11.3 %collective-permute-start.6 = (bf16[128,2752]{0,1:T(8,128)(2,1)}, bf16[128,2752]{0,1:T(8,128)(2,1)}, u32[]{:S(2)}, u32[]{:S(2)}) collective-permute-start(bf16[128,2752]{0,1:T(8,128)(2,1)} %collective-permute-done.5), channel_id=1, source_target_pairs={{1,0},{3,2},{5,4},{7,6},{9,8},{11,10},{13,12},{15,14},{17,16},{19,... | collective-permute-start | bytes 2113544 | tf_op jit(solution)/shard_map/ppermute | solution.py:192
  134.4 23.9 %collective-permute-start.40 = (bf16[256,192]{1,0:T(8,128)(2,1)S(1)}, bf16[256,192]{1,0:T(8,128)(2,1)S(1)}, u32[]{:S(2)}, u32[]{:S(2)}) collective-permute-start(bf16[256,192]{1,0:T(8,128)(2,1)S(1)} %project.25.refs_4_), channel_id=1, source_target_pairs={{0,4},{12,8},{1,5},{13,9},{2,6},{14,10},{3,7},{15,11},{16,20},{28,... | collective-permute-start | bytes 294920 | tf_op jit(solution)/shard_map/ppermute | solution.py:146
  150.5 50.2 %collective-permute-start.16 = (bf16[256,640]{1,0:T(8,128)(2,1)S(1)}, bf16[256,640]{1,0:T(8,128)(2,1)S(1)}, u32[]{:S(2)}, u32[]{:S(2)}) collective-permute-start(bf16[256,640]{1,0:T(8,128)(2,1)S(1)} %project.17.refs_4_), channel_id=1, source_target_pairs={{0,4},{12,8},{1,5},{13,9},{2,6},{14,10},{3,7},{15,11},{16,20},{28,... | collective-permute-start | bytes 983048 | tf_op jit(solution)/shard_map/ppermute | solution.py:146
  151.9 10.1 %collective-permute-start.7 = (bf16[256,256]{1,0:T(8,128)(2,1)S(1)}, bf16[256,256]{1,0:T(8,128)(2,1)S(1)}, u32[]{:S(2)}, u32[]{:S(2)}) collective-permute-start(bf16[256,256]{1,0:T(8,128)(2,1)S(1)} %project.14.refs_4_), channel_id=1, source_target_pairs={{0,4},{12,8},{1,5},{13,9},{2,6},{14,10},{3,7},{15,11},{16,20},{28,... | collective-permute-start | bytes 393224 | tf_op jit(solution)/shard_map/ppermute | solution.py:146
  158.3 43.3 %collective-permute-start.22 = (bf16[256,640]{1,0:T(8,128)(2,1)S(1)}, bf16[256,640]{1,0:T(8,128)(2,1)S(1)}, u32[]{:S(2)}, u32[]{:S(2)}) collective-permute-start(bf16[256,640]{1,0:T(8,128)(2,1)S(1)} %project.19.refs_4_), channel_id=1, source_target_pairs={{0,4},{12,8},{1,5},{13,9},{2,6},{14,10},{3,7},{15,11},{16,20},{28,... | collective-permute-start | bytes 983048 | tf_op jit(solution)/shard_map/ppermute | solution.py:146
  162.0 11.2 %collective-permute-start.34 = (bf16[256,384]{1,0:T(8,128)(2,1)S(1)}, bf16[256,384]{1,0:T(8,128)(2,1)S(1)}, u32[]{:S(2)}, u32[]{:S(2)}) collective-permute-start(bf16[256,384]{1,0:T(8,128)(2,1)S(1)} %project.23.refs_4_), channel_id=1, source_target_pairs={{0,4},{12,8},{1,5},{13,9},{2,6},{14,10},{3,7},{15,11},{16,20},{28,... | collective-permute-start | bytes 589832 | tf_op jit(solution)/shard_map/ppermute | solution.py:146
  173.2 0.7 collective-permute-start.41
  174.7 21.7 %collective-permute-start.42 = (bf16[256,192]{1,0:T(8,128)(2,1)S(1)}, bf16[256,192]{1,0:T(8,128)(2,1)S(1)}, u32[]{:S(2)}, u32[]{:S(2)}) collective-permute-start(bf16[256,192]{1,0:T(8,128)(2,1)S(1)} %fusion.23), channel_id=1, source_target_pairs={{8,12},{4,0},{9,13},{5,1},{10,14},{6,2},{11,15},{7,3},{24,28},{20,... | collective-permute-start | bytes 294920 | tf_op jit(solution)/shard_map/ppermute | solution.py:146
  176.0 36.7 %collective-permute-start.33 = (bf16[256,384]{1,0:T(8,128)(2,1)S(1)}, bf16[256,384]{1,0:T(8,128)(2,1)S(1)}, u32[]{:S(2)}, u32[]{:S(2)}) collective-permute-start(bf16[256,384]{1,0:T(8,128)(2,1)S(1)} %copy-done.39), channel_id=1, source_target_pairs={{8,12},{4,0},{9,13},{5,1},{10,14},{6,2},{11,15},{7,3},{24,28},{20,... | collective-permute-start | bytes 589832 | tf_op jit(solution)/shard_map/ppermute | solution.py:146
  196.4 7.4 %collective-permute-start.28 = (bf16[256,640]{1,0:T(8,128)(2,1)S(1)}, bf16[256,640]{1,0:T(8,128)(2,1)S(1)}, u32[]{:S(2)}, u32[]{:S(2)}) collective-permute-start(bf16[256,640]{1,0:T(8,128)(2,1)S(1)} %project.21.refs_4_), channel_id=1, source_target_pairs={{0,4},{12,8},{1,5},{13,9},{2,6},{14,10},{3,7},{15,11},{16,20},{28,... | collective-permute-start | bytes 983048 | tf_op jit(solution)/shard_map/ppermute | solution.py:146
  200.7 2.3 collective-permute-start.35
  201.6 6.9 %collective-permute-start.9 = (bf16[256,256]{1,0:T(8,128)(2,1)S(1)}, bf16[256,256]{1,0:T(8,128)(2,1)S(1)}, u32[]{:S(2)}, u32[]{:S(2)}) collective-permute-start(bf16[256,256]{1,0:T(8,128)(2,1)S(1)} %fusion.19), channel_id=1, source_target_pairs={{8,12},{4,0},{9,13},{5,1},{10,14},{6,2},{11,15},{7,3},{24,28},{20,... | collective-permute-start | bytes 393224 | tf_op jit(solution)/shard_map/ppermute | solution.py:146
  203.0 19.9 %collective-permute-start.17 = (bf16[256,640]{1,0:T(8,128)(2,1)S(1)}, bf16[256,640]{1,0:T(8,128)(2,1)S(1)}, u32[]{:S(2)}, u32[]{:S(2)}) collective-permute-start(bf16[256,640]{1,0:T(8,128)(2,1)S(1)} %fusion.2), channel_id=1, source_target_pairs={{4,8},{8,4},{5,9},{9,5},{6,10},{10,6},{7,11},{11,7},{20,24},{24,20... | collective-permute-start | bytes 983048 | tf_op jit(solution)/shard_map/ppermute | solution.py:146
  203.8 14.7 %collective-permute-start.36 = (bf16[256,384]{1,0:T(8,128)(2,1)S(1)}, bf16[256,384]{1,0:T(8,128)(2,1)S(1)}, u32[]{:S(2)}, u32[]{:S(2)}) collective-permute-start(bf16[256,384]{1,0:T(8,128)(2,1)S(1)} %fusion.15), channel_id=1, source_target_pairs={{8,12},{4,0},{9,13},{5,1},{10,14},{6,2},{11,15},{7,3},{24,28},{20,... | collective-permute-start | bytes 589832 | tf_op jit(solution)/shard_map/ppermute | solution.py:146
  205.2 21.5 %collective-permute-start.15 = (bf16[256,640]{1,0:T(8,128)(2,1)S(1)}, bf16[256,640]{1,0:T(8,128)(2,1)S(1)}, u32[]{:S(2)}, u32[]{:S(2)}) collective-permute-start(bf16[256,640]{1,0:T(8,128)(2,1)S(1)} %copy-done.37), channel_id=1, source_target_pairs={{8,12},{4,0},{9,13},{5,1},{10,14},{6,2},{11,15},{7,3},{24,28},{20,... | collective-permute-start | bytes 983048 | tf_op jit(solution)/shard_map/ppermute | solution.py:146
  208.5 43.4 %collective-permute-start.21 = (bf16[256,640]{1,0:T(8,128)(2,1)S(1)}, bf16[256,640]{1,0:T(8,128)(2,1)S(1)}, u32[]{:S(2)}, u32[]{:S(2)}) collective-permute-start(bf16[256,640]{1,0:T(8,128)(2,1)S(1)} %copy-done.35), channel_id=1, source_target_pairs={{8,12},{4,0},{9,13},{5,1},{10,14},{6,2},{11,15},{7,3},{24,28},{20,... | collective-permute-start | bytes 983048 | tf_op jit(solution)/shard_map/ppermute | solution.py:146
  212.8 44.6 %collective-permute-start.27 = (bf16[256,640]{1,0:T(8,128)(2,1)S(1)}, bf16[256,640]{1,0:T(8,128)(2,1)S(1)}, u32[]{:S(2)}, u32[]{:S(2)}) collective-permute-start(bf16[256,640]{1,0:T(8,128)(2,1)S(1)} %copy-done.36), channel_id=1, source_target_pairs={{8,12},{4,0},{9,13},{5,1},{10,14},{6,2},{11,15},{7,3},{24,28},{20,... | collective-permute-start | bytes 983048 | tf_op jit(solution)/shard_map/ppermute | solution.py:146
  218.5 5.4 %collective-permute-start.23 = (bf16[256,640]{1,0:T(8,128)(2,1)S(1)}, bf16[256,640]{1,0:T(8,128)(2,1)S(1)}, u32[]{:S(2)}, u32[]{:S(2)}) collective-permute-start(bf16[256,640]{1,0:T(8,128)(2,1)S(1)} %fusion.6), channel_id=1, source_target_pairs={{4,8},{8,4},{5,9},{9,5},{6,10},{10,6},{7,11},{11,7},{20,24},{24,20... | collective-permute-start | bytes 983048 | tf_op jit(solution)/shard_map/ppermute | solution.py:146
  223.0 2.3 collective-permute-start.29
  223.9 22.7 %collective-permute-start.18 = (bf16[256,640]{1,0:T(8,128)(2,1)S(1)}, bf16[256,640]{1,0:T(8,128)(2,1)S(1)}, u32[]{:S(2)}, u32[]{:S(2)}) collective-permute-start(bf16[256,640]{1,0:T(8,128)(2,1)S(1)} %fusion.3), channel_id=1, source_target_pairs={{8,12},{4,0},{9,13},{5,1},{10,14},{6,2},{11,15},{7,3},{24,28},{20,... | collective-permute-start | bytes 983048 | tf_op jit(solution)/shard_map/ppermute | solution.py:146
  225.3 26.9 %collective-permute-start.24 = (bf16[256,640]{1,0:T(8,128)(2,1)S(1)}, bf16[256,640]{1,0:T(8,128)(2,1)S(1)}, u32[]{:S(2)}, u32[]{:S(2)}) collective-permute-start(bf16[256,640]{1,0:T(8,128)(2,1)S(1)} %fusion.7), channel_id=1, source_target_pairs={{8,12},{4,0},{9,13},{5,1},{10,14},{6,2},{11,15},{7,3},{24,28},{20,... | collective-permute-start | bytes 983048 | tf_op jit(solution)/shard_map/ppermute | solution.py:146
  226.7 30.7 %collective-permute-start.30 = (bf16[256,640]{1,0:T(8,128)(2,1)S(1)}, bf16[256,640]{1,0:T(8,128)(2,1)S(1)}, u32[]{:S(2)}, u32[]{:S(2)}) collective-permute-start(bf16[256,640]{1,0:T(8,128)(2,1)S(1)} %fusion.11), channel_id=1, source_target_pairs={{8,12},{4,0},{9,13},{5,1},{10,14},{6,2},{11,15},{7,3},{24,28},{20,... | collective-permute-start | bytes 983048 | tf_op jit(solution)/shard_map/ppermute | solution.py:146
  262.8 1.9 collective-permute-start.43
  262.8 3.7 %collective-permute-start.44 = (f32[4,16]{1,0:T(4,128)S(1)}, f32[4,16]{1,0:T(4,128)S(1)}, u32[]{:S(2)}, u32[]{:S(2)}) collective-permute-start(f32[4,16]{1,0:T(4,128)S(1)} %maximum_select_fusion), channel_id=1, source_target_pairs={{0,2},{1,3},{2,0},{3,1},{4,6},{5,7},{6,4},{7,5},{8,10},{9,11},{10,... | collective-permute-start | bytes 776 | tf_op jit(solution)/shard_map/ppermute | solution.py:157
  264.3 3.0 %collective-permute-start.45 = (f32[4,16]{1,0:T(4,128)S(1)}, f32[4,16]{1,0:T(4,128)S(1)}, u32[]{:S(2)}, u32[]{:S(2)}) collective-permute-start(f32[4,16]{1,0:T(4,128)S(1)} %maximum_select_fusion), channel_id=1, source_target_pairs={{0,3},{1,2},{2,1},{3,0},{4,7},{5,6},{6,5},{7,4},{8,11},{9,10},{10,... | collective-permute-start | bytes 776 | tf_op jit(solution)/shard_map/ppermute | solution.py:157
  267.3 4.4 %collective-permute-start.46 = (f32[4,16]{1,0:T(4,128)S(1)}, f32[4,16]{1,0:T(4,128)S(1)}, u32[]{:S(2)}, u32[]{:S(2)}) collective-permute-start(f32[4,16]{1,0:T(4,128)S(1)} %add_add_fusion.2), channel_id=1, source_target_pairs={{0,4},{4,0},{8,12},{12,8},{1,5},{5,1},{9,13},{13,9},{2,6},{6,2},{1... | collective-permute-start | bytes 776 | tf_op jit(solution)/shard_map/ppermute | solution.py:157
  267.3 4.5 %collective-permute-start.47 = (f32[4,16]{1,0:T(4,128)S(1)}, f32[4,16]{1,0:T(4,128)S(1)}, u32[]{:S(2)}, u32[]{:S(2)}) collective-permute-start(f32[4,16]{1,0:T(4,128)S(1)} %add_add_fusion.2), channel_id=1, source_target_pairs={{0,8},{4,12},{8,0},{12,4},{1,9},{5,13},{9,1},{13,5},{2,10},{6,14},... | collective-permute-start | bytes 776 | tf_op jit(solution)/shard_map/ppermute | solution.py:157
  269.5 5.4 %collective-permute-start.48 = (f32[4,16]{1,0:T(4,128)S(1)}, f32[4,16]{1,0:T(4,128)S(1)}, u32[]{:S(2)}, u32[]{:S(2)}) collective-permute-start(f32[4,16]{1,0:T(4,128)S(1)} %add_add_fusion.2), channel_id=1, source_target_pairs={{0,12},{4,8},{8,4},{12,0},{1,13},{5,9},{9,5},{13,1},{2,14},{6,10},... | collective-permute-start | bytes 776 | tf_op jit(solution)/shard_map/ppermute | solution.py:157
  (44 other events, 665.5 us)

commit v2 on v0

v2 whole, which is shorter than its diff:
```python
import functools
import math

import jax
import jax.numpy as jnp
from jax import lax
from jax.experimental import pallas as pl
from jax.experimental.pallas import tpu as pltpu
from jax.sharding import PartitionSpec as P

D = 4096
FF = 11008
TC_DEV = 128
EX_DEV = 2
QLEN = 16
PAD = 1
MIB = 1024 * 1024
TILE = 256
WIDTHS = (1024, 1024)
F32 = jnp.float32
BF16 = jnp.bfloat16
VMEM = pl.BlockSpec(memory_space=pltpu.VMEM)
SMEM = pl.BlockSpec(memory_space=pltpu.SMEM)
ANY = pl.BlockSpec(memory_space=pl.ANY)
HBM = pl.BlockSpec(memory_space=pltpu.HBM)
ORDER = jax.ShapeDtypeStruct((8, 128), F32)
QUICK = pl.CostEstimate(flops=1024, bytes_accessed=1024, transcendentals=0)


def params(mib):
    return pltpu.CompilerParams(vmem_limit_bytes=mib * MIB)


def chunk_bounds(total):
    bounds = []
    start = 0
    for width in WIDTHS:
        if start + width < total:
            bounds.append((start, width))
            start += width
    bounds.append((start, total - start))
    return bounds


def total_of(values):
    return functools.reduce(lambda a, b: a + b, values)


def project_kernel(terms, order_ref, *refs):
    del order_ref
    if terms:
        firsts, seconds = refs[:terms], refs[terms : 2 * terms]
        basis_ref, wide_ref, send_ref, rows_ref, done_ref = refs[2 * terms :]

        @pl.when(pl.program_id(0) == 0)
        def _():
            split = firsts[0].shape[1]
            rows_ref[:split] = total_of([r[...] for r in firsts]).T
            rows_ref[split:] = total_of([r[...] for r in seconds]).T
    else:
        rows_ref, basis_ref, wide_ref, send_ref, done_ref = refs
    product = jnp.dot(rows_ref[...], basis_ref[...], preferred_element_type=F32)
    wide_ref[...] = product
    send_ref[...] = product.astype(send_ref.dtype)
    done_ref[...] = jnp.zeros_like(done_ref)


def project(order, inputs, basis, start, width):
    depth = basis.shape[0]
    whole = lambda shape: pl.BlockSpec(shape, lambda i: (0, 0))
    if isinstance(inputs, tuple):
        firsts, seconds = inputs
        terms = len(firsts)
        arrays = list(firsts) + list(seconds)
        rows = firsts[0].shape[1] + seconds[0].shape[1]
    else:
        terms = 0
        arrays = [inputs]
        rows = inputs.shape[0]
    tiles = pl.cdiv(width, TILE)
    first_tile = start // TILE
    out_specs = [pl.BlockSpec((rows, TILE), lambda i: (0, i))] * 2
    out_shape = [
        jax.ShapeDtypeStruct((rows, width), F32),
        jax.ShapeDtypeStruct((rows, width), BF16),
    ]
    if terms:
        out_specs.append(whole((rows, depth)))
        out_shape.append(jax.ShapeDtypeStruct((rows, depth), BF16))
    out = pl.pallas_call(
        functools.partial(project_kernel, terms),
        grid=(tiles,),
        in_specs=[ANY]
        + [whole(a.shape) for a in arrays]
        + [pl.BlockSpec((depth, TILE), lambda i: (0, first_tile + i))],
        out_specs=out_specs + [whole((8, 128))],
        out_shape=out_shape + [ORDER],
        compiler_params=params(50),
        cost_estimate=QUICK,
        name="project",
    )(order, *arrays, basis)
    if terms:
        return out
    return out[0], out[1], inputs, out[2]


def act_kernel(order_ref, cand_ref, query_ref, basis_ref, away_ref, mine_ref, done_ref):
    del order_ref
    cand_first = lax.axis_index("sub") != 0

    def both(first_ref, second_ref):
        away_ref[...] = jnp.dot(first_ref[...], basis_ref[...], preferred_element_type=F32)
        mine_ref[...] = jnp.dot(second_ref[...], basis_ref[...], preferred_element_type=F32)

    @pl.when(cand_first)
    def _():
        both(cand_ref, query_ref)

    @pl.when(jnp.logical_not(cand_first))
    def _():
        both(query_ref, cand_ref)

    done_ref[...] = jnp.zeros_like(done_ref)


def act_shares(order, cand_act, query_act, basis):
    rows, depth = cand_act.shape
    features = basis.shape[1]
    tile = min(TILE, features)
    whole = lambda shape: pl.BlockSpec(shape, lambda i: (0, 0))
    return pl.pallas_call(
        act_kernel,
        grid=(features // tile,),
        in_specs=[
            ANY,
            whole((rows, depth)),
            whole((rows, depth)),
            pl.BlockSpec((depth, tile), lambda i: (0, i)),
        ],
        out_specs=[pl.BlockSpec((rows, tile), lambda i: (0, i))] * 2 + [whole((8, 128))],
        out_shape=[jax.ShapeDtypeStruct((rows, features), F32)] * 2 + [ORDER],
        compiler_params=params(16),
        cost_estimate=QUICK,
        name="acts",
    )(order, cand_act, query_act, basis)


def add_kernel(order_ref, *refs):
    del order_ref
    sum_ref, done_ref = refs[-2:]
    sum_ref[...] = total_of([r[...].astype(F32) for r in refs[:-2]]).astype(sum_ref.dtype)
    done_ref[...] = jnp.zeros_like(done_ref)


def add(order, *arrays):
    return pl.pallas_call(
        add_kernel,
        in_specs=[ANY] + [VMEM] * len(arrays),
        out_specs=[VMEM, VMEM],
        out_shape=[jax.ShapeDtypeStruct(arrays[0].shape, BF16), ORDER],
        compiler_params=params(16),
        cost_estimate=QUICK,
        name="add",
    )(order, *arrays)


def half_kernel(order_ref, mine_ref, came_ref, cand_ids_ref, query_ids_ref, half_ref, done_ref):
    del order_ref
    rows = mine_ref.shape[0]
    ids = jnp.where(lax.axis_index("sub") == 0, cand_ids_ref[...], query_ids_ref[...])
    keep = jnp.where(ids != PAD, 1.0, 0.0).astype(F32)
    keep = jnp.broadcast_to(keep, (rows, rows)).T[:, :1]
    half_ref[...] = ((mine_ref[...] + came_ref[...]) * keep).astype(BF16)
    done_ref[...] = jnp.zeros_like(done_ref)


def half_acts(order, mine, came, cand_ids, query_ids):
    return pl.pallas_call(
        half_kernel,
        in_specs=[ANY] + [VMEM] * 4,
        out_specs=[VMEM, VMEM],
        out_shape=[jax.ShapeDtypeStruct(mine.shape, BF16), ORDER],
        compiler_params=params(16),
        cost_estimate=QUICK,
        name="half_acts",
    )(order, mine, came, cand_ids[None, :], query_ids[None, :])


def split_kernel(examples, order_ref, offsets_ref, own, over, own_sw, over_sw, split_ref, query_ref, done_ref):
    del order_ref
    rows, features = own.shape
    cand_here = lax.axis_index("sub") == 0
    ex = lax.axis_index("ex")
    spot = lax.broadcasted_iota(jnp.int32, (rows, 1), 0)
    for place, kept, swapped in ((0, own, own_sw), (1, over, over_sw)):
        span = pl.ds(place * rows, rows)
        first = (ex if place == 0 else 1 - ex) * rows
        cand = jnp.where(cand_here, kept[...], swapped[...])
        query_ref[span, :] = jnp.where(cand_here, swapped[...], kept[...])
        for k in range(examples):
            member = spot + first >= offsets_ref[k]
            if k + 1 < examples:
                member = member & (spot + first < offsets_ref[k + 1])
            member = jnp.where(member, 1.0, 0.0).astype(BF16)
            split_ref[span, k * features : (k + 1) * features] = cand * member
    done_ref[...] = jnp.zeros_like(done_ref)


def split_acts(order, offsets, own, over, own_sw, over_sw):
    rows, features = own.shape
    examples = offsets.shape[0]
    return pl.pallas_call(
        functools.partial(split_kernel, examples),
        in_specs=[ANY, SMEM] + [VMEM] * 4,
        out_specs=[VMEM] * 3,
        out_shape=[
            jax.ShapeDtypeStruct((2 * rows, examples * features), BF16),
            jax.ShapeDtypeStruct((2 * rows, features), BF16),
            ORDER,
        ],
        compiler_params=params(16),
        cost_estimate=QUICK,
        name="split_acts",
    )(order, offsets, own, over, own_sw, over_sw)


def row_tiles(width):
    tiles = []
    start = 0
    while start < width:
        size = min(512, width - start)
        tiles.append((start, size))
        start += size
    return tiles


def score_kernel(blocks, pick, cand_rows, examples, first, order_ref, *refs):
    del order_ref
    per_block = 2 if pick else 1
    parts = refs[: blocks * per_block]
    eig_hbm, split_ref, query_act_ref, out_ref, done_ref, eig_ref, sems = refs[blocks * per_block :]
    width = parts[0].shape[1]
    base = lax.axis_index("sub") * (eig_hbm.shape[0] // lax.axis_size("sub")) + first
    copies = []
    for n, (start, size) in enumerate(row_tiles(width)):
        copies.append(
            pltpu.make_async_copy(
                eig_hbm.at[pl.ds(pl.multiple_of(base + start, 8), size), :],
                eig_ref.at[pl.ds(start, size), :],
                sems.at[n],
            )
        )
    for copy in copies:
        copy.start()
    sums = []
    for b in range(blocks):
        here = parts[b * per_block]
        if pick:
            spot = lax.axis_index("hid")
            inner = (spot != 0) & (spot != lax.axis_size("hid") - 1)
            sums.append(jnp.where(inner, here[...], parts[b * per_block + 1][...]))
        else:
            sums.append(here[...])
    features = eig_ref.shape[1]
    cand = jnp.concatenate([s[:cand_rows] for s in sums], 0)
    query = jnp.concatenate([s[cand_rows:] for s in sums], 0)
    scores = [0.0] * examples
    for copy, (start, size) in zip(copies, row_tiles(width)):
        copy.wait()
        cand_tile = cand[:, start : start + size].T
        query_tile = query[:, start : start + size].T.astype(F32)
        inverse = 1.0 / eig_ref[start : start + size, :]
        for k in range(examples):
            outer = jnp.dot(
                cand_tile,
                split_ref[:, k * features : (k + 1) * features],
                preferred_element_type=F32,
            )
            weights = (outer * inverse).astype(BF16)
            image = lax.dot_general(
                weights,
                query_act_ref[...],
                (((1,), (1,)), ((), ())),
                preferred_element_type=F32,
            )
            scores[k] = scores[k] + jnp.sum(image * query_tile, axis=0, keepdims=True)
    for k in range(examples):
        out_ref[k : k + 1, :] = scores[k]
    done_ref[...] = jnp.zeros_like(done_ref)


def score_chunk(order, blocks, pick, cand_rows, eigvals, first, split, query_acts, examples):
    parts = [a for block in blocks for a in block]
    width = parts[0].shape[1]
    features = eigvals.shape[1]
    return pl.pallas_call(
        functools.partial(score_kernel, len(blocks), pick, cand_rows, examples, first),
        in_specs=[ANY] + [VMEM] * len(parts) + [HBM, VMEM, VMEM],
        out_specs=[VMEM, VMEM],
        out_shape=[jax.ShapeDtypeStruct((examples, query_acts.shape[0]), F32), ORDER],
        scratch_shapes=[
            pltpu.VMEM((width, features), F32),
            pltpu.SemaphoreType.DMA((len(row_tiles(width)),)),
        ],
        compiler_params=params(44),
        cost_estimate=QUICK,
        name="score",
    )(order, *parts, eigvals, split, query_acts)


def small_sum(value, axes):
    size = lax.axis_size(axes)
    if size > 4:
        return lax.psum(value, axes)
    terms = [value]
    for other in range(1, size):
        terms.append(lax.ppermute(value, axes, [(i, i ^ other) for i in range(size)]))
    while len(terms) > 1:
        terms = [a + b for a, b in zip(terms[::2], terms[1::2])]
    return terms[0]


def token_scores_paired(
    cand_grad, query_grad, cand_act, query_act, cand_ids, query_ids, cand_offsets, basis_g, basis_a, eigvals
):
    rows = cand_grad.shape[0]
    examples = cand_offsets.shape[0]
    both = ("ex", "sub")
    bounds = chunk_bounds(basis_g.shape[1])
    count = len(bounds)
    swap = lambda a, axis: lax.ppermute(a, axis, [(0, 1), (1, 0)])
    inward = lambda a: lax.ppermute(a, "hid", [(0, 1), (3, 2)])
    across = lambda a: lax.ppermute(a, "hid", [(1, 2), (2, 1)])
    outward = lambda a: lax.ppermute(a, "hid", [(1, 0), (2, 3)])

    cand_over = lax.ppermute(cand_grad, both, [(0, 2), (2, 0)])
    query_over = lax.ppermute(query_grad, both, [(1, 3), (3, 1)])
    cand_across = lax.ppermute(cand_over, both, [(0, 1), (2, 3)])
    query_across = lax.ppermute(query_over, both, [(1, 0), (3, 2)])
    tokens = [
        ([cand_grad.T], [query_grad.T]),
        ([cand_over.T, cand_across.T], [query_over.T, query_across.T]),
    ]
    order = jnp.zeros((8, 128), F32)
    wide, came_in, came_across, summed, came_out = {}, {}, {}, {}, {}
    scores = []

    def step_project(c):
        nonlocal order
        block, q = divmod(c, count)
        wide[c], send, tokens[block], order = project(order, tokens[block], basis_g, *bounds[q])
        came_in[c] = inward(send)

    def step_across(c):
        nonlocal order
        send, order = add(order, wide[c], came_in[c])
        came_across[c] = across(send)

    def step_outward(c):
        nonlocal order
        summed[c], order = add(order, wide[c], came_in[c], came_across[c])
        came_out[c] = outward(summed[c])

    def step_score(q):
        nonlocal order
        out, order = score_chunk(
            order,
            [(summed[c], came_out[c]) for c in (q, count + q)],
            True,
            rows,
            eigvals,
            bounds[q][0],
            split,
            query_acts,
            examples,
        )
        scores.append(out)

    step_project(0)
    step_project(1)
    away, mine, order = act_shares(order, cand_act, query_act, basis_a)
    came = swap(away, "sub")
    step_across(0)
    step_project(2)
    half_own, order = half_acts(order, mine, came, cand_ids, query_ids)
    half_over = swap(half_own, "ex")
    own_swapped = swap(half_own, "sub")
    step_outward(0)
    step_across(1)
    step_project(3)
    step_across(2)
    step_outward(1)
    over_swapped = swap(half_over, "sub")
    step_project(4)
    step_across(3)
    step_outward(2)
    split, query_acts, order = split_acts(
        order, cand_offsets, half_own, half_over, own_swapped, over_swapped
    )
    step_project(5)
    step_across(4)
    step_outward(3)
    step_across(5)
    step_outward(4)
    step_score(0)
    step_outward(5)
    step_score(1)
    step_score(2)
    return total_of(scores)


def token_scores_gathered(
    cand_grad, query_grad, cand_act, query_act, cand_ids, query_ids, cand_offsets, basis_g, basis_a, eigvals
):
    gather = lambda a: lax.all_gather(a, "ex", axis=0, tiled=True)
    examples = cand_offsets.shape[0]
    features = basis_a.shape[1]
    order = jnp.zeros((8, 128), F32)
    keep = lambda ids: (ids != PAD).astype(BF16)[:, None]
    share = lambda a: lax.psum(jnp.dot(a, basis_a, preferred_element_type=F32), "sub")
    cands = gather(share(cand_act).astype(BF16) * keep(cand_ids))
    query_acts = gather(share(query_act).astype(BF16) * keep(query_ids))
    cand_rows = cands.shape[0]
    positions = jnp.arange(cand_rows, dtype=jnp.int32)
    example_ends = jnp.concatenate([cand_offsets[1:], jnp.full((1,), cand_rows, jnp.int32)])
    member = (positions[:, None] >= cand_offsets[None, :]) & (
        positions[:, None] < example_ends[None, :]
    )
    split = (member.astype(BF16)[:, :, None] * cands[:, None, :]).reshape(
        cand_rows, examples * features
    )
    tokens = ([gather(cand_grad).T], [gather(query_grad).T])
    scores = []
    for start, width in chunk_bounds(basis_g.shape[1]):
        wide, _, tokens, order = project(order, tokens, basis_g, start, width)
        total = lax.psum(wide, "hid").astype(BF16)
        out, order = score_chunk(
            order, [(total,)], False, cand_rows, eigvals, start, split, query_acts, examples
        )
        scores.append(out)
    return total_of(scores)


def per_device(
    cand_grad,
    query_grad,
    cand_act,
    query_act,
    cand_ids,
    query_ids,
    cand_offsets,
    basis_g,
    basis_a,
    eigvals,
):
    groups = lax.axis_size("ex")
    halves = lax.axis_size("sub")
    ex = lax.axis_index("ex")
    sub = lax.axis_index("sub")
    examples = cand_offsets.shape[0]
    paired = (
        groups == 2
        and halves == 2
        and lax.axis_size("hid") == 4
        and cand_grad.shape[0] == query_grad.shape[0]
    )
    arrays = (
        cand_grad, query_grad, cand_act, query_act, cand_ids, query_ids, cand_offsets, basis_g, basis_a, eigvals
    )
    token_scores = token_scores_paired(*arrays) if paired else token_scores_gathered(*arrays)
    queries = groups * query_grad.shape[0] // QLEN
    partial_value = token_scores.reshape(examples, queries, QLEN).sum(2)
    if paired:
        turned = jnp.roll(partial_value, queries // 2, axis=1)
        partial_value = jnp.where(ex == 0, partial_value, turned)
    total = small_sum(small_sum(partial_value, ("ex", "sub")), "hid")
    mine = lax.dynamic_slice_in_dim(total, sub * (queries // halves), queries // halves, 1)
    factor = 1.0 / math.sqrt(FF * D * QLEN * (TC_DEV // EX_DEV))
    return mine * factor


def solution(mesh):
    return jax.shard_map(
        per_device,
        mesh=mesh,
        in_specs=(
            P(("grp", "ex"), "hid"),
            P(("grp", "ex"), "hid"),
            P(("grp", "ex"), "sub"),
            P(("grp", "ex"), "sub"),
            P(("grp", "ex")),
            P(("grp", "ex")),
            P("grp"),
            P("hid", ("ex", "sub")),
            P("sub", "hid"),
            P("ex", "hid"),
        ),
        out_specs=P("grp", "sub"),
        check_vma=False,
    )
```

time: 462 us -> 184 us (0.40)
  blocking collectives: 218 us -> 0 us
  matrix products: 139 us -> 0 us
  starting transfers between devices: 0.35 us -> 60.3 us
  Pallas kernels: 0 us -> 59.3 us
  local copies, waits for them, and re-layouts: 38.2 us -> 3.75 us
  between operations: 13.2 us -> 0.49 us
  waiting for transfers between devices: 47.4 us -> 58 us
    psum x2 -> x0, blocking collectives: 218 us -> none  [the longest x1 196 us: per_device(): summed_grads = lax.psum(basis_term, 'hid').astype(jnp.bfloat16)]
    dot_general x11 -> x0, matrix products: 139 us -> none  [the longest x8 117 us: one_query(): jnp.dot(cand_eigen_grad, precond, preferred_element_type=jnp.float32)]
    ppermute x0 -> x32, starting transfers between devices: none -> 60.3 us  [the longest x6 30.5 us: token_scores_paired(): inward = lambda a: lax.ppermute(a, 'hid', [(0, 1), (3, 2)])]
    pallas_call x0 -> x24, Pallas kernels: none -> 59.3 us  [the longest x6 30.5 us: project(): pl.pallas_call(functools.partial(project_kernel, terms), grid=(tiles,), i...]
    ppermute x0 -> x32, waiting for transfers between devices: none -> 58 us  [the longest x6 36.3 us: token_scores_paired(): outward = lambda a: lax.ppermute(a, 'hid', [(1, 0), (2, 3)])]
    all_gather x5 -> x0, waiting for transfers between devices: 46.6 us -> none  [the longest x1 42.1 us: per_device(): lax.all_gather(all_grads, 'ex', axis=0, tiled=True)]
    reshape x2 -> x1, local copies, waits for them, and re-layouts: 18.1 us -> 0.08 us  [per_device(): partial_value = token_scores.reshape(examples, queries, QLEN).sum(2)]
    slice x4 -> x1, local copies, waits for them, and re-layouts: 16.8 us -> 0.07 us  [per_device(): turned = jnp.roll(partial_value, queries // 2, axis=1)]
  transfers between devices with their start and end apart: 5 -> 32, of which waited for: 2 -> 16; matrix products, arithmetic and copies ran while one was open for 13% -> 0% of each run, Pallas kernels for 0% -> 29%
where the time goes in v2:
time: 184 us; the launch traced here: 183 us
  starting transfers between devices  60.3 us (33%)
  Pallas kernels  59.3 us (32%)
  waiting for transfers between devices  58 us (32%)
  local copies, waits for them, and re-layouts  3.75 us (2%)
    ppermute x6, waiting for transfers between devices, token_scores_paired(): outward = lambda a: lax.ppermute(a, 'hid', [(1, 0), (2, 3)])  36.3 us
    pallas_call x6, Pallas kernels, project(): pl.pallas_call(functools.partial(project_kernel, terms), grid=(tiles,), i...  30.5 us
    ppermute x6, starting transfers between devices, token_scores_paired(): inward = lambda a: lax.ppermute(a, 'hid', [(0, 1), (3, 2)])  30.5 us
    pallas_call x3, Pallas kernels, score_chunk(): pl.pallas_call(functools.partial(score_kernel, len(blocks), pick, cand_ro...  22 us
    ppermute x6, waiting for transfers between devices, token_scores_paired(): inward = lambda a: lax.ppermute(a, 'hid', [(0, 1), (3, 2)])  10.5 us
    ppermute x6, starting transfers between devices, token_scores_paired(): outward = lambda a: lax.ppermute(a, 'hid', [(1, 0), (2, 3)])  7.91 us
    ppermute x6, starting transfers between devices, small_sum(): lax.ppermute(value, axes, [(i, i ^ other) for i in range(size)])  6.25 us
    ppermute x6, waiting for transfers between devices, small_sum(): lax.ppermute(value, axes, [(i, i ^ other) for i in range(size)])  5.66 us
  transfers between devices with their start and end apart: 32, of which 16 were waited for; matrix products, arithmetic and copies ran while one was open for 0% of the time, Pallas kernels for 29%

profile of v2, /device:TPU:0, one launch (start us, length us, event | category | flops | bytes accessed | tf_op | source)
XLA Modules:
  0.0 182.7 jit_solution(3947756742916951325)
XLA Ops:
  0.0 4.8 %collective-permute-start.4 = (bf16[128,2752]{0,1:T(8,128)(2,1)}, bf16[128,2752]{0,1:T(8,128)(2,1)S(1)}, u32[]{:S(2)}, u32[]{:S(2)}) collective-permute-start(bf16[128,2752]{0,1:T(8,128)(2,1)} %param.10), channel_id=1, source_target_pairs={{0,2},{2,0},{4,6},{6,4},{8,10},{10,8},{12,14},{14,12},{16,18},{18,... | collective-permute-start | bytes 2113544 | tf_op jit(solution)/shard_map/ppermute | solution.py:336
  5.6 1.1 copy-done.4
  6.7 1.1 copy-done.5
  7.8 6.1 %project.6 = (f32[256,1024]{1,0:T(8,128)S(1)}, bf16[256,1024]{1,0:T(8,128)(2,1)S(1)}, bf16[256,2752]{1,0:T(8,128)(2,1)}, f32[8,128]{1,0:T(8,128)S(1)}) custom-call(f32[8,128]{1,0:T(8,128)S(1)} %broadcast_in_dim.9.order_ref, bf16[2752,128]{1,0:T(8,128)(2,1)S(1)} %bitcast.8, bf16[2752,128]{1,0:T(8,128)(2,1)S(1)} %bitcast.9, bf16[2752,2752]{1,0:T(8,128)(2,1)} %refs_1_.7), custom_call_target="tpu_custom_call" | custom-call | flops 1024 | bytes 1024 | tf_op jit(solution)/shard_map/project/pallas_call | solution.py:90
  13.9 3.5 %collective-permute-start = (bf16[256,1024]{1,0:T(8,128)(2,1)S(1)}, bf16[256,1024]{1,0:T(8,128)(2,1)S(1)}, u32[]{:S(2)}, u32[]{:S(2)}) collective-permute-start(bf16[256,1024]{1,0:T(8,128)(2,1)S(1)} %get-tuple-element.67), channel_id=1, source_target_pairs={{0,4},{12,8},{1,5},{13,9},{2,6},{14,10},{3,7},{15,11},{16,20},{28,... | collective-permute-start | bytes 1572872 | tf_op jit(solution)/shard_map/ppermute | solution.py:332
  17.4 4.1 %collective-permute-done.4 = bf16[128,2752]{0,1:T(8,128)(2,1)S(1)} collective-permute-done((bf16[128,2752]{0,1:T(8,128)(2,1)}, bf16[128,2752]{0,1:T(8,128)(2,1)S(1)}, u32[]{:S(2)}, u32[]{:S(2)}) %collective-permute-start.4) | collective-permute-done | bytes 704544 | tf_op jit(solution)/shard_map/ppermute | solution.py:336
  21.5 1.3 collective-permute-start.5
  22.9 1.3 collective-permute-start.7
  24.2 1.4 copy-done.1
  25.6 5.7 %project.7 = (f32[256,1024]{1,0:T(8,128)S(1)}, bf16[256,1024]{1,0:T(8,128)(2,1)}, f32[8,128]{1,0:T(8,128)S(1)}) custom-call(f32[8,128]{1,0:T(8,128)S(1)} %get-tuple-element.62.order_ref, bf16[256,2752]{1,0:T(8,128)(2,1)S(1)} %copy-done.1, bf16[2752,2752]{1,0:T(8,128)(2,1)} %refs_1_.7), custom_call_target="tpu_custom_call" | custom-call | flops 1024 | bytes 1024 | tf_op jit(solution)/shard_map/project/pallas_call | solution.py:90
  31.2 2.6 %acts.1 = (f32[128,1024]{1,0:T(8,128)S(1)}, f32[128,1024]{1,0:T(8,128)S(1)}, f32[8,128]{1,0:T(8,128)S(1)}) custom-call(f32[8,128]{1,0:T(8,128)S(1)} %get-tuple-element.64.order_ref, bf16[128,2048]{1,0:T(8,128)(2,1)S(1)} %copy-done.6, bf16[128,2048]{1,0:T(8,128)(2,1)S(1)} %copy-done.7, bf16[2048,1024]{1,0:T(8,128)(2,1)S(1)} %copy-done.2), custom_call_target="tpu_custom_call" | custom-call | flops 1024 | bytes 1024 | tf_op jit(solution)/shard_map/acts/pallas_call | solution.py:131
  33.9 1.2 collective-permute-start.1
  35.9 6.5 %collective-permute-start.3 = (bf16[256,1024]{1,0:T(8,128)(2,1)}, bf16[256,1024]{1,0:T(8,128)(2,1)S(1)}, u32[]{:S(2)}, u32[]{:S(2)}) collective-permute-start(bf16[256,1024]{1,0:T(8,128)(2,1)} %get-tuple-element.76), channel_id=1, source_target_pairs={{0,4},{12,8},{1,5},{13,9},{2,6},{14,10},{3,7},{15,11},{16,20},{28,... | collective-permute-start | bytes 1572872 | tf_op jit(solution)/shard_map/ppermute | solution.py:332
  42.5 3.9 %project.8 = (f32[256,704]{1,0:T(8,128)S(1)}, bf16[256,704]{1,0:T(8,128)(2,1)S(1)}, f32[8,128]{1,0:T(8,128)S(1)}) custom-call(f32[8,128]{1,0:T(8,128)S(1)} %get-tuple-element.68.order_ref, bf16[256,2752]{1,0:T(8,128)(2,1)S(1)} %copy-done.1, bf16[2752,2752]{1,0:T(8,128)(2,1)} %refs_1_.7), custom_call_target="tpu_custom_call" | custom-call | flops 1024 | bytes 1024 | tf_op jit(solution)/shard_map/project/pallas_call | solution.py:90
  46.8 7.0 %collective-permute-done.3.refs_1_ = bf16[256,1024]{1,0:T(8,128)(2,1)S(1)} collective-permute-done((bf16[256,1024]{1,0:T(8,128)(2,1)}, bf16[256,1024]{1,0:T(8,128)(2,1)S(1)}, u32[]{:S(2)}, u32[]{:S(2)}) %collective-permute-start.3) | collective-permute-done | bytes 524320 | tf_op jit(solution)/shard_map/ppermute | solution.py:332
  54.6 6.0 %collective-permute-start.8 = (bf16[256,704]{1,0:T(8,128)(2,1)S(1)}, bf16[256,704]{1,0:T(8,128)(2,1)S(1)}, u32[]{:S(2)}, u32[]{:S(2)}) collective-permute-start(bf16[256,704]{1,0:T(8,128)(2,1)S(1)} %get-tuple-element.80), channel_id=1, source_target_pairs={{0,4},{12,8},{1,5},{13,9},{2,6},{14,10},{3,7},{15,11},{16,20},{28,... | collective-permute-start | bytes 1081352 | tf_op jit(solution)/shard_map/ppermute | solution.py:332
  60.6 6.3 %project.9 = (f32[256,1024]{1,0:T(8,128)}, bf16[256,1024]{1,0:T(8,128)(2,1)S(1)}, bf16[256,2752]{1,0:T(8,128)(2,1)}, f32[8,128]{1,0:T(8,128)S(1)}) custom-call(f32[8,128]{1,0:T(8,128)S(1)} %get-tuple-element.77.order_ref, bf16[2752,128]{1,0:T(8,128)(2,1)S(1)} %bitcast.10, bf16[2752,128]{1,0:T(8,128)(2,1)S(1)} %bitcast.12, bf16[2752,128]{1,0:T(8,128)(2,1)S(1)} %bitcast.11, ...), custom_call_target="tpu_custom_call" | custom-call | flops 1024 | bytes 1024 | tf_op jit(solution)/shard_map/project/pallas_call | solution.py:90
  66.9 1.4 collective-permute-start.10
  68.4 1.6 collective-permute-start.12
  70.0 0.9 add.60
  71.0 4.7 %project.10 = (f32[256,1024]{1,0:T(8,128)S(1)}, bf16[256,1024]{1,0:T(8,128)(2,1)S(1)}, f32[8,128]{1,0:T(8,128)S(1)}) custom-call(f32[8,128]{1,0:T(8,128)S(1)} %get-tuple-element.83.order_ref, bf16[256,2752]{1,0:T(8,128)(2,1)S(1)} %copy-done, bf16[2752,2752]{1,0:T(8,128)(2,1)} %refs_1_.7), custom_call_target="tpu_custom_call" | custom-call | flops 1024 | bytes 1024 | tf_op jit(solution)/shard_map/project/pallas_call | solution.py:90
  75.7 2.7 %collective-permute-start.15 = (bf16[256,1024]{1,0:T(8,128)(2,1)S(1)}, bf16[256,1024]{1,0:T(8,128)(2,1)S(1)}, u32[]{:S(2)}, u32[]{:S(2)}) collective-permute-start(bf16[256,1024]{1,0:T(8,128)(2,1)S(1)} %get-tuple-element.95), channel_id=1, source_target_pairs={{0,4},{12,8},{1,5},{13,9},{2,6},{14,10},{3,7},{15,11},{16,20},{28,... | collective-permute-start | bytes 1572872 | tf_op jit(solution)/shard_map/ppermute | solution.py:332
  79.1 1.6 collective-permute-done.10.refs_1_
  82.2 0.9 collective-permute-done.13.own_sw
  84.3 3.9 %project.11 = (f32[256,704]{1,0:T(8,128)S(1)}, bf16[256,704]{1,0:T(8,128)(2,1)S(1)}, f32[8,128]{1,0:T(8,128)S(1)}) custom-call(f32[8,128]{1,0:T(8,128)S(1)} %get-tuple-element.92.order_ref, bf16[256,2752]{1,0:T(8,128)(2,1)S(1)} %copy-done, bf16[2752,2752]{1,0:T(8,128)(2,1)} %refs_1_.7), custom_call_target="tpu_custom_call" | custom-call | flops 1024 | bytes 1024 | tf_op jit(solution)/shard_map/project/pallas_call | solution.py:90
  88.2 10.3 %collective-permute-start.17 = (bf16[256,704]{1,0:T(8,128)(2,1)S(1)}, bf16[256,704]{1,0:T(8,128)(2,1)S(1)}, u32[]{:S(2)}, u32[]{:S(2)}) collective-permute-start(bf16[256,704]{1,0:T(8,128)(2,1)S(1)} %get-tuple-element.100), channel_id=1, source_target_pairs={{0,4},{12,8},{1,5},{13,9},{2,6},{14,10},{3,7},{15,11},{16,20},{28,... | collective-permute-start | bytes 1081352 | tf_op jit(solution)/shard_map/ppermute | solution.py:332
  99.3 1.3 collective-permute-start.19
  100.8 1.3 collective-permute-start.20
  102.1 1.9 %collective-permute-done.17.refs_1_ = bf16[256,704]{1,0:T(8,128)(2,1)S(1)} collective-permute-done((bf16[256,704]{1,0:T(8,128)(2,1)S(1)}, bf16[256,704]{1,0:T(8,128)(2,1)S(1)}, u32[]{:S(2)}, u32[]{:S(2)}) %collective-permute-start.17) | collective-permute-done | bytes 360480 | tf_op jit(solution)/shard_map/ppermute | solution.py:332
  104.8 1.3 collective-permute-start.22
  106.1 1.0 add.66
  107.1 1.3 collective-permute-start.23
  108.4 7.7 %collective-permute-done.19.refs_1_ = bf16[256,1024]{1,0:T(8,128)(2,1)S(1)} collective-permute-done((bf16[256,1024]{1,0:T(8,128)(2,1)S(1)}, bf16[256,1024]{1,0:T(8,128)(2,1)S(1)}, u32[]{:S(2)}, u32[]{:S(2)}) %collective-permute-start.19) | collective-permute-done | bytes 524320 | tf_op jit(solution)/shard_map/ppermute | solution.py:334
  116.1 1.5 collective-permute-start.24
  117.6 9.8 %collective-permute-done.20.refs_3_ = bf16[256,1024]{1,0:T(8,128)(2,1)S(1)} collective-permute-done((bf16[256,1024]{1,0:T(8,128)(2,1)S(1)}, bf16[256,1024]{1,0:T(8,128)(2,1)S(1)}, u32[]{:S(2)}, u32[]{:S(2)}) %collective-permute-start.20) | collective-permute-done | bytes 524320 | tf_op jit(solution)/shard_map/ppermute | solution.py:334
  127.3 6.6 %score.3 = (f32[4,256]{1,0:T(4,128)S(1)}, f32[8,128]{1,0:T(8,128)S(1)}) custom-call(f32[8,128]{1,0:T(8,128)S(1)} %get-tuple-element.103.order_ref, bf16[256,1024]{1,0:T(8,128)(2,1)S(1)} %get-tuple-element.104.refs_0_, bf16[256,1024]{1,0:T(8,128)(2,1)S(1)} %collective-permute-done.19.refs_1_, bf16[256,1024]{1,0:T(8,128)(2,1)S(1)} %get-tuple-element.105.refs_2_, ...), custom_call_target="tpu_custom_call" | custom-call | flops 1024 | bytes 1024 | tf_op jit(solution)/shard_map/score/pallas_call | solution.py:296
  134.1 1.3 collective-permute-start.25
  135.5 3.2 %collective-permute-done.22.refs_1_ = bf16[256,1024]{1,0:T(8,128)(2,1)} collective-permute-done((bf16[256,1024]{1,0:T(8,128)(2,1)}, bf16[256,1024]{1,0:T(8,128)(2,1)}, u32[]{:S(2)}, u32[]{:S(2)}) %collective-permute-start.22) | collective-permute-done | bytes 524320 | tf_op jit(solution)/shard_map/ppermute | solution.py:334
  138.7 11.2 %collective-permute-done.23.refs_3_ = bf16[256,1024]{1,0:T(8,128)(2,1)} collective-permute-done((bf16[256,1024]{1,0:T(8,128)(2,1)}, bf16[256,1024]{1,0:T(8,128)(2,1)}, u32[]{:S(2)}, u32[]{:S(2)}) %collective-permute-start.23) | collective-permute-done | bytes 524320 | tf_op jit(solution)/shard_map/ppermute | solution.py:334
  149.9 8.1 %score.4 = (f32[4,256]{1,0:T(4,128)S(1)}, f32[8,128]{1,0:T(8,128)S(1)}) custom-call(f32[8,128]{1,0:T(8,128)S(1)} %get-tuple-element.111.order_ref, bf16[256,1024]{1,0:T(8,128)(2,1)} %get-tuple-element.112.refs_0_, bf16[256,1024]{1,0:T(8,128)(2,1)} %collective-permute-done.22.refs_1_, bf16[256,1024]{1,0:T(8,128)(2,1)} %get-tuple-element.113.refs_2_, ...), custom_call_target="tpu_custom_call" | custom-call | flops 1024 | bytes 1024 | tf_op jit(solution)/shard_map/score/pallas_call | solution.py:296
  158.3 4.2 %collective-permute-done.25.refs_3_ = bf16[256,704]{1,0:T(8,128)(2,1)} collective-permute-done((bf16[256,704]{1,0:T(8,128)(2,1)S(1)}, bf16[256,704]{1,0:T(8,128)(2,1)}, u32[]{:S(2)}, u32[]{:S(2)}) %collective-permute-start.25) | collective-permute-done | bytes 360480 | tf_op jit(solution)/shard_map/ppermute | solution.py:334
  162.5 7.3 %score.5 = (f32[4,256]{1,0:T(4,128)S(1)}, f32[8,128]{1,0:T(8,128)}) custom-call(f32[8,128]{1,0:T(8,128)S(1)} %get-tuple-element.115.order_ref, bf16[256,704]{1,0:T(8,128)(2,1)S(1)} %get-tuple-element.116.refs_0_, bf16[256,704]{1,0:T(8,128)(2,1)} %collective-permute-done.24.refs_1_, bf16[256,704]{1,0:T(8,128)(2,1)S(1)} %get-tuple-element.117.refs_2_, ...), custom_call_target="tpu_custom_call" | custom-call | flops 1024 | bytes 1024 | tf_op jit(solution)/shard_map/score/pallas_call | solution.py:296
  170.1 1.6 collective-permute-start.27
  172.0 1.8 collective-permute-done.27
  173.8 1.0 collective-permute-done.28
  174.7 1.9 %collective-permute-start.30 = (f32[4,16]{1,0:T(4,128)S(1)}, f32[4,16]{1,0:T(4,128)S(1)}, u32[]{:S(2)}, u32[]{:S(2)}) collective-permute-start(f32[4,16]{1,0:T(4,128)S(1)} %add_add_fusion.2), channel_id=1, source_target_pairs={{0,8},{4,12},{8,0},{12,4},{1,9},{5,13},{9,1},{13,5},{2,10},{6,14},... | collective-permute-start | bytes 776 | tf_op jit(solution)/shard_map/ppermute | solution.py:317
  176.6 2.5 %collective-permute-start.31 = (f32[4,16]{1,0:T(4,128)S(1)}, f32[4,16]{1,0:T(4,128)S(1)}, u32[]{:S(2)}, u32[]{:S(2)}) collective-permute-start(f32[4,16]{1,0:T(4,128)S(1)} %add_add_fusion.2), channel_id=1, source_target_pairs={{0,12},{4,8},{8,4},{12,0},{1,13},{5,9},{9,5},{13,1},{2,14},{6,10},... | collective-permute-start | bytes 776 | tf_op jit(solution)/shard_map/ppermute | solution.py:317
  179.3 2.7 %collective-permute-done.31 = f32[4,16]{1,0:T(4,128)S(1)} collective-permute-done((f32[4,16]{1,0:T(4,128)S(1)}, f32[4,16]{1,0:T(4,128)S(1)}, u32[]{:S(2)}, u32[]{:S(2)}) %collective-permute-start.31) | collective-permute-done | bytes 288 | tf_op jit(solution)/shard_map/ppermute | solution.py:317
  (71 shorter events, 9.8 us)
Async XLA Ops:
  0.0 21.5 %collective-permute-start.4 = (bf16[128,2752]{0,1:T(8,128)(2,1)}, bf16[128,2752]{0,1:T(8,128)(2,1)S(1)}, u32[]{:S(2)}, u32[]{:S(2)}) collective-permute-start(bf16[128,2752]{0,1:T(8,128)(2,1)} %param.10), channel_id=1, source_target_pairs={{0,2},{2,0},{4,6},{6,4},{8,10},{10,8},{12,14},{14,12},{16,18},{18,... | collective-permute-start | bytes 2113544 | tf_op jit(solution)/shard_map/ppermute | solution.py:336
  4.8 18.0 %collective-permute-start.6 = (bf16[128,2752]{0,1:T(8,128)(2,1)}, bf16[128,2752]{0,1:T(8,128)(2,1)S(1)}, u32[]{:S(2)}, u32[]{:S(2)}) collective-permute-start(bf16[128,2752]{0,1:T(8,128)(2,1)} %param.11), channel_id=1, source_target_pairs={{1,3},{3,1},{5,7},{7,5},{9,11},{11,9},{13,15},{15,13},{17,19},{19,... | collective-permute-start | bytes 2113544 | tf_op jit(solution)/shard_map/ppermute | solution.py:337
  5.6 1.1 copy-start.4
  6.7 1.1 copy-start.5
  13.9 21.2 %collective-permute-start = (bf16[256,1024]{1,0:T(8,128)(2,1)S(1)}, bf16[256,1024]{1,0:T(8,128)(2,1)S(1)}, u32[]{:S(2)}, u32[]{:S(2)}) collective-permute-start(bf16[256,1024]{1,0:T(8,128)(2,1)S(1)} %get-tuple-element.67), channel_id=1, source_target_pairs={{0,4},{12,8},{1,5},{13,9},{2,6},{14,10},{3,7},{15,11},{16,20},{28,... | collective-permute-start | bytes 1572872 | tf_op jit(solution)/shard_map/ppermute | solution.py:332
  21.5 39.0 %collective-permute-start.5 = (bf16[128,2752]{0,1:T(8,128)(2,1)S(1)}, bf16[128,2752]{0,1:T(8,128)(2,1)S(1)}, u32[]{:S(2)}, u32[]{:S(2)}) collective-permute-start(bf16[128,2752]{0,1:T(8,128)(2,1)S(1)} %collective-permute-done.4), channel_id=1, source_target_pairs={{0,1},{2,3},{4,5},{6,7},{8,9},{10,11},{12,13},{14,15},{16,17},{18,... | collective-permute-start | bytes 2113544 | tf_op jit(solution)/shard_map/ppermute | solution.py:338
  22.9 37.7 %collective-permute-start.7 = (bf16[128,2752]{0,1:T(8,128)(2,1)S(1)}, bf16[128,2752]{0,1:T(8,128)(2,1)S(1)}, u32[]{:S(2)}, u32[]{:S(2)}) collective-permute-start(bf16[128,2752]{0,1:T(8,128)(2,1)S(1)} %collective-permute-done.6), channel_id=1, source_target_pairs={{1,0},{3,2},{5,4},{7,6},{9,8},{11,10},{13,12},{15,14},{17,16},{19,... | collective-permute-start | bytes 2113544 | tf_op jit(solution)/shard_map/ppermute | solution.py:339
  24.2 1.4 copy-start.1
  25.5 5.7 %copy-start.2 = (bf16[2048,1024]{1,0:T(8,128)(2,1)S(1)}, bf16[2048,1024]{1,0:T(8,128)(2,1)}, u32[]{:S(2)}) copy-start(bf16[2048,1024]{1,0:T(8,128)(2,1)} %basis_ref.1) | copy-start | bytes 12582916
  25.5 5.7 %copy-start.6 = (bf16[128,2048]{1,0:T(8,128)(2,1)S(1)}, bf16[128,2048]{1,0:T(8,128)(2,1)}, u32[]{:S(2)}) copy-start(bf16[128,2048]{1,0:T(8,128)(2,1)} %cand_ref.1) | copy-start | bytes 1572868
  25.5 5.7 %copy-start.7 = (bf16[128,2048]{1,0:T(8,128)(2,1)S(1)}, bf16[128,2048]{1,0:T(8,128)(2,1)}, u32[]{:S(2)}) copy-start(bf16[128,2048]{1,0:T(8,128)(2,1)} %query_ref.1) | copy-start | bytes 1572868
  33.9 12.5 %collective-permute-start.1 = (f32[128,1024]{1,0:T(8,128)S(1)}, f32[128,1024]{1,0:T(8,128)S(1)}, u32[]{:S(2)}, u32[]{:S(2)}) collective-permute-start(f32[128,1024]{1,0:T(8,128)S(1)} %get-tuple-element.71), channel_id=1, source_target_pairs={{0,1},{1,0},{2,3},{3,2},{4,5},{5,4},{6,7},{7,6},{8,9},{9,8},{10,11... | collective-permute-start | bytes 1572872 | tf_op jit(solution)/shard_map/ppermute | solution.py:331
  35.2 11.4 %collective-permute-start.2 = (bf16[256,1024]{1,0:T(8,128)(2,1)S(1)}, bf16[256,1024]{1,0:T(8,128)(2,1)S(1)}, u32[]{:S(2)}, u32[]{:S(2)}) collective-permute-start(bf16[256,1024]{1,0:T(8,128)(2,1)S(1)} %get-tuple-element.73), channel_id=1, source_target_pairs={{4,8},{8,4},{5,9},{9,5},{6,10},{10,6},{7,11},{11,7},{20,24},{24,20... | collective-permute-start | bytes 1572872 | tf_op jit(solution)/shard_map/ppermute | solution.py:333
  35.9 17.9 %collective-permute-start.3 = (bf16[256,1024]{1,0:T(8,128)(2,1)}, bf16[256,1024]{1,0:T(8,128)(2,1)S(1)}, u32[]{:S(2)}, u32[]{:S(2)}) collective-permute-start(bf16[256,1024]{1,0:T(8,128)(2,1)} %get-tuple-element.76), channel_id=1, source_target_pairs={{0,4},{12,8},{1,5},{13,9},{2,6},{14,10},{3,7},{15,11},{16,20},{28,... | collective-permute-start | bytes 1572872 | tf_op jit(solution)/shard_map/ppermute | solution.py:332
  42.4 3.9 %copy-start.8 = (s32[128]{0:T(128)S(1)}, s32[128]{0:T(128)}, u32[]{:S(2)}) copy-start(s32[128]{0:T(128)} %param.14) | copy-start | bytes 1540
  42.5 3.9 %copy-start.9 = (s32[128]{0:T(128)S(1)}, s32[128]{0:T(128)}, u32[]{:S(2)}) copy-start(s32[128]{0:T(128)} %param.15) | copy-start | bytes 1540
  53.9 16.1 %collective-permute-start.9 = (bf16[256,1024]{1,0:T(8,128)(2,1)S(1)}, bf16[256,1024]{1,0:T(8,128)(2,1)S(1)}, u32[]{:S(2)}, u32[]{:S(2)}) collective-permute-start(bf16[256,1024]{1,0:T(8,128)(2,1)S(1)} %get-tuple-element.82), channel_id=1, source_target_pairs={{4,8},{8,4},{5,9},{9,5},{6,10},{10,6},{7,11},{11,7},{20,24},{24,20... | collective-permute-start | bytes 1572872 | tf_op jit(solution)/shard_map/ppermute | solution.py:333
  54.6 15.4 %collective-permute-start.8 = (bf16[256,704]{1,0:T(8,128)(2,1)S(1)}, bf16[256,704]{1,0:T(8,128)(2,1)S(1)}, u32[]{:S(2)}, u32[]{:S(2)}) collective-permute-start(bf16[256,704]{1,0:T(8,128)(2,1)S(1)} %get-tuple-element.80), channel_id=1, source_target_pairs={{0,4},{12,8},{1,5},{13,9},{2,6},{14,10},{3,7},{15,11},{16,20},{28,... | collective-permute-start | bytes 1081352 | tf_op jit(solution)/shard_map/ppermute | solution.py:332
  66.9 4.1 %copy-start = (bf16[256,2752]{1,0:T(8,128)(2,1)S(1)}, bf16[256,2752]{1,0:T(8,128)(2,1)}, u32[]{:S(2)}) copy-start(bf16[256,2752]{1,0:T(8,128)(2,1)} %get-tuple-element.84.refs_0_) | copy-start | bytes 4227076
  66.9 13.8 %collective-permute-start.10 = (bf16[256,1024]{1,0:T(8,128)(2,1)S(1)}, bf16[256,1024]{1,0:T(8,128)(2,1)S(1)}, u32[]{:S(2)}, u32[]{:S(2)}) collective-permute-start(bf16[256,1024]{1,0:T(8,128)(2,1)S(1)} %get-tuple-element.87), channel_id=1, source_target_pairs={{0,4},{12,8},{1,5},{13,9},{2,6},{14,10},{3,7},{15,11},{16,20},{28,... | collective-permute-start | bytes 1572872 | tf_op jit(solution)/shard_map/ppermute | solution.py:332
  68.4 13.2 %collective-permute-start.12 = (bf16[128,1024]{1,0:T(8,128)(2,1)S(1)}, bf16[128,1024]{1,0:T(8,128)(2,1)S(1)}, u32[]{:S(2)}, u32[]{:S(2)}) collective-permute-start(bf16[128,1024]{1,0:T(8,128)(2,1)S(1)} %get-tuple-element.91.own), channel_id=1, source_target_pairs={{0,2},{2,0},{1,3},{3,1},{4,6},{6,4},{5,7},{7,5},{8,10},{10,8},{9,1... | collective-permute-start | bytes 786440 | tf_op jit(solution)/shard_map/ppermute | solution.py:331
  71.0 9.7 %copy-start.3 = (f32[256,1024]{1,0:T(8,128)S(1)}, f32[256,1024]{1,0:T(8,128)}, u32[]{:S(2)}) copy-start(f32[256,1024]{1,0:T(8,128)} %get-tuple-element.86.refs_0_) | copy-start | bytes 3145732
  71.0 12.5 %copy-start.10 = (s32[4]{0:T(128)S(1)}, s32[4]{0:T(128)}, u32[]{:S(2)}) copy-start(s32[4]{0:T(128)} %offsets_ref.1) | copy-start | bytes 52
  75.7 22.9 %collective-permute-start.15 = (bf16[256,1024]{1,0:T(8,128)(2,1)S(1)}, bf16[256,1024]{1,0:T(8,128)(2,1)S(1)}, u32[]{:S(2)}, u32[]{:S(2)}) collective-permute-start(bf16[256,1024]{1,0:T(8,128)(2,1)S(1)} %get-tuple-element.95), channel_id=1, source_target_pairs={{0,4},{12,8},{1,5},{13,9},{2,6},{14,10},{3,7},{15,11},{16,20},{28,... | collective-permute-start | bytes 1572872 | tf_op jit(solution)/shard_map/ppermute | solution.py:332
  78.4 3.7 %collective-permute-start.11 = (bf16[256,704]{1,0:T(8,128)(2,1)S(1)}, bf16[256,704]{1,0:T(8,128)(2,1)S(1)}, u32[]{:S(2)}, u32[]{:S(2)}) collective-permute-start(bf16[256,704]{1,0:T(8,128)(2,1)S(1)} %get-tuple-element.89), channel_id=1, source_target_pairs={{4,8},{8,4},{5,9},{9,5},{6,10},{10,6},{7,11},{11,7},{20,24},{24,20... | collective-permute-start | bytes 1081352 | tf_op jit(solution)/shard_map/ppermute | solution.py:333
  80.8 19.8 %collective-permute-start.16 = (bf16[256,1024]{1,0:T(8,128)(2,1)S(1)}, bf16[256,1024]{1,0:T(8,128)(2,1)S(1)}, u32[]{:S(2)}, u32[]{:S(2)}) collective-permute-start(bf16[256,1024]{1,0:T(8,128)(2,1)S(1)} %get-tuple-element.97), channel_id=1, source_target_pairs={{4,8},{8,4},{5,9},{9,5},{6,10},{10,6},{7,11},{11,7},{20,24},{24,20... | collective-permute-start | bytes 1572872 | tf_op jit(solution)/shard_map/ppermute | solution.py:333
  81.5 1.6 collective-permute-start.13
  81.6 1.9 %collective-permute-start.14 = (bf16[128,1024]{1,0:T(8,128)(2,1)S(1)}, bf16[128,1024]{1,0:T(8,128)(2,1)S(1)}, u32[]{:S(2)}, u32[]{:S(2)}) collective-permute-start(bf16[128,1024]{1,0:T(8,128)(2,1)S(1)} %collective-permute-done.12.over), channel_id=1, source_target_pairs={{0,1},{1,0},{2,3},{3,2},{4,5},{5,4},{6,7},{7,6},{8,9},{9,8},{10,11... | collective-permute-start | bytes 786440 | tf_op jit(solution)/shard_map/ppermute | solution.py:331
  88.2 15.8 %collective-permute-start.17 = (bf16[256,704]{1,0:T(8,128)(2,1)S(1)}, bf16[256,704]{1,0:T(8,128)(2,1)S(1)}, u32[]{:S(2)}, u32[]{:S(2)}) collective-permute-start(bf16[256,704]{1,0:T(8,128)(2,1)S(1)} %get-tuple-element.100), channel_id=1, source_target_pairs={{0,4},{12,8},{1,5},{13,9},{2,6},{14,10},{3,7},{15,11},{16,20},{28,... | collective-permute-start | bytes 1081352 | tf_op jit(solution)/shard_map/ppermute | solution.py:332
  98.6 7.5 %collective-permute-start.18 = (bf16[256,1024]{1,0:T(8,128)(2,1)S(1)}, bf16[256,1024]{1,0:T(8,128)(2,1)S(1)}, u32[]{:S(2)}, u32[]{:S(2)}) collective-permute-start(bf16[256,1024]{1,0:T(8,128)(2,1)S(1)} %get-tuple-element.102), channel_id=1, source_target_pairs={{4,8},{8,4},{5,9},{9,5},{6,10},{10,6},{7,11},{11,7},{20,24},{24,20... | collective-permute-start | bytes 1572872 | tf_op jit(solution)/shard_map/ppermute | solution.py:333
  99.3 16.8 %collective-permute-start.19 = (bf16[256,1024]{1,0:T(8,128)(2,1)S(1)}, bf16[256,1024]{1,0:T(8,128)(2,1)S(1)}, u32[]{:S(2)}, u32[]{:S(2)}) collective-permute-start(bf16[256,1024]{1,0:T(8,128)(2,1)S(1)} %get-tuple-element.104.refs_0_), channel_id=1, source_target_pairs={{4,0},{8,12},{5,1},{9,13},{6,2},{10,14},{7,3},{11,15},{20,16},{24,... | collective-permute-start | bytes 1572872 | tf_op jit(solution)/shard_map/ppermute | solution.py:334
  100.8 26.5 %collective-permute-start.20 = (bf16[256,1024]{1,0:T(8,128)(2,1)S(1)}, bf16[256,1024]{1,0:T(8,128)(2,1)S(1)}, u32[]{:S(2)}, u32[]{:S(2)}) collective-permute-start(bf16[256,1024]{1,0:T(8,128)(2,1)S(1)} %get-tuple-element.105.refs_2_), channel_id=1, source_target_pairs={{4,0},{8,12},{5,1},{9,13},{6,2},{10,14},{7,3},{11,15},{20,16},{24,... | collective-permute-start | bytes 1572872 | tf_op jit(solution)/shard_map/ppermute | solution.py:334
  104.1 29.8 %collective-permute-start.21 = (bf16[256,704]{1,0:T(8,128)(2,1)S(1)}, bf16[256,704]{1,0:T(8,128)(2,1)S(1)}, u32[]{:S(2)}, u32[]{:S(2)}) collective-permute-start(bf16[256,704]{1,0:T(8,128)(2,1)S(1)} %get-tuple-element.110), channel_id=1, source_target_pairs={{4,8},{8,4},{5,9},{9,5},{6,10},{10,6},{7,11},{11,7},{20,24},{24,20... | collective-permute-start | bytes 1081352 | tf_op jit(solution)/shard_map/ppermute | solution.py:333
  104.8 33.8 %collective-permute-start.22 = (bf16[256,1024]{1,0:T(8,128)(2,1)}, bf16[256,1024]{1,0:T(8,128)(2,1)}, u32[]{:S(2)}, u32[]{:S(2)}) collective-permute-start(bf16[256,1024]{1,0:T(8,128)(2,1)} %get-tuple-element.112.refs_0_), channel_id=1, source_target_pairs={{4,0},{8,12},{5,1},{9,13},{6,2},{10,14},{7,3},{11,15},{20,16},{24,... | collective-permute-start | bytes 1572872 | tf_op jit(solution)/shard_map/ppermute | solution.py:334
  107.1 42.8 %collective-permute-start.23 = (bf16[256,1024]{1,0:T(8,128)(2,1)}, bf16[256,1024]{1,0:T(8,128)(2,1)}, u32[]{:S(2)}, u32[]{:S(2)}) collective-permute-start(bf16[256,1024]{1,0:T(8,128)(2,1)} %get-tuple-element.113.refs_2_), channel_id=1, source_target_pairs={{4,0},{8,12},{5,1},{9,13},{6,2},{10,14},{7,3},{11,15},{20,16},{24,... | collective-permute-start | bytes 1572872 | tf_op jit(solution)/shard_map/ppermute | solution.py:334
  116.1 42.2 %collective-permute-start.24 = (bf16[256,704]{1,0:T(8,128)(2,1)S(1)}, bf16[256,704]{1,0:T(8,128)(2,1)}, u32[]{:S(2)}, u32[]{:S(2)}) collective-permute-start(bf16[256,704]{1,0:T(8,128)(2,1)S(1)} %get-tuple-element.116.refs_0_), channel_id=1, source_target_pairs={{4,0},{8,12},{5,1},{9,13},{6,2},{10,14},{7,3},{11,15},{20,16},{24,... | collective-permute-start | bytes 1081352 | tf_op jit(solution)/shard_map/ppermute | solution.py:334
  134.1 28.3 %collective-permute-start.25 = (bf16[256,704]{1,0:T(8,128)(2,1)S(1)}, bf16[256,704]{1,0:T(8,128)(2,1)}, u32[]{:S(2)}, u32[]{:S(2)}) collective-permute-start(bf16[256,704]{1,0:T(8,128)(2,1)S(1)} %get-tuple-element.117.refs_2_), channel_id=1, source_target_pairs={{4,0},{8,12},{5,1},{9,13},{6,2},{10,14},{7,3},{11,15},{20,16},{24,... | collective-permute-start | bytes 1081352 | tf_op jit(solution)/shard_map/ppermute | solution.py:334
  170.1 1.9 %collective-permute-start.26 = (f32[4,16]{1,0:T(4,128)S(1)}, f32[4,16]{1,0:T(4,128)S(1)}, u32[]{:S(2)}, u32[]{:S(2)}) collective-permute-start(f32[4,16]{1,0:T(4,128)S(1)} %maximum_select_fusion), channel_id=1, source_target_pairs={{0,1},{1,0},{2,3},{3,2},{4,5},{5,4},{6,7},{7,6},{8,9},{9,8},{10,11... | collective-permute-start | bytes 776 | tf_op jit(solution)/shard_map/ppermute | solution.py:317
  170.1 3.7 %collective-permute-start.27 = (f32[4,16]{1,0:T(4,128)S(1)}, f32[4,16]{1,0:T(4,128)S(1)}, u32[]{:S(2)}, u32[]{:S(2)}) collective-permute-start(f32[4,16]{1,0:T(4,128)S(1)} %maximum_select_fusion), channel_id=1, source_target_pairs={{0,2},{1,3},{2,0},{3,1},{4,6},{5,7},{6,4},{7,5},{8,10},{9,11},{10,... | collective-permute-start | bytes 776 | tf_op jit(solution)/shard_map/ppermute | solution.py:317
  171.7 3.0 %collective-permute-start.28 = (f32[4,16]{1,0:T(4,128)S(1)}, f32[4,16]{1,0:T(4,128)S(1)}, u32[]{:S(2)}, u32[]{:S(2)}) collective-permute-start(f32[4,16]{1,0:T(4,128)S(1)} %maximum_select_fusion), channel_id=1, source_target_pairs={{0,3},{1,2},{2,1},{3,0},{4,7},{5,6},{6,5},{7,4},{8,11},{9,10},{10,... | collective-permute-start | bytes 776 | tf_op jit(solution)/shard_map/ppermute | solution.py:317
  174.7 4.4 %collective-permute-start.29 = (f32[4,16]{1,0:T(4,128)S(1)}, f32[4,16]{1,0:T(4,128)S(1)}, u32[]{:S(2)}, u32[]{:S(2)}) collective-permute-start(f32[4,16]{1,0:T(4,128)S(1)} %add_add_fusion.2), channel_id=1, source_target_pairs={{0,4},{4,0},{8,12},{12,8},{1,5},{5,1},{9,13},{13,9},{2,6},{6,2},{1... | collective-permute-start | bytes 776 | tf_op jit(solution)/shard_map/ppermute | solution.py:317
  174.7 4.5 %collective-permute-start.30 = (f32[4,16]{1,0:T(4,128)S(1)}, f32[4,16]{1,0:T(4,128)S(1)}, u32[]{:S(2)}, u32[]{:S(2)}) collective-permute-start(f32[4,16]{1,0:T(4,128)S(1)} %add_add_fusion.2), channel_id=1, source_target_pairs={{0,8},{4,12},{8,0},{12,4},{1,9},{5,13},{9,1},{13,5},{2,10},{6,14},... | collective-permute-start | bytes 776 | tf_op jit(solution)/shard_map/ppermute | solution.py:317
  176.6 5.4 %collective-permute-start.31 = (f32[4,16]{1,0:T(4,128)S(1)}, f32[4,16]{1,0:T(4,128)S(1)}, u32[]{:S(2)}, u32[]{:S(2)}) collective-permute-start(f32[4,16]{1,0:T(4,128)S(1)} %add_add_fusion.2), channel_id=1, source_target_pairs={{0,12},{4,8},{8,4},{12,0},{1,13},{5,9},{9,5},{13,1},{2,14},{6,10},... | collective-permute-start | bytes 776 | tf_op jit(solution)/shard_map/ppermute | solution.py:317

commit v3 on v2

v3 whole, which is shorter than its diff:
```python
import functools
import math

import jax
import jax.numpy as jnp
from jax import lax
from jax.experimental import pallas as pl
from jax.experimental.pallas import tpu as pltpu
from jax.sharding import PartitionSpec as P

D = 4096
FF = 11008
TC_DEV = 128
EX_DEV = 2
QLEN = 16
PAD = 1
MIB = 1024 * 1024
TILE = 256
WIDTHS = (1024, 1024)
F32 = jnp.float32
BF16 = jnp.bfloat16
VMEM = pl.BlockSpec(memory_space=pltpu.VMEM)
SMEM = pl.BlockSpec(memory_space=pltpu.SMEM)
ANY = pl.BlockSpec(memory_space=pl.ANY)
HBM = pl.BlockSpec(memory_space=pltpu.HBM)
ORDER = jax.ShapeDtypeStruct((8, 128), F32)
QUICK = pl.CostEstimate(flops=1024, bytes_accessed=1024, transcendentals=0)


def params(mib):
    return pltpu.CompilerParams(vmem_limit_bytes=mib * MIB)


def chunk_bounds(total):
    bounds = []
    start = 0
    for width in WIDTHS:
        if start + width < total:
            bounds.append((start, width))
            start += width
    bounds.append((start, total - start))
    return bounds


def total_of(values):
    return functools.reduce(lambda a, b: a + b, values)


def column_tiles(width):
    return [(start, min(TILE, width - start)) for start in range(0, width, TILE)]


def basis_copies(basis_hbm, basis_ref, sems, first):
    depth = basis_hbm.shape[0]
    upper = depth // 32 * 16
    copies = []
    for n, (start, size) in enumerate(column_tiles(basis_ref.shape[1])):
        copies.append(
            [
                pltpu.make_async_copy(
                    basis_hbm.at[top : top + rows, first + start : first + start + size],
                    basis_ref.at[top : top + rows, start : start + size],
                    sems.at[n, half],
                )
                for half, (top, rows) in enumerate(((0, upper), (upper, depth - upper)))
            ]
        )
    return copies


def project_kernel(terms, far, first, order_ref, *refs):
    del order_ref
    arrays = refs[: 2 * terms] if terms else ()
    if terms:
        basis_hbm, wide_ref, send_ref, rows_ref, done_ref = refs[2 * terms : 2 * terms + 5]
        scratch = refs[2 * terms + 5 :]
    else:
        rows_ref, basis_hbm, wide_ref, send_ref, done_ref = refs[:5]
        scratch = refs[5:]
    basis_ref, sems = scratch[:2]
    copies = basis_copies(basis_hbm, basis_ref, sems, first)
    if far:
        taken, row_sems = scratch[2:]
        row_copies = [
            pltpu.make_async_copy(a, taken.at[n], row_sems.at[n]) for n, a in enumerate(arrays)
        ]
        for copy in row_copies:
            copy.start()
    for pair in copies:
        for copy in pair:
            copy.start()
    if terms:
        split = arrays[0].shape[1]
        for n in range(2):
            if far:
                row_copies[n].wait()
                rows_ref[n * split : (n + 1) * split] = taken[n].T
            else:
                part = total_of([r[...] for r in arrays[n * terms : (n + 1) * terms]])
                rows_ref[n * split : (n + 1) * split] = part.T
    for pair, (start, size) in zip(copies, column_tiles(basis_ref.shape[1])):
        for copy in pair:
            copy.wait()
        product = jnp.dot(
            rows_ref[...], basis_ref[:, start : start + size], preferred_element_type=F32
        )
        wide_ref[:, start : start + size] = product
        send_ref[:, start : start + size] = product.astype(send_ref.dtype)
    done_ref[...] = jnp.zeros_like(done_ref)


def project(order, inputs, basis, start, width, far=False):
    depth = basis.shape[0]
    tiles = len(column_tiles(width))
    scratch = [pltpu.VMEM((depth, width), basis.dtype), pltpu.SemaphoreType.DMA((tiles, 2))]
    if isinstance(inputs, tuple):
        terms = len(inputs[0])
        arrays = list(inputs[0]) + list(inputs[1])
        rows = 2 * arrays[0].shape[1]
        specs = [HBM if far else VMEM] * (2 * terms)
        if far:
            scratch += [
                pltpu.VMEM((2,) + arrays[0].shape, BF16),
                pltpu.SemaphoreType.DMA((2,)),
            ]
    else:
        terms = 0
        arrays = [inputs]
        rows = inputs.shape[0]
        specs = [VMEM]
    out_shape = [
        jax.ShapeDtypeStruct((rows, width), F32),
        jax.ShapeDtypeStruct((rows, width), BF16),
    ]
    if terms:
        out_shape.append(jax.ShapeDtypeStruct((rows, depth), BF16))
    out = pl.pallas_call(
        functools.partial(project_kernel, terms, far, start),
        in_specs=[ANY] + specs + [HBM],
        out_specs=[VMEM] * (len(out_shape) + 1),
        out_shape=out_shape + [ORDER],
        scratch_shapes=scratch,
        compiler_params=params(59 if far else 48),
        cost_estimate=QUICK,
        name="project",
    )(order, *arrays, basis)
    if terms:
        return out
    return out[0], out[1], inputs, out[2]


def act_kernel(order_ref, cand_ref, query_ref, basis_hbm, share_ref, done_ref, basis_ref, sems):
    del order_ref
    copies = basis_copies(basis_hbm, basis_ref, sems, 0)
    for pair in copies:
        for copy in pair:
            copy.start()
    rows = jnp.concatenate([cand_ref[...], query_ref[...]], 0)
    for pair, (start, size) in zip(copies, column_tiles(basis_ref.shape[1])):
        for copy in pair:
            copy.wait()
        share_ref[:, start : start + size] = jnp.dot(
            rows, basis_ref[:, start : start + size], preferred_element_type=F32
        )
    done_ref[...] = jnp.zeros_like(done_ref)


def act_shares(order, cand_act, query_act, basis):
    rows = cand_act.shape[0] + query_act.shape[0]
    return pl.pallas_call(
        act_kernel,
        in_specs=[ANY, VMEM, VMEM, HBM],
        out_specs=[VMEM, VMEM],
        out_shape=[jax.ShapeDtypeStruct((rows, basis.shape[1]), F32), ORDER],
        scratch_shapes=[
            pltpu.VMEM(basis.shape, basis.dtype),
            pltpu.SemaphoreType.DMA((len(column_tiles(basis.shape[1])), 2)),
        ],
        compiler_params=params(24),
        cost_estimate=QUICK,
        name="acts",
    )(order, cand_act, query_act, basis)


def is_inner():
    spot = lax.axis_index("hid")
    return (spot != 0) & (spot != lax.axis_size("hid") - 1)


def add_kernel(count, order_ref, *refs):
    del order_ref
    sum_ref, done_ref = refs[-2:]
    sum_ref[...] = total_of([r[...].astype(F32) for r in refs[:count]]).astype(sum_ref.dtype)
    done_ref[...] = jnp.zeros_like(done_ref)


def add(order, arrays, after=()):
    return pl.pallas_call(
        functools.partial(add_kernel, len(arrays)),
        in_specs=[ANY] + [VMEM] * len(arrays) + [ANY] * len(after),
        out_specs=[VMEM, VMEM],
        out_shape=[jax.ShapeDtypeStruct(arrays[0].shape, BF16), ORDER],
        compiler_params=params(16),
        cost_estimate=QUICK,
        name="add",
    )(order, *arrays, *after)


def exchange_kernel(order_ref, wide_ref, in_ref, across_ref, next_ref, sum_ref, send_ref, done_ref):
    del order_ref

    @pl.when(is_inner())
    def _():
        total = wide_ref[...] + in_ref[...].astype(F32) + across_ref[...].astype(F32)
        sum_ref[...] = total.astype(BF16)
        send_ref[...] = total.astype(BF16)

    @pl.when(jnp.logical_not(is_inner()))
    def _():
        sum_ref[...] = jnp.zeros_like(sum_ref)
        send_ref[...] = next_ref[...]

    done_ref[...] = jnp.zeros_like(done_ref)


def exchange(order, wide, came_in, across, following):
    shape = jax.ShapeDtypeStruct(wide.shape, BF16)
    return pl.pallas_call(
        exchange_kernel,
        in_specs=[ANY] + [VMEM] * 4,
        out_specs=[VMEM] * 3,
        out_shape=[shape, shape, ORDER],
        compiler_params=params(16),
        cost_estimate=QUICK,
        name="exchange",
    )(order, wide, came_in, across, following)


def masked_kernel(order_ref, share_ref, came_ref, cand_ids_ref, query_ids_ref, acts_ref, done_ref):
    del order_ref
    rows = cand_ids_ref.shape[1]
    for n, ids_ref in enumerate((cand_ids_ref, query_ids_ref)):
        span = slice(n * rows, (n + 1) * rows)
        keep = jnp.where(ids_ref[...] != PAD, 1.0, 0.0).astype(F32)
        keep = jnp.broadcast_to(keep, (rows, rows)).T[:, :1]
        acts_ref[span, :] = ((share_ref[span, :] + came_ref[span, :]) * keep).astype(BF16)
    done_ref[...] = jnp.zeros_like(done_ref)


def masked_acts(order, share, came, cand_ids, query_ids):
    return pl.pallas_call(
        masked_kernel,
        in_specs=[ANY] + [VMEM] * 4,
        out_specs=[VMEM, VMEM],
        out_shape=[jax.ShapeDtypeStruct(share.shape, BF16), ORDER],
        compiler_params=params(16),
        cost_estimate=QUICK,
        name="masked_acts",
    )(order, share, came, cand_ids[None, :], query_ids[None, :])


def split_kernel(examples, order_ref, offsets_ref, own, over, split_ref, query_ref, done_ref):
    del order_ref
    rows, features = own.shape[0] // 2, own.shape[1]
    ex = lax.axis_index("ex")
    spot = lax.broadcasted_iota(jnp.int32, (rows, 1), 0)
    for place, acts in enumerate((own, over)):
        span = slice(place * rows, (place + 1) * rows)
        first = (ex if place == 0 else 1 - ex) * rows
        cand = acts[:rows, :]
        query_ref[span, :] = acts[rows:, :]
        for k in range(examples):
            member = spot + first >= offsets_ref[k]
            if k + 1 < examples:
                member = member & (spot + first < offsets_ref[k + 1])
            member = jnp.where(member, 1.0, 0.0).astype(BF16)
            split_ref[span, k * features : (k + 1) * features] = cand * member
    done_ref[...] = jnp.zeros_like(done_ref)


def split_acts(order, offsets, own, over):
    rows, features = own.shape
    examples = offsets.shape[0]
    return pl.pallas_call(
        functools.partial(split_kernel, examples),
        in_specs=[ANY, SMEM, VMEM, VMEM],
        out_specs=[VMEM] * 3,
        out_shape=[
            jax.ShapeDtypeStruct((rows, examples * features), BF16),
            jax.ShapeDtypeStruct((rows, features), BF16),
            ORDER,
        ],
        compiler_params=params(16),
        cost_estimate=QUICK,
        name="split_acts",
    )(order, offsets, own, over)


def row_tiles(width):
    return [(start, min(512, width - start)) for start in range(0, width, 512)]


def score_kernel(blocks, pick, cand_rows, examples, first, order_ref, *refs):
    del order_ref
    per_block = 2 if pick else 1
    parts = refs[: blocks * per_block]
    eig_hbm, split_ref, query_act_ref, out_ref, done_ref, eig_ref, sems = refs[blocks * per_block :]
    width = parts[0].shape[1]
    base = lax.axis_index("sub") * (eig_hbm.shape[0] // lax.axis_size("sub")) + first
    copies = []
    for n, (start, size) in enumerate(row_tiles(width)):
        pieces = []
        for m, top in enumerate(range(0, size, 128)):
            rows = min(128, size - top)
            pieces.append(
                pltpu.make_async_copy(
                    eig_hbm.at[pl.ds(pl.multiple_of(base + start + top, 8), rows), :],
                    eig_ref.at[pl.ds(start + top, rows), :],
                    sems.at[n, m],
                )
            )
        copies.append(pieces)
    for pieces in copies:
        for copy in pieces:
            copy.start()
    sums = []
    for b in range(blocks):
        here = parts[b * per_block]
        if pick:
            sums.append(jnp.where(is_inner(), here[...], parts[b * per_block + 1][...]))
        else:
            sums.append(here[...])
    features = eig_ref.shape[1]
    cand = jnp.concatenate([s[:cand_rows] for s in sums], 0)
    query = jnp.concatenate([s[cand_rows:] for s in sums], 0)
    scores = [0.0] * examples
    for pieces, (start, size) in zip(copies, row_tiles(width)):
        cand_tile = cand[:, start : start + size].T
        query_tile = query[:, start : start + size].T.astype(F32)
        for copy in pieces:
            copy.wait()
        inverse = 1.0 / eig_ref[start : start + size, :]
        for k in range(examples):
            outer = jnp.dot(
                cand_tile,
                split_ref[:, k * features : (k + 1) * features],
                preferred_element_type=F32,
            )
            weights = (outer * inverse).astype(BF16)
            image = lax.dot_general(
                weights,
                query_act_ref[...],
                (((1,), (1,)), ((), ())),
                preferred_element_type=F32,
            )
            scores[k] = scores[k] + jnp.sum(image * query_tile, axis=0, keepdims=True)
    for k in range(examples):
        out_ref[k : k + 1, :] = scores[k]
    done_ref[...] = jnp.zeros_like(done_ref)


def score_chunk(order, blocks, pick, cand_rows, eigvals, first, split, query_acts, examples):
    parts = [a for block in blocks for a in block]
    width = parts[0].shape[1]
    features = eigvals.shape[1]
    return pl.pallas_call(
        functools.partial(score_kernel, len(blocks), pick, cand_rows, examples, first),
        in_specs=[ANY] + [VMEM] * len(parts) + [HBM, VMEM, VMEM],
        out_specs=[VMEM, VMEM],
        out_shape=[jax.ShapeDtypeStruct((examples, query_acts.shape[0]), F32), ORDER],
        scratch_shapes=[
            pltpu.VMEM((width, features), F32),
            pltpu.SemaphoreType.DMA((len(row_tiles(width)), 4)),
        ],
        compiler_params=params(42),
        cost_estimate=QUICK,
        name="score",
    )(order, *parts, eigvals, split, query_acts)


def small_sum(value, axes):
    size = lax.axis_size(axes)
    if size > 4:
        return lax.psum(value, axes)
    terms = [value]
    for other in range(1, size):
        terms.append(lax.ppermute(value, axes, [(i, i ^ other) for i in range(size)]))
    while len(terms) > 1:
        terms = [a + b for a, b in zip(terms[::2], terms[1::2])]
    return terms[0]


STEPS = (
    "P0 P1 A1 S0 P2 S1 P3 E0 P4 S2 E1 HF P5 S3 E2 S4 F3 SP S5 F4 Z0 F5 Z1 Z2"
)


def token_scores_paired(
    cand_grad, query_grad, cand_act, query_act, cand_ids, query_ids, cand_offsets, basis_g, basis_a, eigvals
):
    rows = cand_grad.shape[0]
    examples = cand_offsets.shape[0]
    bounds = chunk_bounds(basis_g.shape[1])
    count = len(bounds)
    swap = lambda a, axis: lax.ppermute(a, axis, [(0, 1), (1, 0)])
    inward = lambda a: lax.ppermute(a, "hid", [(0, 1), (3, 2)])
    across = lambda a: lax.ppermute(a, "hid", [(1, 2), (2, 1)])
    outward = lambda a: lax.ppermute(a, "hid", [(1, 0), (2, 3)])
    beside = lambda a: lax.ppermute(a, "hid", [(0, 1), (1, 0), (2, 3), (3, 2)])

    tokens = [
        ([cand_grad.T], [query_grad.T]),
        ([swap(cand_grad, "ex").T], [swap(query_grad, "ex").T]),
    ]
    order = jnp.zeros((8, 128), F32)
    wide, sends, ins, crossed, summed, outs = {}, {}, {}, {}, {}, {}
    scores = []
    share = came = acts = acts_over = split = query_acts = None
    for step in STEPS.split():
        kind, c = step[0], int(step[1]) if step[1].isdigit() else None
        if kind == "P":
            block, q = divmod(c, count)
            wide[c], sends[c], tokens[block], order = project(
                order, tokens[block], basis_g, *bounds[q], far=c == 0
            )
            if block == 0:
                ins[c] = inward(sends[c])
        elif step == "A1":
            share, order = act_shares(order, cand_act, query_act, basis_a)
            came = swap(share, "sub")
        elif step == "HF":
            acts, order = masked_acts(order, share, came, cand_ids, query_ids)
            acts_over = swap(acts, "ex")
        elif step == "SP":
            split, query_acts, order = split_acts(order, cand_offsets, acts, acts_over)
        elif kind == "S":
            send, order = add(order, [wide[c], ins[c]])
            crossed[c] = across(send)
        elif kind == "E":
            summed[c], send, order = exchange(
                order, wide[c], ins[c], crossed[c], sends[c + count]
            )
            ins[c + count] = outs[c] = beside(send)
        elif kind == "F":
            summed[c], order = add(order, [wide[c], ins[c], crossed[c]])
            outs[c] = outward(summed[c])
        elif kind == "Z":
            out, order = score_chunk(
                order,
                [(summed[n], outs[n]) for n in (c, count + c)],
                True,
                rows,
                eigvals,
                bounds[c][0],
                split,
                query_acts,
                examples,
            )
            scores.append(out)
    return total_of(scores)


def token_scores_gathered(
    cand_grad, query_grad, cand_act, query_act, cand_ids, query_ids, cand_offsets, basis_g, basis_a, eigvals
):
    gather = lambda a: lax.all_gather(a, "ex", axis=0, tiled=True)
    examples = cand_offsets.shape[0]
    features = basis_a.shape[1]
    order = jnp.zeros((8, 128), F32)
    keep = lambda ids: (ids != PAD).astype(BF16)[:, None]
    share = lambda a: lax.psum(jnp.dot(a, basis_a, preferred_element_type=F32), "sub")
    cands = gather(share(cand_act).astype(BF16) * keep(cand_ids))
    query_acts = gather(share(query_act).astype(BF16) * keep(query_ids))
    cand_rows = cands.shape[0]
    positions = jnp.arange(cand_rows, dtype=jnp.int32)
    example_ends = jnp.concatenate([cand_offsets[1:], jnp.full((1,), cand_rows, jnp.int32)])
    member = (positions[:, None] >= cand_offsets[None, :]) & (
        positions[:, None] < example_ends[None, :]
    )
    split = (member.astype(BF16)[:, :, None] * cands[:, None, :]).reshape(
        cand_rows, examples * features
    )
    tokens = jnp.concatenate([gather(cand_grad), gather(query_grad)], 0)
    scores = []
    for start, width in chunk_bounds(basis_g.shape[1]):
        wide, _, tokens, order = project(order, tokens, basis_g, start, width)
        total = lax.psum(wide, "hid").astype(BF16)
        out, order = score_chunk(
            order, [(total,)], False, cand_rows, eigvals, start, split, query_acts, examples
        )
        scores.append(out)
    return total_of(scores)


def per_device(
    cand_grad,
    query_grad,
    cand_act,
    query_act,
    cand_ids,
    query_ids,
    cand_offsets,
    basis_g,
    basis_a,
    eigvals,
):
    groups = lax.axis_size("ex")
    halves = lax.axis_size("sub")
    ex = lax.axis_index("ex")
    sub = lax.axis_index("sub")
    examples = cand_offsets.shape[0]
    paired = (
        groups == 2
        and halves == 2
        and lax.axis_size("hid") == 4
        and cand_grad.shape[0] == query_grad.shape[0]
    )
    arrays = (
        cand_grad, query_grad, cand_act, query_act, cand_ids, query_ids, cand_offsets, basis_g, basis_a, eigvals
    )
    token_scores = token_scores_paired(*arrays) if paired else token_scores_gathered(*arrays)
    queries = groups * query_grad.shape[0] // QLEN
    partial_value = token_scores.reshape(examples, queries, QLEN).sum(2)
    if paired:
        turned = jnp.roll(partial_value, queries // 2, axis=1)
        partial_value = jnp.where(ex == 0, partial_value, turned)
    total = small_sum(small_sum(partial_value, ("ex", "sub")), "hid")
    mine = lax.dynamic_slice_in_dim(total, sub * (queries // halves), queries // halves, 1)
    factor = 1.0 / math.sqrt(FF * D * QLEN * (TC_DEV // EX_DEV))
    return mine * factor


def solution(mesh):
    return jax.shard_map(
        per_device,
        mesh=mesh,
        in_specs=(
            P(("grp", "ex"), "hid"),
            P(("grp", "ex"), "hid"),
            P(("grp", "ex"), "sub"),
            P(("grp", "ex"), "sub"),
            P(("grp", "ex")),
            P(("grp", "ex")),
            P("grp"),
            P("hid", ("ex", "sub")),
            P("sub", "hid"),
            P("ex", "hid"),
        ),
        out_specs=P("grp", "sub"),
        check_vma=False,
    )
```

time: 184 us -> 139 us (0.76)
  waiting for transfers between devices: 58 us -> 34.6 us
  starting transfers between devices: 60.3 us -> 37.6 us
    ppermute x6 -> x3, waiting for transfers between devices: 36.3 us -> 11.5 us  [token_scores_paired(): outward = lambda a: lax.ppermute(a, 'hid', [(1, 0), (2, 3)])]
    ppermute x6 -> x3, starting transfers between devices: 30.5 us -> 13.6 us  [token_scores_paired(): inward = lambda a: lax.ppermute(a, 'hid', [(0, 1), (3, 2)])]
    ppermute x6 -> x3, waiting for transfers between devices: 10.5 us -> 3.64 us  [token_scores_paired(): inward = lambda a: lax.ppermute(a, 'hid', [(0, 1), (3, 2)])]
    ppermute x4 -> x3, waiting for transfers between devices: 4.15 us -> 10.9 us  [token_scores_paired(): beside = lambda a: lax.ppermute(a, 'hid', [(0, 1), (1, 0), (2, 3), (3, 2)])]
    ppermute x6 -> x3, starting transfers between devices: 7.91 us -> 4.07 us  [token_scores_paired(): outward = lambda a: lax.ppermute(a, 'hid', [(1, 0), (2, 3)])]
    ppermute x4 -> x3, starting transfers between devices: 8.16 us -> 5.84 us  [token_scores_paired(): beside = lambda a: lax.ppermute(a, 'hid', [(0, 1), (1, 0), (2, 3), (3, 2)])]
    unnamed x22 -> x30, local copies, waits for them, and re-layouts: 3.59 us -> 3.93 us
  transfers between devices with their start and end apart: 32 -> 25, of which waited for: 16 -> 11; matrix products, arithmetic and copies ran while one was open for 0% -> 0% of each run, Pallas kernels for 29% -> 32%
where the time goes in v3:
time: 139 us
  Pallas kernels  60.5 us (44%)
  starting transfers between devices  37.6 us (27%)
  waiting for transfers between devices  34.6 us (25%)
  local copies, waits for them, and re-layouts  4.67 us (3%)
    pallas_call x6, Pallas kernels, project(): pl.pallas_call(functools.partial(project_kernel, terms, far, start), in_s...  31.3 us
    pallas_call x3, Pallas kernels, score_chunk(): pl.pallas_call(functools.partial(score_kernel, len(blocks), pick, cand_ro...  21.8 us
    ppermute x3, starting transfers between devices, token_scores_paired(): inward = lambda a: lax.ppermute(a, 'hid', [(0, 1), (3, 2)])  13.6 us
    ppermute x3, waiting for transfers between devices, token_scores_paired(): outward = lambda a: lax.ppermute(a, 'hid', [(1, 0), (2, 3)])  11.5 us
    ppermute x3, waiting for transfers between devices, token_scores_paired(): beside = lambda a: lax.ppermute(a, 'hid', [(0, 1), (1, 0), (2, 3), (3, 2)])  10.9 us
    ppermute x6, waiting for transfers between devices, small_sum(): lax.ppermute(value, axes, [(i, i ^ other) for i in range(size)])  6.75 us
    ppermute x6, starting transfers between devices, small_sum(): lax.ppermute(value, axes, [(i, i ^ other) for i in range(size)])  6.25 us
    ppermute x3, starting transfers between devices, token_scores_paired(): beside = lambda a: lax.ppermute(a, 'hid', [(0, 1), (1, 0), (2, 3), (3, 2)])  5.84 us
  transfers between devices with their start and end apart: 25, of which 11 were waited for; matrix products, arithmetic and copies ran while one was open for 0% of the time, Pallas kernels for 32%

profile of v3, /device:TPU:0, one launch (start us, length us, event | category | flops | bytes accessed | tf_op | source)
XLA Modules:
  0.0 138.8 jit_solution(464211957547840146)
XLA Ops:
  0.0 0.6 broadcast_in_dim.9.order_ref
  0.6 8.5 %project.6 = (f32[256,1024]{1,0:T(8,128)}, bf16[256,1024]{1,0:T(8,128)(2,1)}, bf16[256,2752]{1,0:T(8,128)(2,1)}, f32[8,128]{1,0:T(8,128)}) custom-call(f32[8,128]{1,0:T(8,128)} %broadcast_in_dim.9.order_ref, bf16[2752,128]{1,0:T(8,128)(2,1)} %bitcast.10, bf16[2752,128]{1,0:T(8,128)(2,1)} %bitcast.11, bf16[2752,2752]{1,0:T(8,128)(2,1)} %refs_1_.7), custom_call_target="tpu_custom_call" | custom-call | flops 1024 | bytes 1024 | tf_op jit(solution)/shard_map/project/pallas_call | solution.py:137
  9.1 5.0 %collective-permute-start = (bf16[256,1024]{1,0:T(8,128)(2,1)}, bf16[256,1024]{1,0:T(8,128)(2,1)S(1)}, u32[]{:S(2)}, u32[]{:S(2)}) collective-permute-start(bf16[256,1024]{1,0:T(8,128)(2,1)} %get-tuple-element.69), channel_id=1, source_target_pairs={{0,4},{12,8},{1,5},{13,9},{2,6},{14,10},{3,7},{15,11},{16,20},{28,... | collective-permute-start | bytes 1572872 | tf_op jit(solution)/shard_map/ppermute | solution.py:406
  14.1 1.6 %collective-permute-start.2 = (bf16[128,2752]{0,1:T(8,128)(2,1)S(1)}, bf16[128,2752]{0,1:T(8,128)(2,1)S(1)}, u32[]{:S(2)}, u32[]{:S(2)}) collective-permute-start(bf16[128,2752]{0,1:T(8,128)(2,1)S(1)} %copy-done.13), channel_id=1, source_target_pairs={{0,2},{2,0},{1,3},{3,1},{4,6},{6,4},{5,7},{7,5},{8,10},{10,8},{9,1... | collective-permute-start | bytes 2113544 | tf_op jit(solution)/shard_map/ppermute | solution.py:405
  16.2 1.4 copy-done
  17.5 0.7 copy-done.9
  18.2 5.1 %project.7 = (f32[256,1024]{1,0:T(8,128)S(1)}, bf16[256,1024]{1,0:T(8,128)(2,1)S(1)}, f32[8,128]{1,0:T(8,128)S(1)}) custom-call(f32[8,128]{1,0:T(8,128)S(1)} %copy-done.9, bf16[256,2752]{1,0:T(8,128)(2,1)S(1)} %copy-done, bf16[2752,2752]{1,0:T(8,128)(2,1)} %refs_1_.7), custom_call_target="tpu_custom_call" | custom-call | flops 1024 | bytes 1024 | tf_op jit(solution)/shard_map/project/pallas_call | solution.py:137
  23.4 1.5 %collective-permute-start.1 = (bf16[256,1024]{1,0:T(8,128)(2,1)S(1)}, bf16[256,1024]{1,0:T(8,128)(2,1)S(1)}, u32[]{:S(2)}, u32[]{:S(2)}) collective-permute-start(bf16[256,1024]{1,0:T(8,128)(2,1)S(1)} %get-tuple-element.73), channel_id=1, source_target_pairs={{0,4},{12,8},{1,5},{13,9},{2,6},{14,10},{3,7},{15,11},{16,20},{28,... | collective-permute-start | bytes 1572872 | tf_op jit(solution)/shard_map/ppermute | solution.py:406
  24.8 3.5 %acts.1 = (f32[256,1024]{1,0:T(8,128)S(1)}, f32[8,128]{1,0:T(8,128)S(1)}) custom-call(f32[8,128]{1,0:T(8,128)S(1)} %get-tuple-element.66.order_ref, bf16[128,2048]{1,0:T(8,128)(2,1)S(1)} %copy-done.3, bf16[128,2048]{1,0:T(8,128)(2,1)S(1)} %copy-done.4, bf16[2048,1024]{1,0:T(8,128)(2,1)S(1)} %copy-done.2), custom_call_target="tpu_custom_call" | custom-call | flops 1024 | bytes 1024 | tf_op jit(solution)/shard_map/acts/pallas_call | solution.py:170
  28.6 0.7 collective-permute-start.4
  29.3 3.7 %project.8 = (f32[256,704]{1,0:T(8,128)S(1)}, bf16[256,704]{1,0:T(8,128)(2,1)S(1)}, f32[8,128]{1,0:T(8,128)S(1)}) custom-call(f32[8,128]{1,0:T(8,128)S(1)} %get-tuple-element.70.order_ref, bf16[256,2752]{1,0:T(8,128)(2,1)S(1)} %copy-done, bf16[2752,2752]{1,0:T(8,128)(2,1)} %refs_1_.7), custom_call_target="tpu_custom_call" | custom-call | flops 1024 | bytes 1024 | tf_op jit(solution)/shard_map/project/pallas_call | solution.py:137
  33.0 3.6 %collective-permute-done.1.refs_1_.in_ref = bf16[256,1024]{1,0:T(8,128)(2,1)S(1)} collective-permute-done((bf16[256,1024]{1,0:T(8,128)(2,1)S(1)}, bf16[256,1024]{1,0:T(8,128)(2,1)S(1)}, u32[]{:S(2)}, u32[]{:S(2)}) %collective-permute-start.1) | collective-permute-done | bytes 524320 | tf_op jit(solution)/shard_map/ppermute | solution.py:406
  36.7 0.7 collective-permute-start.6
  37.5 7.2 %collective-permute-start.5 = (bf16[256,704]{1,0:T(8,128)(2,1)S(1)}, bf16[256,704]{1,0:T(8,128)(2,1)S(1)}, u32[]{:S(2)}, u32[]{:S(2)}) collective-permute-start(bf16[256,704]{1,0:T(8,128)(2,1)S(1)} %get-tuple-element.82), channel_id=1, source_target_pairs={{0,4},{12,8},{1,5},{13,9},{2,6},{14,10},{3,7},{15,11},{16,20},{28,... | collective-permute-start | bytes 1081352 | tf_op jit(solution)/shard_map/ppermute | solution.py:406
  44.7 1.8 %collective-permute-done.3 = bf16[128,2752]{0,1:T(8,128)(2,1)S(1)} collective-permute-done((bf16[128,2752]{0,1:T(8,128)(2,1)S(1)}, bf16[128,2752]{0,1:T(8,128)(2,1)S(1)}, u32[]{:S(2)}, u32[]{:S(2)}) %collective-permute-start.3) | collective-permute-done | bytes 704544 | tf_op jit(solution)/shard_map/ppermute | solution.py:405
  46.5 5.2 %project.9 = (f32[256,1024]{1,0:T(8,128)S(1)}, bf16[256,1024]{1,0:T(8,128)(2,1)S(1)}, bf16[256,2752]{1,0:T(8,128)(2,1)S(1)}, f32[8,128]{1,0:T(8,128)S(1)}) custom-call(f32[8,128]{1,0:T(8,128)S(1)} %get-tuple-element.74.order_ref, bf16[2752,128]{1,0:T(8,128)(2,1)S(1)} %bitcast.6, bf16[2752,128]{1,0:T(8,128)(2,1)S(1)} %bitcast.7, bf16[2752,2752]{1,0:T(8,128)(2,1)} %refs_1_.7), custom_call_target="tpu_custom_call" | custom-call | flops 1024 | bytes 1024 | tf_op jit(solution)/shard_map/project/pallas_call | solution.py:137
  52.0 5.0 %project.10 = (f32[256,1024]{1,0:T(8,128)S(1)}, bf16[256,1024]{1,0:T(8,128)(2,1)S(1)}, f32[8,128]{1,0:T(8,128)S(1)}) custom-call(f32[8,128]{1,0:T(8,128)S(1)} %get-tuple-element.78.order_ref, bf16[256,2752]{1,0:T(8,128)(2,1)S(1)} %get-tuple-element.79.refs_0_, bf16[2752,2752]{1,0:T(8,128)(2,1)} %refs_1_.7), custom_call_target="tpu_custom_call" | custom-call | flops 1024 | bytes 1024 | tf_op jit(solution)/shard_map/project/pallas_call | solution.py:137
  57.3 0.8 copy-done.5
  58.1 2.1 %collective-permute-start.10 = (bf16[256,1024]{1,0:T(8,128)(2,1)S(1)}, bf16[256,1024]{1,0:T(8,128)(2,1)S(1)}, u32[]{:S(2)}, u32[]{:S(2)}) collective-permute-start(bf16[256,1024]{1,0:T(8,128)(2,1)S(1)} %get-tuple-element.97), channel_id=1, source_target_pairs={{0,4},{4,0},{8,12},{12,8},{1,5},{5,1},{9,13},{13,9},{2,6},{6,2},{1... | collective-permute-start | bytes 1572872 | tf_op jit(solution)/shard_map/ppermute | solution.py:409
  60.2 0.7 collective-permute-start.9
  61.2 3.7 %project.11 = (f32[256,704]{1,0:T(8,128)S(1)}, bf16[256,704]{1,0:T(8,128)(2,1)S(1)}, f32[8,128]{1,0:T(8,128)S(1)}) custom-call(f32[8,128]{1,0:T(8,128)S(1)} %get-tuple-element.88.order_ref, bf16[256,2752]{1,0:T(8,128)(2,1)S(1)} %get-tuple-element.79.refs_0_, bf16[2752,2752]{1,0:T(8,128)(2,1)} %refs_1_.7), custom_call_target="tpu_custom_call" | custom-call | flops 1024 | bytes 1024 | tf_op jit(solution)/shard_map/project/pallas_call | solution.py:137
  64.9 2.0 %collective-permute-done.8.refs_1_ = bf16[256,1024]{1,0:T(8,128)(2,1)S(1)} collective-permute-done((bf16[256,1024]{1,0:T(8,128)(2,1)S(1)}, bf16[256,1024]{1,0:T(8,128)(2,1)S(1)}, u32[]{:S(2)}, u32[]{:S(2)}) %collective-permute-start.8) | collective-permute-done | bytes 524320 | tf_op jit(solution)/shard_map/ppermute | solution.py:409
  67.0 0.7 collective-permute-start.11
  67.7 1.6 %collective-permute-start.12 = (bf16[256,1024]{1,0:T(8,128)(2,1)S(1)}, bf16[256,1024]{1,0:T(8,128)(2,1)S(1)}, u32[]{:S(2)}, u32[]{:S(2)}) collective-permute-start(bf16[256,1024]{1,0:T(8,128)(2,1)S(1)} %get-tuple-element.101.own), channel_id=1, source_target_pairs={{0,2},{2,0},{1,3},{3,1},{4,6},{6,4},{5,7},{7,5},{8,10},{10,8},{9,1... | collective-permute-start | bytes 1572872 | tf_op jit(solution)/shard_map/ppermute | solution.py:405
  69.3 3.6 %collective-permute-start.13 = (bf16[256,704]{1,0:T(8,128)(2,1)S(1)}, bf16[256,704]{1,0:T(8,128)(2,1)S(1)}, u32[]{:S(2)}, u32[]{:S(2)}) collective-permute-start(bf16[256,704]{1,0:T(8,128)(2,1)S(1)} %get-tuple-element.104), channel_id=1, source_target_pairs={{0,4},{4,0},{8,12},{12,8},{1,5},{5,1},{9,13},{13,9},{2,6},{6,2},{1... | collective-permute-start | bytes 1081352 | tf_op jit(solution)/shard_map/ppermute | solution.py:409
  72.9 5.2 %collective-permute-done.10.refs_1_ = bf16[256,1024]{1,0:T(8,128)(2,1)S(1)} collective-permute-done((bf16[256,1024]{1,0:T(8,128)(2,1)S(1)}, bf16[256,1024]{1,0:T(8,128)(2,1)S(1)}, u32[]{:S(2)}, u32[]{:S(2)}) %collective-permute-start.10) | collective-permute-done | bytes 524320 | tf_op jit(solution)/shard_map/ppermute | solution.py:409
  78.2 0.7 collective-permute-start.14
  79.1 1.3 collective-permute-start.15
  80.4 0.8 split_acts.1
  81.2 3.8 %collective-permute-done.13.refs_1_ = bf16[256,704]{1,0:T(8,128)(2,1)S(1)} collective-permute-done((bf16[256,704]{1,0:T(8,128)(2,1)S(1)}, bf16[256,704]{1,0:T(8,128)(2,1)S(1)}, u32[]{:S(2)}, u32[]{:S(2)}) %collective-permute-start.13) | collective-permute-done | bytes 360480 | tf_op jit(solution)/shard_map/ppermute | solution.py:409
  85.0 0.7 collective-permute-start.16
  85.7 1.0 add.60
  86.7 1.3 collective-permute-start.17
  88.0 7.4 %collective-permute-done.15.refs_3_ = bf16[256,1024]{1,0:T(8,128)(2,1)S(1)} collective-permute-done((bf16[256,1024]{1,0:T(8,128)(2,1)S(1)}, bf16[256,1024]{1,0:T(8,128)(2,1)S(1)}, u32[]{:S(2)}, u32[]{:S(2)}) %collective-permute-start.15) | collective-permute-done | bytes 524320 | tf_op jit(solution)/shard_map/ppermute | solution.py:408
  95.4 6.5 %score.3 = (f32[4,256]{1,0:T(4,128)S(1)}, f32[8,128]{1,0:T(8,128)S(1)}) custom-call(f32[8,128]{1,0:T(8,128)S(1)} %get-tuple-element.107.order_ref, bf16[256,1024]{1,0:T(8,128)(2,1)S(1)} %get-tuple-element.108.refs_0_, bf16[256,1024]{1,0:T(8,128)(2,1)S(1)} %collective-permute-done.8.refs_1_, bf16[256,1024]{1,0:T(8,128)(2,1)S(1)} %get-tuple-element.109.refs_2_, ...), custom_call_target="tpu_custom_call" | custom-call | flops 1024 | bytes 1024 | tf_op jit(solution)/shard_map/score/pallas_call | solution.py:366
  101.9 0.9 add.61
  102.9 1.5 %collective-permute-start.18 = (bf16[256,704]{1,0:T(8,128)(2,1)}, bf16[256,704]{1,0:T(8,128)(2,1)}, u32[]{:S(2)}, u32[]{:S(2)}) collective-permute-start(bf16[256,704]{1,0:T(8,128)(2,1)} %get-tuple-element.121.refs_2_), channel_id=1, source_target_pairs={{4,0},{8,12},{5,1},{9,13},{6,2},{10,14},{7,3},{11,15},{20,16},{24,... | collective-permute-start | bytes 1081352 | tf_op jit(solution)/shard_map/ppermute | solution.py:408
  104.4 4.1 %collective-permute-done.17.refs_3_ = bf16[256,1024]{1,0:T(8,128)(2,1)} collective-permute-done((bf16[256,1024]{1,0:T(8,128)(2,1)}, bf16[256,1024]{1,0:T(8,128)(2,1)}, u32[]{:S(2)}, u32[]{:S(2)}) %collective-permute-start.17) | collective-permute-done | bytes 524320 | tf_op jit(solution)/shard_map/ppermute | solution.py:408
  108.5 1.0 copy-done.6
  109.5 7.9 %score.4 = (f32[4,256]{1,0:T(4,128)S(1)}, f32[8,128]{1,0:T(8,128)S(1)}) custom-call(f32[8,128]{1,0:T(8,128)S(1)} %get-tuple-element.115.order_ref, bf16[256,1024]{1,0:T(8,128)(2,1)S(1)} %copy-done.6, bf16[256,1024]{1,0:T(8,128)(2,1)S(1)} %collective-permute-done.10.refs_1_, bf16[256,1024]{1,0:T(8,128)(2,1)} %get-tuple-element.117.refs_2_, ...), custom_call_target="tpu_custom_call" | custom-call | flops 1024 | bytes 1024 | tf_op jit(solution)/shard_map/score/pallas_call | solution.py:366
  117.5 7.3 %score.5 = (f32[4,256]{1,0:T(4,128)S(1)}, f32[8,128]{1,0:T(8,128)}) custom-call(f32[8,128]{1,0:T(8,128)S(1)} %get-tuple-element.119.order_ref, bf16[256,704]{1,0:T(8,128)(2,1)S(1)} %copy-done.8, bf16[256,704]{1,0:T(8,128)(2,1)S(1)} %collective-permute-done.13.refs_1_, bf16[256,704]{1,0:T(8,128)(2,1)} %get-tuple-element.121.refs_2_, ...), custom_call_target="tpu_custom_call" | custom-call | flops 1024 | bytes 1024 | tf_op jit(solution)/shard_map/score/pallas_call | solution.py:366
  125.1 1.5 %collective-permute-start.20 = (f32[4,16]{1,0:T(4,128)S(1)}, f32[4,16]{1,0:T(4,128)S(1)}, u32[]{:S(2)}, u32[]{:S(2)}) collective-permute-start(f32[4,16]{1,0:T(4,128)S(1)} %maximum_select_fusion), channel_id=1, source_target_pairs={{0,2},{1,3},{2,0},{3,1},{4,6},{5,7},{6,4},{7,5},{8,10},{9,11},{10,... | collective-permute-start | bytes 776 | tf_op jit(solution)/shard_map/ppermute | solution.py:387
  127.0 1.8 %collective-permute-done.20 = f32[4,16]{1,0:T(4,128)S(1)} collective-permute-done((f32[4,16]{1,0:T(4,128)S(1)}, f32[4,16]{1,0:T(4,128)S(1)}, u32[]{:S(2)}, u32[]{:S(2)}) %collective-permute-start.20) | collective-permute-done | bytes 288 | tf_op jit(solution)/shard_map/ppermute | solution.py:387
  128.8 0.9 collective-permute-done.21
  129.7 3.1 %collective-permute-start.23 = (f32[4,16]{1,0:T(4,128)S(1)}, f32[4,16]{1,0:T(4,128)S(1)}, u32[]{:S(2)}, u32[]{:S(2)}) collective-permute-start(f32[4,16]{1,0:T(4,128)S(1)} %add_add_fusion.2), channel_id=1, source_target_pairs={{0,8},{4,12},{8,0},{12,4},{1,9},{5,13},{9,1},{13,5},{2,10},{6,14},... | collective-permute-start | bytes 776 | tf_op jit(solution)/shard_map/ppermute | solution.py:387
  132.7 1.3 collective-permute-start.24
  134.3 3.8 %collective-permute-done.24 = f32[4,16]{1,0:T(4,128)S(1)} collective-permute-done((f32[4,16]{1,0:T(4,128)S(1)}, f32[4,16]{1,0:T(4,128)S(1)}, u32[]{:S(2)}, u32[]{:S(2)}) %collective-permute-start.24) | collective-permute-done | bytes 288 | tf_op jit(solution)/shard_map/ppermute | solution.py:387
  138.1 0.7 dynamic-slice_multiply_fusion
  (65 shorter events, 3.0 us)
Async XLA Ops:
  0.6 13.5 %copy-start.13 = (bf16[128,2752]{0,1:T(8,128)(2,1)S(1)}, bf16[128,2752]{0,1:T(8,128)(2,1)}, u32[]{:S(2)}) copy-start(bf16[128,2752]{0,1:T(8,128)(2,1)} %param.10) | copy-start | bytes 2113540
  0.6 15.0 %copy-start.14 = (bf16[128,2752]{0,1:T(8,128)(2,1)S(1)}, bf16[128,2752]{0,1:T(8,128)(2,1)}, u32[]{:S(2)}) copy-start(bf16[128,2752]{0,1:T(8,128)(2,1)} %param.11) | copy-start | bytes 2113540
  9.1 19.3 %collective-permute-start = (bf16[256,1024]{1,0:T(8,128)(2,1)}, bf16[256,1024]{1,0:T(8,128)(2,1)S(1)}, u32[]{:S(2)}, u32[]{:S(2)}) collective-permute-start(bf16[256,1024]{1,0:T(8,128)(2,1)} %get-tuple-element.69), channel_id=1, source_target_pairs={{0,4},{12,8},{1,5},{13,9},{2,6},{14,10},{3,7},{15,11},{16,20},{28,... | collective-permute-start | bytes 1572872 | tf_op jit(solution)/shard_map/ppermute | solution.py:406
  14.1 23.4 %collective-permute-start.2 = (bf16[128,2752]{0,1:T(8,128)(2,1)S(1)}, bf16[128,2752]{0,1:T(8,128)(2,1)S(1)}, u32[]{:S(2)}, u32[]{:S(2)}) collective-permute-start(bf16[128,2752]{0,1:T(8,128)(2,1)S(1)} %copy-done.13), channel_id=1, source_target_pairs={{0,2},{2,0},{1,3},{3,1},{4,6},{6,4},{5,7},{7,5},{8,10},{10,8},{9,1... | collective-permute-start | bytes 2113544 | tf_op jit(solution)/shard_map/ppermute | solution.py:405
  15.6 30.8 %collective-permute-start.3 = (bf16[128,2752]{0,1:T(8,128)(2,1)S(1)}, bf16[128,2752]{0,1:T(8,128)(2,1)S(1)}, u32[]{:S(2)}, u32[]{:S(2)}) collective-permute-start(bf16[128,2752]{0,1:T(8,128)(2,1)S(1)} %copy-done.14), channel_id=1, source_target_pairs={{0,2},{2,0},{1,3},{3,1},{4,6},{6,4},{5,7},{7,5},{8,10},{10,8},{9,1... | collective-permute-start | bytes 2113544 | tf_op jit(solution)/shard_map/ppermute | solution.py:405
  16.2 1.4 copy-start
  17.5 0.7 copy-start.9
  18.2 6.6 %copy-start.2 = (bf16[2048,1024]{1,0:T(8,128)(2,1)S(1)}, bf16[2048,1024]{1,0:T(8,128)(2,1)}, u32[]{:S(2)}) copy-start(bf16[2048,1024]{1,0:T(8,128)(2,1)} %basis_hbm.1) | copy-start | bytes 12582916
  18.2 6.6 %copy-start.3 = (bf16[128,2048]{1,0:T(8,128)(2,1)S(1)}, bf16[128,2048]{1,0:T(8,128)(2,1)}, u32[]{:S(2)}) copy-start(bf16[128,2048]{1,0:T(8,128)(2,1)} %cand_ref.1) | copy-start | bytes 1572868
  18.2 6.6 %copy-start.4 = (bf16[128,2048]{1,0:T(8,128)(2,1)S(1)}, bf16[128,2048]{1,0:T(8,128)(2,1)}, u32[]{:S(2)}) copy-start(bf16[128,2048]{1,0:T(8,128)(2,1)} %query_ref.1) | copy-start | bytes 1572868
  23.3 5.1 %copy-start.1 = (f32[256,1024]{1,0:T(8,128)S(1)}, f32[256,1024]{1,0:T(8,128)}, u32[]{:S(2)}) copy-start(f32[256,1024]{1,0:T(8,128)} %get-tuple-element.68.refs_0_.wide_ref) | copy-start | bytes 3145732
  23.4 13.3 %collective-permute-start.1 = (bf16[256,1024]{1,0:T(8,128)(2,1)S(1)}, bf16[256,1024]{1,0:T(8,128)(2,1)S(1)}, u32[]{:S(2)}, u32[]{:S(2)}) collective-permute-start(bf16[256,1024]{1,0:T(8,128)(2,1)S(1)} %get-tuple-element.73), channel_id=1, source_target_pairs={{0,4},{12,8},{1,5},{13,9},{2,6},{14,10},{3,7},{15,11},{16,20},{28,... | collective-permute-start | bytes 1572872 | tf_op jit(solution)/shard_map/ppermute | solution.py:406
  28.3 32.6 %collective-permute-start.7 = (f32[256,1024]{1,0:T(8,128)S(1)}, f32[256,1024]{1,0:T(8,128)S(1)}, u32[]{:S(2)}, u32[]{:S(2)}) collective-permute-start(f32[256,1024]{1,0:T(8,128)S(1)} %get-tuple-element.87.share_ref), channel_id=1, source_target_pairs={{0,1},{1,0},{2,3},{3,2},{4,5},{5,4},{6,7},{7,6},{8,9},{9,8},{10,11... | collective-permute-start | bytes 3145736 | tf_op jit(solution)/shard_map/ppermute | solution.py:405
  28.6 23.1 %collective-permute-start.4 = (bf16[256,1024]{1,0:T(8,128)(2,1)S(1)}, bf16[256,1024]{1,0:T(8,128)(2,1)S(1)}, u32[]{:S(2)}, u32[]{:S(2)}) collective-permute-start(bf16[256,1024]{1,0:T(8,128)(2,1)S(1)} %get-tuple-element.76), channel_id=1, source_target_pairs={{4,8},{8,4},{5,9},{9,5},{6,10},{10,6},{7,11},{11,7},{20,24},{24,20... | collective-permute-start | bytes 1572872 | tf_op jit(solution)/shard_map/ppermute | solution.py:407
  36.7 20.4 %collective-permute-start.6 = (bf16[256,1024]{1,0:T(8,128)(2,1)S(1)}, bf16[256,1024]{1,0:T(8,128)(2,1)S(1)}, u32[]{:S(2)}, u32[]{:S(2)}) collective-permute-start(bf16[256,1024]{1,0:T(8,128)(2,1)S(1)} %get-tuple-element.84), channel_id=1, source_target_pairs={{4,8},{8,4},{5,9},{9,5},{6,10},{10,6},{7,11},{11,7},{20,24},{24,20... | collective-permute-start | bytes 1572872 | tf_op jit(solution)/shard_map/ppermute | solution.py:407
  37.5 19.6 %collective-permute-start.5 = (bf16[256,704]{1,0:T(8,128)(2,1)S(1)}, bf16[256,704]{1,0:T(8,128)(2,1)S(1)}, u32[]{:S(2)}, u32[]{:S(2)}) collective-permute-start(bf16[256,704]{1,0:T(8,128)(2,1)S(1)} %get-tuple-element.82), channel_id=1, source_target_pairs={{0,4},{12,8},{1,5},{13,9},{2,6},{14,10},{3,7},{15,11},{16,20},{28,... | collective-permute-start | bytes 1081352 | tf_op jit(solution)/shard_map/ppermute | solution.py:406
  51.9 14.9 %collective-permute-start.8 = (bf16[256,1024]{1,0:T(8,128)(2,1)S(1)}, bf16[256,1024]{1,0:T(8,128)(2,1)S(1)}, u32[]{:S(2)}, u32[]{:S(2)}) collective-permute-start(bf16[256,1024]{1,0:T(8,128)(2,1)S(1)} %get-tuple-element.91), channel_id=1, source_target_pairs={{0,4},{4,0},{8,12},{12,8},{1,5},{5,1},{9,13},{13,9},{2,6},{6,2},{1... | collective-permute-start | bytes 1572872 | tf_op jit(solution)/shard_map/ppermute | solution.py:409
  52.0 8.9 %copy-start.11 = (s32[128]{0:T(128)S(1)}, s32[128]{0:T(128)}, u32[]{:S(2)}) copy-start(s32[128]{0:T(128)} %param.14) | copy-start | bytes 1540
  52.0 8.9 %copy-start.12 = (s32[128]{0:T(128)S(1)}, s32[128]{0:T(128)}, u32[]{:S(2)}) copy-start(s32[128]{0:T(128)} %param.15) | copy-start | bytes 1540
  57.3 0.8 copy-start.5
  58.1 20.0 %collective-permute-start.10 = (bf16[256,1024]{1,0:T(8,128)(2,1)S(1)}, bf16[256,1024]{1,0:T(8,128)(2,1)S(1)}, u32[]{:S(2)}, u32[]{:S(2)}) collective-permute-start(bf16[256,1024]{1,0:T(8,128)(2,1)S(1)} %get-tuple-element.97), channel_id=1, source_target_pairs={{0,4},{4,0},{8,12},{12,8},{1,5},{5,1},{9,13},{13,9},{2,6},{6,2},{1... | collective-permute-start | bytes 1572872 | tf_op jit(solution)/shard_map/ppermute | solution.py:409
  60.2 9.0 %collective-permute-start.9 = (bf16[256,704]{1,0:T(8,128)(2,1)S(1)}, bf16[256,704]{1,0:T(8,128)(2,1)S(1)}, u32[]{:S(2)}, u32[]{:S(2)}) collective-permute-start(bf16[256,704]{1,0:T(8,128)(2,1)S(1)} %get-tuple-element.93), channel_id=1, source_target_pairs={{4,8},{8,4},{5,9},{9,5},{6,10},{10,6},{7,11},{11,7},{20,24},{24,20... | collective-permute-start | bytes 1081352 | tf_op jit(solution)/shard_map/ppermute | solution.py:407
  64.9 15.5 %copy-start.10 = (s32[4]{0:T(128)S(1)}, s32[4]{0:T(128)}, u32[]{:S(2)}) copy-start(s32[4]{0:T(128)} %offsets_ref.1) | copy-start | bytes 52
  67.0 11.9 %collective-permute-start.11 = (bf16[256,1024]{1,0:T(8,128)(2,1)S(1)}, bf16[256,1024]{1,0:T(8,128)(2,1)S(1)}, u32[]{:S(2)}, u32[]{:S(2)}) collective-permute-start(bf16[256,1024]{1,0:T(8,128)(2,1)S(1)} %get-tuple-element.99), channel_id=1, source_target_pairs={{4,8},{8,4},{5,9},{9,5},{6,10},{10,6},{7,11},{11,7},{20,24},{24,20... | collective-permute-start | bytes 1572872 | tf_op jit(solution)/shard_map/ppermute | solution.py:407
  67.7 12.7 %collective-permute-start.12 = (bf16[256,1024]{1,0:T(8,128)(2,1)S(1)}, bf16[256,1024]{1,0:T(8,128)(2,1)S(1)}, u32[]{:S(2)}, u32[]{:S(2)}) collective-permute-start(bf16[256,1024]{1,0:T(8,128)(2,1)S(1)} %get-tuple-element.101.own), channel_id=1, source_target_pairs={{0,2},{2,0},{1,3},{3,1},{4,6},{6,4},{5,7},{7,5},{8,10},{10,8},{9,1... | collective-permute-start | bytes 1572872 | tf_op jit(solution)/shard_map/ppermute | solution.py:405
  69.3 9.6 %copy-start.7 = (bf16[256,704]{1,0:T(8,128)(2,1)}, bf16[256,704]{1,0:T(8,128)(2,1)S(1)}, u32[]{:S(2)}) copy-start(bf16[256,704]{1,0:T(8,128)(2,1)S(1)} %get-tuple-element.120.refs_0_) | copy-start | bytes 1081348
  69.3 15.6 %collective-permute-start.13 = (bf16[256,704]{1,0:T(8,128)(2,1)S(1)}, bf16[256,704]{1,0:T(8,128)(2,1)S(1)}, u32[]{:S(2)}, u32[]{:S(2)}) collective-permute-start(bf16[256,704]{1,0:T(8,128)(2,1)S(1)} %get-tuple-element.104), channel_id=1, source_target_pairs={{0,4},{4,0},{8,12},{12,8},{1,5},{5,1},{9,13},{13,9},{2,6},{6,2},{1... | collective-permute-start | bytes 1081352 | tf_op jit(solution)/shard_map/ppermute | solution.py:409
  78.2 7.5 %collective-permute-start.14 = (bf16[256,1024]{1,0:T(8,128)(2,1)S(1)}, bf16[256,1024]{1,0:T(8,128)(2,1)S(1)}, u32[]{:S(2)}, u32[]{:S(2)}) collective-permute-start(bf16[256,1024]{1,0:T(8,128)(2,1)S(1)} %get-tuple-element.106), channel_id=1, source_target_pairs={{4,8},{8,4},{5,9},{9,5},{6,10},{10,6},{7,11},{11,7},{20,24},{24,20... | collective-permute-start | bytes 1572872 | tf_op jit(solution)/shard_map/ppermute | solution.py:407
  79.1 16.3 %collective-permute-start.15 = (bf16[256,1024]{1,0:T(8,128)(2,1)S(1)}, bf16[256,1024]{1,0:T(8,128)(2,1)S(1)}, u32[]{:S(2)}, u32[]{:S(2)}) collective-permute-start(bf16[256,1024]{1,0:T(8,128)(2,1)S(1)} %get-tuple-element.109.refs_2_), channel_id=1, source_target_pairs={{4,0},{8,12},{5,1},{9,13},{6,2},{10,14},{7,3},{11,15},{20,16},{24,... | collective-permute-start | bytes 1572872 | tf_op jit(solution)/shard_map/ppermute | solution.py:408
  85.0 16.9 %collective-permute-start.16 = (bf16[256,704]{1,0:T(8,128)(2,1)S(1)}, bf16[256,704]{1,0:T(8,128)(2,1)S(1)}, u32[]{:S(2)}, u32[]{:S(2)}) collective-permute-start(bf16[256,704]{1,0:T(8,128)(2,1)S(1)} %get-tuple-element.114), channel_id=1, source_target_pairs={{4,8},{8,4},{5,9},{9,5},{6,10},{10,6},{7,11},{11,7},{20,24},{24,20... | collective-permute-start | bytes 1081352 | tf_op jit(solution)/shard_map/ppermute | solution.py:407
  86.7 21.8 %collective-permute-start.17 = (bf16[256,1024]{1,0:T(8,128)(2,1)}, bf16[256,1024]{1,0:T(8,128)(2,1)}, u32[]{:S(2)}, u32[]{:S(2)}) collective-permute-start(bf16[256,1024]{1,0:T(8,128)(2,1)} %get-tuple-element.117.refs_2_), channel_id=1, source_target_pairs={{4,0},{8,12},{5,1},{9,13},{6,2},{10,14},{7,3},{11,15},{20,16},{24,... | collective-permute-start | bytes 1572872 | tf_op jit(solution)/shard_map/ppermute | solution.py:408
  102.9 14.6 %collective-permute-start.18 = (bf16[256,704]{1,0:T(8,128)(2,1)}, bf16[256,704]{1,0:T(8,128)(2,1)}, u32[]{:S(2)}, u32[]{:S(2)}) collective-permute-start(bf16[256,704]{1,0:T(8,128)(2,1)} %get-tuple-element.121.refs_2_), channel_id=1, source_target_pairs={{4,0},{8,12},{5,1},{9,13},{6,2},{10,14},{7,3},{11,15},{20,16},{24,... | collective-permute-start | bytes 1081352 | tf_op jit(solution)/shard_map/ppermute | solution.py:408
  108.5 1.0 copy-start.6
  109.5 8.0 %copy-start.8 = (bf16[256,704]{1,0:T(8,128)(2,1)S(1)}, bf16[256,704]{1,0:T(8,128)(2,1)}, u32[]{:S(2)}) copy-start(bf16[256,704]{1,0:T(8,128)(2,1)} %copy-done.7) | copy-start | bytes 1081348
  125.1 1.9 %collective-permute-start.19 = (f32[4,16]{1,0:T(4,128)S(1)}, f32[4,16]{1,0:T(4,128)S(1)}, u32[]{:S(2)}, u32[]{:S(2)}) collective-permute-start(f32[4,16]{1,0:T(4,128)S(1)} %maximum_select_fusion), channel_id=1, source_target_pairs={{0,1},{1,0},{2,3},{3,2},{4,5},{5,4},{6,7},{7,6},{8,9},{9,8},{10,11... | collective-permute-start | bytes 776 | tf_op jit(solution)/shard_map/ppermute | solution.py:387
  125.1 3.7 %collective-permute-start.20 = (f32[4,16]{1,0:T(4,128)S(1)}, f32[4,16]{1,0:T(4,128)S(1)}, u32[]{:S(2)}, u32[]{:S(2)}) collective-permute-start(f32[4,16]{1,0:T(4,128)S(1)} %maximum_select_fusion), channel_id=1, source_target_pairs={{0,2},{1,3},{2,0},{3,1},{4,6},{5,7},{6,4},{7,5},{8,10},{9,11},{10,... | collective-permute-start | bytes 776 | tf_op jit(solution)/shard_map/ppermute | solution.py:387
  126.7 3.0 %collective-permute-start.21 = (f32[4,16]{1,0:T(4,128)S(1)}, f32[4,16]{1,0:T(4,128)S(1)}, u32[]{:S(2)}, u32[]{:S(2)}) collective-permute-start(f32[4,16]{1,0:T(4,128)S(1)} %maximum_select_fusion), channel_id=1, source_target_pairs={{0,3},{1,2},{2,1},{3,0},{4,7},{5,6},{6,5},{7,4},{8,11},{9,10},{10,... | collective-permute-start | bytes 776 | tf_op jit(solution)/shard_map/ppermute | solution.py:387
  129.7 4.4 %collective-permute-start.22 = (f32[4,16]{1,0:T(4,128)S(1)}, f32[4,16]{1,0:T(4,128)S(1)}, u32[]{:S(2)}, u32[]{:S(2)}) collective-permute-start(f32[4,16]{1,0:T(4,128)S(1)} %add_add_fusion.2), channel_id=1, source_target_pairs={{0,4},{4,0},{8,12},{12,8},{1,5},{5,1},{9,13},{13,9},{2,6},{6,2},{1... | collective-permute-start | bytes 776 | tf_op jit(solution)/shard_map/ppermute | solution.py:387
  129.7 4.6 %collective-permute-start.23 = (f32[4,16]{1,0:T(4,128)S(1)}, f32[4,16]{1,0:T(4,128)S(1)}, u32[]{:S(2)}, u32[]{:S(2)}) collective-permute-start(f32[4,16]{1,0:T(4,128)S(1)} %add_add_fusion.2), channel_id=1, source_target_pairs={{0,8},{4,12},{8,0},{12,4},{1,9},{5,13},{9,1},{13,5},{2,10},{6,14},... | collective-permute-start | bytes 776 | tf_op jit(solution)/shard_map/ppermute | solution.py:387
  132.7 5.4 %collective-permute-start.24 = (f32[4,16]{1,0:T(4,128)S(1)}, f32[4,16]{1,0:T(4,128)S(1)}, u32[]{:S(2)}, u32[]{:S(2)}) collective-permute-start(f32[4,16]{1,0:T(4,128)S(1)} %add_add_fusion.2), channel_id=1, source_target_pairs={{0,12},{4,8},{8,4},{12,0},{1,13},{5,9},{9,5},{13,1},{2,14},{6,10},... | collective-permute-start | bytes 776 | tf_op jit(solution)/shard_map/ppermute | solution.py:387

commit v4 on v3

--- a/solution.py
+++ b/solution.py
@@ -15,7 +15,7 @@
 QLEN = 16
 PAD = 1
 MIB = 1024 * 1024
-TILE = 256
+TILE = 512
 WIDTHS = (1024, 1024)
 F32 = jnp.float32
 BF16 = jnp.bfloat16
@@ -68,7 +68,7 @@
     return copies
 
 
-def project_kernel(terms, far, first, order_ref, *refs):
+def project_kernel(terms, first, order_ref, *refs):
     del order_ref
     arrays = refs[: 2 * terms] if terms else ()
     if terms:
@@ -79,25 +79,29 @@
         scratch = refs[5:]
     basis_ref, sems = scratch[:2]
     copies = basis_copies(basis_hbm, basis_ref, sems, first)
-    if far:
+    if terms == 1:
         taken, row_sems = scratch[2:]
         row_copies = [
             pltpu.make_async_copy(a, taken.at[n], row_sems.at[n]) for n, a in enumerate(arrays)
         ]
         for copy in row_copies:
             copy.start()
-    for pair in copies:
+    for pair in copies[: 1 if terms == 1 else None]:
         for copy in pair:
             copy.start()
     if terms:
         split = arrays[0].shape[1]
         for n in range(2):
-            if far:
+            if terms == 1:
                 row_copies[n].wait()
                 rows_ref[n * split : (n + 1) * split] = taken[n].T
             else:
                 part = total_of([r[...] for r in arrays[n * terms : (n + 1) * terms]])
                 rows_ref[n * split : (n + 1) * split] = part.T
+    if terms == 1:
+        for pair in copies[1:]:
+            for copy in pair:
+                copy.start()
     for pair, (start, size) in zip(copies, column_tiles(basis_ref.shape[1])):
         for copy in pair:
             copy.wait()
@@ -109,7 +113,7 @@
     done_ref[...] = jnp.zeros_like(done_ref)
 
 
-def project(order, inputs, basis, start, width, far=False):
+def project(order, inputs, basis, start, width):
     depth = basis.shape[0]
     tiles = len(column_tiles(width))
     scratch = [pltpu.VMEM((depth, width), basis.dtype), pltpu.SemaphoreType.DMA((tiles, 2))]
@@ -117,8 +121,8 @@
         terms = len(inputs[0])
         arrays = list(inputs[0]) + list(inputs[1])
         rows = 2 * arrays[0].shape[1]
-        specs = [HBM if far else VMEM] * (2 * terms)
-        if far:
+        specs = [HBM if terms == 1 else VMEM] * (2 * terms)
+        if terms == 1:
             scratch += [
                 pltpu.VMEM((2,) + arrays[0].shape, BF16),
                 pltpu.SemaphoreType.DMA((2,)),
@@ -135,12 +139,12 @@
     if terms:
         out_shape.append(jax.ShapeDtypeStruct((rows, depth), BF16))
     out = pl.pallas_call(
-        functools.partial(project_kernel, terms, far, start),
+        functools.partial(project_kernel, terms, start),
         in_specs=[ANY] + specs + [HBM],
         out_specs=[VMEM] * (len(out_shape) + 1),
         out_shape=out_shape + [ORDER],
         scratch_shapes=scratch,
-        compiler_params=params(59 if far else 48),
+        compiler_params=params(59 if terms == 1 else 48),
         cost_estimate=QUICK,
         name="project",
     )(order, *arrays, basis)
@@ -234,6 +238,25 @@
         cost_estimate=QUICK,
         name="exchange",
     )(order, wide, came_in, across, following)
+
+
+def gate_kernel(order_ref, first_ref, second_ref, first_out, second_out, done_ref):
+    del order_ref, first_ref, second_ref, first_out, second_out
+    done_ref[...] = jnp.zeros_like(done_ref)
+
+
+def gate(order, first, second):
+    shapes = [jax.ShapeDtypeStruct(a.shape, a.dtype) for a in (first, second)]
+    return pl.pallas_call(
+        gate_kernel,
+        in_specs=[ANY] * 3,
+        out_specs=[ANY, ANY, VMEM],
+        out_shape=shapes + [ORDER],
+        input_output_aliases={1: 0, 2: 1},
+        compiler_params=params(16),
+        cost_estimate=QUICK,
+        name="gate",
+    )(order, first, second)
 
 
 def masked_kernel(order_ref, share_ref, came_ref, cand_ids_ref, query_ids_ref, acts_ref, done_ref):
@@ -296,33 +319,30 @@
     )(order, offsets, own, over)
 
 
-def row_tiles(width):
-    return [(start, min(512, width - start)) for start in range(0, width, 512)]
+def row_pieces(width):
+    return [(start, min(128, width - start)) for start in range(0, width, 128)]
 
 
 def score_kernel(blocks, pick, cand_rows, examples, first, order_ref, *refs):
     del order_ref
     per_block = 2 if pick else 1
     parts = refs[: blocks * per_block]
-    eig_hbm, split_ref, query_act_ref, out_ref, done_ref, eig_ref, sems = refs[blocks * per_block :]
+    (
+        eig_hbm, split_ref, query_act_ref, out_ref, done_ref, eig_ref, weights_ref, sems
+    ) = refs[blocks * per_block :]
     width = parts[0].shape[1]
+    features = eig_ref.shape[1]
     base = lax.axis_index("sub") * (eig_hbm.shape[0] // lax.axis_size("sub")) + first
-    copies = []
-    for n, (start, size) in enumerate(row_tiles(width)):
-        pieces = []
-        for m, top in enumerate(range(0, size, 128)):
-            rows = min(128, size - top)
-            pieces.append(
-                pltpu.make_async_copy(
-                    eig_hbm.at[pl.ds(pl.multiple_of(base + start + top, 8), rows), :],
-                    eig_ref.at[pl.ds(start + top, rows), :],
-                    sems.at[n, m],
-                )
-            )
-        copies.append(pieces)
-    for pieces in copies:
-        for copy in pieces:
-            copy.start()
+    copies = [
+        pltpu.make_async_copy(
+            eig_hbm.at[pl.ds(pl.multiple_of(base + start, 8), rows), :],
+            eig_ref.at[pl.ds(start, rows), :],
+            sems.at[n],
+        )
+        for n, (start, rows) in enumerate(row_pieces(width))
+    ]
+    for copy in copies:
+        copy.start()
     sums = []
     for b in range(blocks):
         here = parts[b * per_block]
@@ -330,32 +350,34 @@
             sums.append(jnp.where(is_inner(), here[...], parts[b * per_block + 1][...]))
         else:
             sums.append(here[...])
-    features = eig_ref.shape[1]
-    cand = jnp.concatenate([s[:cand_rows] for s in sums], 0)
-    query = jnp.concatenate([s[cand_rows:] for s in sums], 0)
-    scores = [0.0] * examples
-    for pieces, (start, size) in zip(copies, row_tiles(width)):
-        cand_tile = cand[:, start : start + size].T
-        query_tile = query[:, start : start + size].T.astype(F32)
-        for copy in pieces:
-            copy.wait()
-        inverse = 1.0 / eig_ref[start : start + size, :]
-        for k in range(examples):
-            outer = jnp.dot(
-                cand_tile,
-                split_ref[:, k * features : (k + 1) * features],
-                preferred_element_type=F32,
-            )
-            weights = (outer * inverse).astype(BF16)
-            image = lax.dot_general(
-                weights,
-                query_act_ref[...],
-                (((1,), (1,)), ((), ())),
-                preferred_element_type=F32,
-            )
-            scores[k] = scores[k] + jnp.sum(image * query_tile, axis=0, keepdims=True)
+    cand = jnp.concatenate([s[:cand_rows] for s in sums], 0).T
+    query = jnp.concatenate([s[cand_rows:] for s in sums], 0).T.astype(F32)
+
+    def outer_of(k):
+        return jnp.dot(
+            cand,
+            split_ref[:, k * features : (k + 1) * features],
+            preferred_element_type=F32,
+        )
+
+    outer = outer_of(0)
+    for copy in copies:
+        copy.wait()
+    eig_ref[...] = 1.0 / eig_ref[...]
     for k in range(examples):
-        out_ref[k : k + 1, :] = scores[k]
+        if k > 0:
+            outer = outer_of(k)
+        weights_ref[k * width : (k + 1) * width, :] = (outer * eig_ref[...]).astype(BF16)
+    image = lax.dot_general(
+        weights_ref[...],
+        query_act_ref[...],
+        (((1,), (1,)), ((), ())),
+        preferred_element_type=F32,
+    )
+    for k in range(examples):
+        out_ref[k : k + 1, :] = jnp.sum(
+            image[k * width : (k + 1) * width] * query, axis=0, keepdims=True
+        )
     done_ref[...] = jnp.zeros_like(done_ref)
 
 
@@ -370,7 +392,8 @@
         out_shape=[jax.ShapeDtypeStruct((examples, query_acts.shape[0]), F32), ORDER],
         scratch_shapes=[
             pltpu.VMEM((width, features), F32),
-            pltpu.SemaphoreType.DMA((len(row_tiles(width)), 4)),
+            pltpu.VMEM((examples * width, features), BF16),
+            pltpu.SemaphoreType.DMA((len(row_pieces(width)),)),
         ],
         compiler_params=params(42),
         cost_estimate=QUICK,
@@ -382,6 +405,10 @@
     size = lax.axis_size(axes)
     if size > 4:
         return lax.psum(value, axes)
+    if axes == "hid":
+        for other in (1, 2)[: size // 2]:
+            value = value + lax.ppermute(value, axes, [(i, i ^ other) for i in range(size)])
+        return value
     terms = [value]
     for other in range(1, size):
         terms.append(lax.ppermute(value, axes, [(i, i ^ other) for i in range(size)]))
@@ -391,7 +418,8 @@
 
 
 STEPS = (
-    "P0 P1 A1 S0 P2 S1 P3 E0 P4 S2 E1 HF P5 S3 E2 S4 F3 SP S5 F4 Z0 F5 Z1 Z2"
+    "P0", "P1", "A1", "XW", "S0", "P2", "S1", "P3", "E0", "P4", "S2", "E1", "HF",
+    "P5", "S3", "E2", "S4", "F3", "SP", "S5", "F4", "Z0", "F5", "Z1", "Z2",
 )
 
 
@@ -400,6 +428,7 @@
 ):
     rows = cand_grad.shape[0]
     examples = cand_offsets.shape[0]
+    both = ("ex", "sub")
     bounds = chunk_bounds(basis_g.shape[1])
     count = len(bounds)
     swap = lambda a, axis: lax.ppermute(a, axis, [(0, 1), (1, 0)])
@@ -408,23 +437,27 @@
     outward = lambda a: lax.ppermute(a, "hid", [(1, 0), (2, 3)])
     beside = lambda a: lax.ppermute(a, "hid", [(0, 1), (1, 0), (2, 3), (3, 2)])
 
-    tokens = [
-        ([cand_grad.T], [query_grad.T]),
-        ([swap(cand_grad, "ex").T], [swap(query_grad, "ex").T]),
-    ]
+    cand_over = lax.ppermute(cand_grad, both, [(0, 2), (2, 0)])
+    query_over = lax.ppermute(query_grad, both, [(1, 3), (3, 1)])
+    tokens = [([cand_grad.T], [query_grad.T]), None]
     order = jnp.zeros((8, 128), F32)
     wide, sends, ins, crossed, summed, outs = {}, {}, {}, {}, {}, {}
     scores = []
     share = came = acts = acts_over = split = query_acts = None
-    for step in STEPS.split():
+    for step in STEPS:
         kind, c = step[0], int(step[1]) if step[1].isdigit() else None
         if kind == "P":
             block, q = divmod(c, count)
             wide[c], sends[c], tokens[block], order = project(
-                order, tokens[block], basis_g, *bounds[q], far=c == 0
+                order, tokens[block], basis_g, *bounds[q]
             )
             if block == 0:
                 ins[c] = inward(sends[c])
+        elif step == "XW":
+            cand_turned, query_turned, order = gate(order, cand_over.T, query_over.T)
+            cand_across = lax.ppermute(cand_turned, both, [(0, 1), (2, 3)])
+            query_across = lax.ppermute(query_turned, both, [(1, 0), (3, 2)])
+            tokens[1] = ([cand_turned, cand_across], [query_turned, query_across])
         elif step == "A1":
             share, order = act_shares(order, cand_act, query_act, basis_a)
             came = swap(share, "sub")

time: 139 us -> 141 us (1.014)
  Pallas kernels: 60.5 us -> 53.9 us
  starting transfers between devices: 37.6 us -> 43.2 us
  waiting for transfers between devices: 34.6 us -> 37.3 us
    ppermute x0 -> x4, starting transfers between devices: none -> 8.17 us  [the longest x1 4.84 us: token_scores_paired(): cand_over = lax.ppermute(cand_grad, both, [(0, 2), (2, 0)])]
    pallas_call x6 -> x7, Pallas kernels: 31.3 us -> 26.3 us  [the longest x6 26.3 us: project(): pl.pallas_call(functools.partial(project_kernel, terms, start), in_specs=...]
    ppermute x3, waiting for transfers between devices: 3.64 us -> 7.23 us  [token_scores_paired(): inward = lambda a: lax.ppermute(a, 'hid', [(0, 1), (3, 2)])]
    ppermute x4 -> x2, waiting for transfers between devices: 1.82 us -> 0.01 us  [token_scores_paired(): swap = lambda a, axis: lax.ppermute(a, axis, [(0, 1), (1, 0)])]
    ppermute x3, starting transfers between devices: 13.6 us -> 12.2 us  [token_scores_paired(): inward = lambda a: lax.ppermute(a, 'hid', [(0, 1), (3, 2)])]
    ppermute x6 -> x5, waiting for transfers between devices: 6.75 us -> 8.03 us  [small_sum(): lax.ppermute(value, axes, [(i, i ^ other) for i in range(size)])]
    ppermute x6 -> x5, starting transfers between devices: 6.25 us -> 5.06 us  [small_sum(): lax.ppermute(value, axes, [(i, i ^ other) for i in range(size)])]
    ppermute x4 -> x2, starting transfers between devices: 3.72 us -> 2.79 us  [token_scores_paired(): swap = lambda a, axis: lax.ppermute(a, axis, [(0, 1), (1, 0)])]
  transfers between devices with their start and end apart: 25 -> 26, of which waited for: 11 -> 11; matrix products, arithmetic and copies ran while one was open for 0% -> 0% of each run, Pallas kernels for 32% -> 34%
where the time goes in v4:
time: 141 us
  Pallas kernels  53.9 us (38%)
  starting transfers between devices  43.2 us (31%)
  waiting for transfers between devices  37.3 us (26%)
  local copies, waits for them, and re-layouts  5.03 us (4%)
    pallas_call x6, Pallas kernels, project(): pl.pallas_call(functools.partial(project_kernel, terms, start), in_specs=...  26.3 us
    pallas_call x3, Pallas kernels, score_chunk(): pl.pallas_call(functools.partial(score_kernel, len(blocks), pick, cand_ro...  21.7 us
    ppermute x3, starting transfers between devices, token_scores_paired(): inward = lambda a: lax.ppermute(a, 'hid', [(0, 1), (3, 2)])  12.2 us
    ppermute x3, waiting for transfers between devices, token_scores_paired(): beside = lambda a: lax.ppermute(a, 'hid', [(0, 1), (1, 0), (2, 3), (3, 2)])  11.7 us
    ppermute x3, waiting for transfers between devices, token_scores_paired(): outward = lambda a: lax.ppermute(a, 'hid', [(1, 0), (2, 3)])  10.3 us
    ppermute x5, waiting for transfers between devices, small_sum(): lax.ppermute(value, axes, [(i, i ^ other) for i in range(size)])  8.03 us
    ppermute x3, waiting for transfers between devices, token_scores_paired(): inward = lambda a: lax.ppermute(a, 'hid', [(0, 1), (3, 2)])  7.23 us
    ppermute x3, starting transfers between devices, token_scores_paired(): beside = lambda a: lax.ppermute(a, 'hid', [(0, 1), (1, 0), (2, 3), (3, 2)])  6.83 us
  transfers between devices with their start and end apart: 26, of which 11 were waited for; matrix products, arithmetic and copies ran while one was open for 0% of the time, Pallas kernels for 34%

profile of v4, /device:TPU:0, one launch (start us, length us, event | category | flops | bytes accessed | tf_op | source)
XLA Modules:
  0.0 140.8 jit_solution(5269912248933000016)
XLA Ops:
  0.0 4.8 %collective-permute-start = (bf16[128,2752]{0,1:T(8,128)(2,1)}, bf16[128,2752]{0,1:T(8,128)(2,1)S(1)}, u32[]{:S(2)}, u32[]{:S(2)}) collective-permute-start(bf16[128,2752]{0,1:T(8,128)(2,1)} %param.10), channel_id=1, source_target_pairs={{0,2},{2,0},{4,6},{6,4},{8,10},{10,8},{12,14},{14,12},{16,18},{18,... | collective-permute-start | bytes 2113544 | tf_op jit(solution)/shard_map/ppermute | solution.py:440
  4.8 0.7 collective-permute-start.1
  6.2 6.2 %project.6 = (f32[256,1024]{1,0:T(8,128)}, bf16[256,1024]{1,0:T(8,128)(2,1)}, bf16[256,2752]{1,0:T(8,128)(2,1)}, f32[8,128]{1,0:T(8,128)}) custom-call(f32[8,128]{1,0:T(8,128)} %broadcast_in_dim.9.order_ref, bf16[2752,128]{1,0:T(8,128)(2,1)} %bitcast.10, bf16[2752,128]{1,0:T(8,128)(2,1)} %bitcast.11, bf16[2752,2752]{1,0:T(8,128)(2,1)} %refs_1_.7), custom_call_target="tpu_custom_call" | custom-call | flops 1024 | bytes 1024 | tf_op jit(solution)/shard_map/project/pallas_call | solution.py:141
  12.4 3.5 %collective-permute-start.2 = (bf16[256,1024]{1,0:T(8,128)(2,1)}, bf16[256,1024]{1,0:T(8,128)(2,1)S(1)}, u32[]{:S(2)}, u32[]{:S(2)}) collective-permute-start(bf16[256,1024]{1,0:T(8,128)(2,1)} %get-tuple-element.73), channel_id=1, source_target_pairs={{0,4},{12,8},{1,5},{13,9},{2,6},{14,10},{3,7},{15,11},{16,20},{28,... | collective-permute-start | bytes 1572872 | tf_op jit(solution)/shard_map/ppermute | solution.py:435
  15.9 1.4 copy-done
  17.9 3.8 %project.7 = (f32[256,1024]{1,0:T(8,128)S(1)}, bf16[256,1024]{1,0:T(8,128)(2,1)S(1)}, f32[8,128]{1,0:T(8,128)S(1)}) custom-call(f32[8,128]{1,0:T(8,128)S(1)} %copy-done.9, bf16[256,2752]{1,0:T(8,128)(2,1)S(1)} %copy-done, bf16[2752,2752]{1,0:T(8,128)(2,1)} %refs_1_.7), custom_call_target="tpu_custom_call" | custom-call | flops 1024 | bytes 1024 | tf_op jit(solution)/shard_map/project/pallas_call | solution.py:141
  22.1 2.1 %acts.1 = (f32[256,1024]{1,0:T(8,128)S(1)}, f32[8,128]{1,0:T(8,128)S(1)}) custom-call(f32[8,128]{1,0:T(8,128)S(1)} %get-tuple-element.69.order_ref, bf16[128,2048]{1,0:T(8,128)(2,1)S(1)} %copy-done.3, bf16[128,2048]{1,0:T(8,128)(2,1)S(1)} %copy-done.4, bf16[2048,1024]{1,0:T(8,128)(2,1)S(1)} %copy-done.2), custom_call_target="tpu_custom_call" | custom-call | flops 1024 | bytes 1024 | tf_op jit(solution)/shard_map/acts/pallas_call | solution.py:174
  24.2 1.3 collective-permute-start.4
  25.6 1.3 collective-permute-start.5
  26.9 1.5 %collective-permute-start.3 = (bf16[256,1024]{1,0:T(8,128)(2,1)S(1)}, bf16[256,1024]{1,0:T(8,128)(2,1)S(1)}, u32[]{:S(2)}, u32[]{:S(2)}) collective-permute-start(bf16[256,1024]{1,0:T(8,128)(2,1)S(1)} %get-tuple-element.77), channel_id=1, source_target_pairs={{0,4},{12,8},{1,5},{13,9},{2,6},{14,10},{3,7},{15,11},{16,20},{28,... | collective-permute-start | bytes 1572872 | tf_op jit(solution)/shard_map/ppermute | solution.py:435
  28.3 1.1 collective-permute-start.9
  29.5 0.7 collective-permute-start.6
  30.2 4.8 %project.8 = (f32[256,704]{1,0:T(8,128)S(1)}, bf16[256,704]{1,0:T(8,128)(2,1)}, f32[8,128]{1,0:T(8,128)S(1)}) custom-call(f32[8,128]{1,0:T(8,128)S(1)} %get-tuple-element.74.order_ref, bf16[256,2752]{1,0:T(8,128)(2,1)S(1)} %copy-done, bf16[2752,2752]{1,0:T(8,128)(2,1)} %refs_1_.7), custom_call_target="tpu_custom_call" | custom-call | flops 1024 | bytes 1024 | tf_op jit(solution)/shard_map/project/pallas_call | solution.py:141
  35.0 5.3 %collective-permute-done.3.refs_1_.in_ref = bf16[256,1024]{1,0:T(8,128)(2,1)S(1)} collective-permute-done((bf16[256,1024]{1,0:T(8,128)(2,1)S(1)}, bf16[256,1024]{1,0:T(8,128)(2,1)S(1)}, u32[]{:S(2)}, u32[]{:S(2)}) %collective-permute-start.3) | collective-permute-done | bytes 524320 | tf_op jit(solution)/shard_map/ppermute | solution.py:435
  40.4 0.7 collective-permute-start.8
  41.1 7.2 %collective-permute-start.7 = (bf16[256,704]{1,0:T(8,128)(2,1)}, bf16[256,704]{1,0:T(8,128)(2,1)S(1)}, u32[]{:S(2)}, u32[]{:S(2)}) collective-permute-start(bf16[256,704]{1,0:T(8,128)(2,1)} %get-tuple-element.88), channel_id=1, source_target_pairs={{0,4},{12,8},{1,5},{13,9},{2,6},{14,10},{3,7},{15,11},{16,20},{28,... | collective-permute-start | bytes 1081352 | tf_op jit(solution)/shard_map/ppermute | solution.py:435
  48.3 3.9 %project.9 = (f32[256,1024]{1,0:T(8,128)S(1)}, bf16[256,1024]{1,0:T(8,128)(2,1)S(1)}, bf16[256,2752]{1,0:T(8,128)(2,1)S(1)}, f32[8,128]{1,0:T(8,128)S(1)}) custom-call(f32[8,128]{1,0:T(8,128)S(1)} %get-tuple-element.78.order_ref, bf16[2752,128]{1,0:T(8,128)(2,1)S(1)} %get-tuple-element.79.refs_0_, bf16[2752,128]{1,0:T(8,128)(2,1)S(1)} %collective-permute-done.4.refs_1_, ...), custom_call_target="tpu_custom_call" | custom-call | flops 1024 | bytes 1024 | tf_op jit(solution)/shard_map/project/pallas_call | solution.py:141
  52.4 3.7 %project.10 = (f32[256,1024]{1,0:T(8,128)S(1)}, bf16[256,1024]{1,0:T(8,128)(2,1)S(1)}, f32[8,128]{1,0:T(8,128)S(1)}) custom-call(f32[8,128]{1,0:T(8,128)S(1)} %get-tuple-element.84.order_ref, bf16[256,2752]{1,0:T(8,128)(2,1)S(1)} %get-tuple-element.85.refs_0_, bf16[2752,2752]{1,0:T(8,128)(2,1)} %refs_1_.7), custom_call_target="tpu_custom_call" | custom-call | flops 1024 | bytes 1024 | tf_op jit(solution)/shard_map/project/pallas_call | solution.py:141
  56.1 2.0 %collective-permute-done.7.refs_1_.in_ref = bf16[256,704]{1,0:T(8,128)(2,1)S(1)} collective-permute-done((bf16[256,704]{1,0:T(8,128)(2,1)}, bf16[256,704]{1,0:T(8,128)(2,1)S(1)}, u32[]{:S(2)}, u32[]{:S(2)}) %collective-permute-start.7) | collective-permute-done | bytes 360480 | tf_op jit(solution)/shard_map/ppermute | solution.py:435
  58.2 0.8 copy-done.5
  59.0 2.5 %collective-permute-start.12 = (bf16[256,1024]{1,0:T(8,128)(2,1)S(1)}, bf16[256,1024]{1,0:T(8,128)(2,1)S(1)}, u32[]{:S(2)}, u32[]{:S(2)}) collective-permute-start(bf16[256,1024]{1,0:T(8,128)(2,1)S(1)} %get-tuple-element.103), channel_id=1, source_target_pairs={{0,4},{4,0},{8,12},{12,8},{1,5},{5,1},{9,13},{13,9},{2,6},{6,2},{1... | collective-permute-start | bytes 1572872 | tf_op jit(solution)/shard_map/ppermute | solution.py:438
  62.4 4.0 %project.11 = (f32[256,704]{1,0:T(8,128)S(1)}, bf16[256,704]{1,0:T(8,128)(2,1)S(1)}, f32[8,128]{1,0:T(8,128)S(1)}) custom-call(f32[8,128]{1,0:T(8,128)S(1)} %get-tuple-element.94.order_ref, bf16[256,2752]{1,0:T(8,128)(2,1)S(1)} %get-tuple-element.85.refs_0_, bf16[2752,2752]{1,0:T(8,128)(2,1)} %refs_1_.7), custom_call_target="tpu_custom_call" | custom-call | flops 1024 | bytes 1024 | tf_op jit(solution)/shard_map/project/pallas_call | solution.py:141
  66.5 2.7 %collective-permute-done.10.refs_1_ = bf16[256,1024]{1,0:T(8,128)(2,1)S(1)} collective-permute-done((bf16[256,1024]{1,0:T(8,128)(2,1)S(1)}, bf16[256,1024]{1,0:T(8,128)(2,1)S(1)}, u32[]{:S(2)}, u32[]{:S(2)}) %collective-permute-start.10) | collective-permute-done | bytes 524320 | tf_op jit(solution)/shard_map/ppermute | solution.py:438
  69.3 0.7 collective-permute-start.13
  70.0 1.7 %collective-permute-start.14 = (bf16[256,1024]{1,0:T(8,128)(2,1)S(1)}, bf16[256,1024]{1,0:T(8,128)(2,1)S(1)}, u32[]{:S(2)}, u32[]{:S(2)}) collective-permute-start(bf16[256,1024]{1,0:T(8,128)(2,1)S(1)} %get-tuple-element.107.own), channel_id=1, source_target_pairs={{0,2},{2,0},{1,3},{3,1},{4,6},{6,4},{5,7},{7,5},{8,10},{10,8},{9,1... | collective-permute-start | bytes 1572872 | tf_op jit(solution)/shard_map/ppermute | solution.py:434
  71.7 4.3 %collective-permute-start.15 = (bf16[256,704]{1,0:T(8,128)(2,1)S(1)}, bf16[256,704]{1,0:T(8,128)(2,1)S(1)}, u32[]{:S(2)}, u32[]{:S(2)}) collective-permute-start(bf16[256,704]{1,0:T(8,128)(2,1)S(1)} %get-tuple-element.110), channel_id=1, source_target_pairs={{0,4},{4,0},{8,12},{12,8},{1,5},{5,1},{9,13},{13,9},{2,6},{6,2},{1... | collective-permute-start | bytes 1081352 | tf_op jit(solution)/shard_map/ppermute | solution.py:438
  76.0 4.4 %collective-permute-done.12.refs_1_ = bf16[256,1024]{1,0:T(8,128)(2,1)S(1)} collective-permute-done((bf16[256,1024]{1,0:T(8,128)(2,1)S(1)}, bf16[256,1024]{1,0:T(8,128)(2,1)S(1)}, u32[]{:S(2)}, u32[]{:S(2)}) %collective-permute-start.12) | collective-permute-done | bytes 524320 | tf_op jit(solution)/shard_map/ppermute | solution.py:438
  80.5 0.7 collective-permute-start.16
  81.4 1.3 collective-permute-start.17
  82.7 0.8 split_acts.1
  83.5 4.6 %collective-permute-done.15.refs_1_ = bf16[256,704]{1,0:T(8,128)(2,1)S(1)} collective-permute-done((bf16[256,704]{1,0:T(8,128)(2,1)S(1)}, bf16[256,704]{1,0:T(8,128)(2,1)S(1)}, u32[]{:S(2)}, u32[]{:S(2)}) %collective-permute-start.15) | collective-permute-done | bytes 360480 | tf_op jit(solution)/shard_map/ppermute | solution.py:438
  88.9 1.0 add.53
  89.8 1.3 collective-permute-start.19
  91.1 6.1 %collective-permute-done.17.refs_3_ = bf16[256,1024]{1,0:T(8,128)(2,1)S(1)} collective-permute-done((bf16[256,1024]{1,0:T(8,128)(2,1)S(1)}, bf16[256,1024]{1,0:T(8,128)(2,1)S(1)}, u32[]{:S(2)}, u32[]{:S(2)}) %collective-permute-start.17) | collective-permute-done | bytes 524320 | tf_op jit(solution)/shard_map/ppermute | solution.py:437
  97.3 6.9 %score.3 = (f32[4,256]{1,0:T(4,128)S(1)}, f32[8,128]{1,0:T(8,128)S(1)}) custom-call(f32[8,128]{1,0:T(8,128)S(1)} %get-tuple-element.113.order_ref, bf16[256,1024]{1,0:T(8,128)(2,1)S(1)} %get-tuple-element.114.refs_0_, bf16[256,1024]{1,0:T(8,128)(2,1)S(1)} %collective-permute-done.10.refs_1_, bf16[256,1024]{1,0:T(8,128)(2,1)S(1)} %get-tuple-element.115.refs_2_, ...), custom_call_target="tpu_custom_call" | custom-call | flops 1024 | bytes 1024 | tf_op jit(solution)/shard_map/score/pallas_call | solution.py:388
  104.2 0.9 add.54
  105.1 1.5 %collective-permute-start.20 = (bf16[256,704]{1,0:T(8,128)(2,1)}, bf16[256,704]{1,0:T(8,128)(2,1)}, u32[]{:S(2)}, u32[]{:S(2)}) collective-permute-start(bf16[256,704]{1,0:T(8,128)(2,1)} %get-tuple-element.127.refs_2_), channel_id=1, source_target_pairs={{4,0},{8,12},{5,1},{9,13},{6,2},{10,14},{7,3},{11,15},{20,16},{24,... | collective-permute-start | bytes 1081352 | tf_op jit(solution)/shard_map/ppermute | solution.py:437
  106.7 4.2 %collective-permute-done.19.refs_3_ = bf16[256,1024]{1,0:T(8,128)(2,1)} collective-permute-done((bf16[256,1024]{1,0:T(8,128)(2,1)}, bf16[256,1024]{1,0:T(8,128)(2,1)}, u32[]{:S(2)}, u32[]{:S(2)}) %collective-permute-start.19) | collective-permute-done | bytes 524320 | tf_op jit(solution)/shard_map/ppermute | solution.py:437
  110.9 1.0 copy-done.6
  111.9 8.1 %score.4 = (f32[4,256]{1,0:T(4,128)S(1)}, f32[8,128]{1,0:T(8,128)S(1)}) custom-call(f32[8,128]{1,0:T(8,128)S(1)} %get-tuple-element.121.order_ref, bf16[256,1024]{1,0:T(8,128)(2,1)S(1)} %copy-done.6, bf16[256,1024]{1,0:T(8,128)(2,1)S(1)} %collective-permute-done.12.refs_1_, bf16[256,1024]{1,0:T(8,128)(2,1)} %get-tuple-element.123.refs_2_, ...), custom_call_target="tpu_custom_call" | custom-call | flops 1024 | bytes 1024 | tf_op jit(solution)/shard_map/score/pallas_call | solution.py:388
  120.0 6.7 %score.5 = (f32[4,256]{1,0:T(4,128)S(1)}, f32[8,128]{1,0:T(8,128)}) custom-call(f32[8,128]{1,0:T(8,128)S(1)} %get-tuple-element.125.order_ref, bf16[256,704]{1,0:T(8,128)(2,1)S(1)} %copy-done.8, bf16[256,704]{1,0:T(8,128)(2,1)S(1)} %collective-permute-done.15.refs_1_, bf16[256,704]{1,0:T(8,128)(2,1)} %get-tuple-element.127.refs_2_, ...), custom_call_target="tpu_custom_call" | custom-call | flops 1024 | bytes 1024 | tf_op jit(solution)/shard_map/score/pallas_call | solution.py:388
  127.1 2.0 %collective-permute-start.22 = (f32[4,16]{1,0:T(4,128)S(1)}, f32[4,16]{1,0:T(4,128)S(1)}, u32[]{:S(2)}, u32[]{:S(2)}) collective-permute-start(f32[4,16]{1,0:T(4,128)S(1)} %maximum_select_fusion), channel_id=1, source_target_pairs={{0,2},{1,3},{2,0},{3,1},{4,6},{5,7},{6,4},{7,5},{8,10},{9,11},{10,... | collective-permute-start | bytes 776 | tf_op jit(solution)/shard_map/ppermute | solution.py:414
  129.1 1.6 %collective-permute-done.22 = f32[4,16]{1,0:T(4,128)S(1)} collective-permute-done((f32[4,16]{1,0:T(4,128)S(1)}, f32[4,16]{1,0:T(4,128)S(1)}, u32[]{:S(2)}, u32[]{:S(2)}) %collective-permute-start.22) | collective-permute-done | bytes 288 | tf_op jit(solution)/shard_map/ppermute | solution.py:414
  130.7 1.4 collective-permute-done.23
  132.1 1.5 %collective-permute-start.24 = (f32[4,16]{1,0:T(4,128)S(1)}, f32[4,16]{1,0:T(4,128)S(1)}, u32[]{:S(2)}, u32[]{:S(2)}) collective-permute-start(f32[4,16]{1,0:T(4,128)S(1)} %add_add_fusion.1), channel_id=1, source_target_pairs={{0,4},{4,0},{8,12},{12,8},{1,5},{5,1},{9,13},{13,9},{2,6},{6,2},{1... | collective-permute-start | bytes 776 | tf_op jit(solution)/shard_map/ppermute | solution.py:410
  133.6 2.0 %collective-permute-done.24 = f32[4,16]{1,0:T(4,128)S(1)} collective-permute-done((f32[4,16]{1,0:T(4,128)S(1)}, f32[4,16]{1,0:T(4,128)S(1)}, u32[]{:S(2)}, u32[]{:S(2)}) %collective-permute-start.24) | collective-permute-done | bytes 288 | tf_op jit(solution)/shard_map/ppermute | solution.py:410
  135.7 1.4 %collective-permute-start.25 = (f32[4,16]{1,0:T(4,128)S(1)}, f32[4,16]{1,0:T(4,128)S(1)}, u32[]{:S(2)}, u32[]{:S(2)}) collective-permute-start(f32[4,16]{1,0:T(4,128)S(1)} %add.38), channel_id=1, source_target_pairs={{0,8},{4,12},{8,0},{12,4},{1,9},{5,13},{9,1},{13,5},{2,10},{6,14},... | collective-permute-start | bytes 776 | tf_op jit(solution)/shard_map/ppermute | solution.py:410
  137.1 3.1 %collective-permute-done.25 = f32[4,16]{1,0:T(4,128)S(1)} collective-permute-done((f32[4,16]{1,0:T(4,128)S(1)}, f32[4,16]{1,0:T(4,128)S(1)}, u32[]{:S(2)}, u32[]{:S(2)}) %collective-permute-start.25) | collective-permute-done | bytes 288 | tf_op jit(solution)/shard_map/ppermute | solution.py:410
  (65 shorter events, 5.4 us)
Async XLA Ops:
  0.0 24.2 %collective-permute-start = (bf16[128,2752]{0,1:T(8,128)(2,1)}, bf16[128,2752]{0,1:T(8,128)(2,1)S(1)}, u32[]{:S(2)}, u32[]{:S(2)}) collective-permute-start(bf16[128,2752]{0,1:T(8,128)(2,1)} %param.10), channel_id=1, source_target_pairs={{0,2},{2,0},{4,6},{6,4},{8,10},{10,8},{12,14},{14,12},{16,18},{18,... | collective-permute-start | bytes 2113544 | tf_op jit(solution)/shard_map/ppermute | solution.py:440
  4.8 19.4 %collective-permute-start.1 = (bf16[128,2752]{0,1:T(8,128)(2,1)}, bf16[128,2752]{0,1:T(8,128)(2,1)S(1)}, u32[]{:S(2)}, u32[]{:S(2)}) collective-permute-start(bf16[128,2752]{0,1:T(8,128)(2,1)} %param.11), channel_id=1, source_target_pairs={{1,3},{3,1},{5,7},{7,5},{9,11},{11,9},{13,15},{15,13},{17,19},{19,... | collective-permute-start | bytes 2113544 | tf_op jit(solution)/shard_map/ppermute | solution.py:441
  12.4 17.1 %collective-permute-start.2 = (bf16[256,1024]{1,0:T(8,128)(2,1)}, bf16[256,1024]{1,0:T(8,128)(2,1)S(1)}, u32[]{:S(2)}, u32[]{:S(2)}) collective-permute-start(bf16[256,1024]{1,0:T(8,128)(2,1)} %get-tuple-element.73), channel_id=1, source_target_pairs={{0,4},{12,8},{1,5},{13,9},{2,6},{14,10},{3,7},{15,11},{16,20},{28,... | collective-permute-start | bytes 1572872 | tf_op jit(solution)/shard_map/ppermute | solution.py:435
  15.9 1.4 copy-start
  17.2 0.7 copy-start.9
  17.9 3.9 %copy-start.2 = (bf16[2048,1024]{1,0:T(8,128)(2,1)S(1)}, bf16[2048,1024]{1,0:T(8,128)(2,1)}, u32[]{:S(2)}) copy-start(bf16[2048,1024]{1,0:T(8,128)(2,1)} %basis_hbm.1) | copy-start | bytes 12582916
  17.9 4.0 %copy-start.3 = (bf16[128,2048]{1,0:T(8,128)(2,1)S(1)}, bf16[128,2048]{1,0:T(8,128)(2,1)}, u32[]{:S(2)}) copy-start(bf16[128,2048]{1,0:T(8,128)(2,1)} %cand_ref.1) | copy-start | bytes 1572868
  17.9 4.2 %copy-start.4 = (bf16[128,2048]{1,0:T(8,128)(2,1)S(1)}, bf16[128,2048]{1,0:T(8,128)(2,1)}, u32[]{:S(2)}) copy-start(bf16[128,2048]{1,0:T(8,128)(2,1)} %query_ref.1) | copy-start | bytes 1572868
  21.7 7.7 %copy-start.1 = (f32[256,1024]{1,0:T(8,128)S(1)}, f32[256,1024]{1,0:T(8,128)}, u32[]{:S(2)}) copy-start(f32[256,1024]{1,0:T(8,128)} %get-tuple-element.72.refs_0_.wide_ref) | copy-start | bytes 3145732
  24.2 16.8 %collective-permute-start.4 = (bf16[2752,128]{1,0:T(8,128)(2,1)S(1)}, bf16[2752,128]{1,0:T(8,128)(2,1)S(1)}, u32[]{:S(2)}, u32[]{:S(2)}) collective-permute-start(bf16[2752,128]{1,0:T(8,128)(2,1)S(1)} %get-tuple-element.79.refs_0_), channel_id=1, source_target_pairs={{0,1},{2,3},{4,5},{6,7},{8,9},{10,11},{12,13},{14,15},{16,17},{18,... | collective-permute-start | bytes 2113544 | tf_op jit(solution)/shard_map/ppermute | solution.py:458
  25.6 22.7 %collective-permute-start.5 = (bf16[2752,128]{1,0:T(8,128)(2,1)S(1)}, bf16[2752,128]{1,0:T(8,128)(2,1)S(1)}, u32[]{:S(2)}, u32[]{:S(2)}) collective-permute-start(bf16[2752,128]{1,0:T(8,128)(2,1)S(1)} %get-tuple-element.80.refs_2_), channel_id=1, source_target_pairs={{1,0},{3,2},{5,4},{7,6},{9,8},{11,10},{13,12},{15,14},{17,16},{19,... | collective-permute-start | bytes 2113544 | tf_op jit(solution)/shard_map/ppermute | solution.py:459
  26.9 13.4 %collective-permute-start.3 = (bf16[256,1024]{1,0:T(8,128)(2,1)S(1)}, bf16[256,1024]{1,0:T(8,128)(2,1)S(1)}, u32[]{:S(2)}, u32[]{:S(2)}) collective-permute-start(bf16[256,1024]{1,0:T(8,128)(2,1)S(1)} %get-tuple-element.77), channel_id=1, source_target_pairs={{0,4},{12,8},{1,5},{13,9},{2,6},{14,10},{3,7},{15,11},{16,20},{28,... | collective-permute-start | bytes 1572872 | tf_op jit(solution)/shard_map/ppermute | solution.py:435
  28.3 33.8 %collective-permute-start.9 = (f32[256,1024]{1,0:T(8,128)S(1)}, f32[256,1024]{1,0:T(8,128)S(1)}, u32[]{:S(2)}, u32[]{:S(2)}) collective-permute-start(f32[256,1024]{1,0:T(8,128)S(1)} %get-tuple-element.93.share_ref), channel_id=1, source_target_pairs={{0,1},{1,0},{2,3},{3,2},{4,5},{5,4},{6,7},{7,6},{8,9},{9,8},{10,11... | collective-permute-start | bytes 3145736 | tf_op jit(solution)/shard_map/ppermute | solution.py:434
  29.5 22.6 %collective-permute-start.6 = (bf16[256,1024]{1,0:T(8,128)(2,1)S(1)}, bf16[256,1024]{1,0:T(8,128)(2,1)S(1)}, u32[]{:S(2)}, u32[]{:S(2)}) collective-permute-start(bf16[256,1024]{1,0:T(8,128)(2,1)S(1)} %get-tuple-element.82), channel_id=1, source_target_pairs={{4,8},{8,4},{5,9},{9,5},{6,10},{10,6},{7,11},{11,7},{20,24},{24,20... | collective-permute-start | bytes 1572872 | tf_op jit(solution)/shard_map/ppermute | solution.py:436
  40.4 17.7 %collective-permute-start.8 = (bf16[256,1024]{1,0:T(8,128)(2,1)S(1)}, bf16[256,1024]{1,0:T(8,128)(2,1)S(1)}, u32[]{:S(2)}, u32[]{:S(2)}) collective-permute-start(bf16[256,1024]{1,0:T(8,128)(2,1)S(1)} %get-tuple-element.90), channel_id=1, source_target_pairs={{4,8},{8,4},{5,9},{9,5},{6,10},{10,6},{7,11},{11,7},{20,24},{24,20... | collective-permute-start | bytes 1572872 | tf_op jit(solution)/shard_map/ppermute | solution.py:436
  41.1 17.0 %collective-permute-start.7 = (bf16[256,704]{1,0:T(8,128)(2,1)}, bf16[256,704]{1,0:T(8,128)(2,1)S(1)}, u32[]{:S(2)}, u32[]{:S(2)}) collective-permute-start(bf16[256,704]{1,0:T(8,128)(2,1)} %get-tuple-element.88), channel_id=1, source_target_pairs={{0,4},{12,8},{1,5},{13,9},{2,6},{14,10},{3,7},{15,11},{16,20},{28,... | collective-permute-start | bytes 1081352 | tf_op jit(solution)/shard_map/ppermute | solution.py:435
  52.3 16.9 %collective-permute-start.10 = (bf16[256,1024]{1,0:T(8,128)(2,1)S(1)}, bf16[256,1024]{1,0:T(8,128)(2,1)S(1)}, u32[]{:S(2)}, u32[]{:S(2)}) collective-permute-start(bf16[256,1024]{1,0:T(8,128)(2,1)S(1)} %get-tuple-element.97), channel_id=1, source_target_pairs={{0,4},{4,0},{8,12},{12,8},{1,5},{5,1},{9,13},{13,9},{2,6},{6,2},{1... | collective-permute-start | bytes 1572872 | tf_op jit(solution)/shard_map/ppermute | solution.py:438
  52.3 9.8 %copy-start.11 = (s32[128]{0:T(128)S(1)}, s32[128]{0:T(128)}, u32[]{:S(2)}) copy-start(s32[128]{0:T(128)} %param.14) | copy-start | bytes 1540
  52.4 9.8 %copy-start.12 = (s32[128]{0:T(128)S(1)}, s32[128]{0:T(128)}, u32[]{:S(2)}) copy-start(s32[128]{0:T(128)} %param.15) | copy-start | bytes 1540
  58.2 0.8 copy-start.5
  59.0 21.4 %collective-permute-start.12 = (bf16[256,1024]{1,0:T(8,128)(2,1)S(1)}, bf16[256,1024]{1,0:T(8,128)(2,1)S(1)}, u32[]{:S(2)}, u32[]{:S(2)}) collective-permute-start(bf16[256,1024]{1,0:T(8,128)(2,1)S(1)} %get-tuple-element.103), channel_id=1, source_target_pairs={{0,4},{4,0},{8,12},{12,8},{1,5},{5,1},{9,13},{13,9},{2,6},{6,2},{1... | collective-permute-start | bytes 1572872 | tf_op jit(solution)/shard_map/ppermute | solution.py:438
  61.5 10.2 %collective-permute-start.11 = (bf16[256,704]{1,0:T(8,128)(2,1)S(1)}, bf16[256,704]{1,0:T(8,128)(2,1)S(1)}, u32[]{:S(2)}, u32[]{:S(2)}) collective-permute-start(bf16[256,704]{1,0:T(8,128)(2,1)S(1)} %get-tuple-element.99), channel_id=1, source_target_pairs={{4,8},{8,4},{5,9},{9,5},{6,10},{10,6},{7,11},{11,7},{20,24},{24,20... | collective-permute-start | bytes 1081352 | tf_op jit(solution)/shard_map/ppermute | solution.py:436
  66.5 16.2 %copy-start.10 = (s32[4]{0:T(128)S(1)}, s32[4]{0:T(128)}, u32[]{:S(2)}) copy-start(s32[4]{0:T(128)} %offsets_ref.1) | copy-start | bytes 52
  69.3 11.9 %collective-permute-start.13 = (bf16[256,1024]{1,0:T(8,128)(2,1)S(1)}, bf16[256,1024]{1,0:T(8,128)(2,1)S(1)}, u32[]{:S(2)}, u32[]{:S(2)}) collective-permute-start(bf16[256,1024]{1,0:T(8,128)(2,1)S(1)} %get-tuple-element.105), channel_id=1, source_target_pairs={{4,8},{8,4},{5,9},{9,5},{6,10},{10,6},{7,11},{11,7},{20,24},{24,20... | collective-permute-start | bytes 1572872 | tf_op jit(solution)/shard_map/ppermute | solution.py:436
  70.0 12.7 %collective-permute-start.14 = (bf16[256,1024]{1,0:T(8,128)(2,1)S(1)}, bf16[256,1024]{1,0:T(8,128)(2,1)S(1)}, u32[]{:S(2)}, u32[]{:S(2)}) collective-permute-start(bf16[256,1024]{1,0:T(8,128)(2,1)S(1)} %get-tuple-element.107.own), channel_id=1, source_target_pairs={{0,2},{2,0},{1,3},{3,1},{4,6},{6,4},{5,7},{7,5},{8,10},{10,8},{9,1... | collective-permute-start | bytes 1572872 | tf_op jit(solution)/shard_map/ppermute | solution.py:434
  71.7 9.5 %copy-start.7 = (bf16[256,704]{1,0:T(8,128)(2,1)}, bf16[256,704]{1,0:T(8,128)(2,1)S(1)}, u32[]{:S(2)}) copy-start(bf16[256,704]{1,0:T(8,128)(2,1)S(1)} %get-tuple-element.126.refs_0_) | copy-start | bytes 1081348
  71.7 16.3 %collective-permute-start.15 = (bf16[256,704]{1,0:T(8,128)(2,1)S(1)}, bf16[256,704]{1,0:T(8,128)(2,1)S(1)}, u32[]{:S(2)}, u32[]{:S(2)}) collective-permute-start(bf16[256,704]{1,0:T(8,128)(2,1)S(1)} %get-tuple-element.110), channel_id=1, source_target_pairs={{0,4},{4,0},{8,12},{12,8},{1,5},{5,1},{9,13},{13,9},{2,6},{6,2},{1... | collective-permute-start | bytes 1081352 | tf_op jit(solution)/shard_map/ppermute | solution.py:438
  80.5 8.4 %collective-permute-start.16 = (bf16[256,1024]{1,0:T(8,128)(2,1)S(1)}, bf16[256,1024]{1,0:T(8,128)(2,1)S(1)}, u32[]{:S(2)}, u32[]{:S(2)}) collective-permute-start(bf16[256,1024]{1,0:T(8,128)(2,1)S(1)} %get-tuple-element.112), channel_id=1, source_target_pairs={{4,8},{8,4},{5,9},{9,5},{6,10},{10,6},{7,11},{11,7},{20,24},{24,20... | collective-permute-start | bytes 1572872 | tf_op jit(solution)/shard_map/ppermute | solution.py:436
  81.4 15.9 %collective-permute-start.17 = (bf16[256,1024]{1,0:T(8,128)(2,1)S(1)}, bf16[256,1024]{1,0:T(8,128)(2,1)S(1)}, u32[]{:S(2)}, u32[]{:S(2)}) collective-permute-start(bf16[256,1024]{1,0:T(8,128)(2,1)S(1)} %get-tuple-element.115.refs_2_), channel_id=1, source_target_pairs={{4,0},{8,12},{5,1},{9,13},{6,2},{10,14},{7,3},{11,15},{20,16},{24,... | collective-permute-start | bytes 1572872 | tf_op jit(solution)/shard_map/ppermute | solution.py:437
  88.1 16.1 %collective-permute-start.18 = (bf16[256,704]{1,0:T(8,128)(2,1)S(1)}, bf16[256,704]{1,0:T(8,128)(2,1)S(1)}, u32[]{:S(2)}, u32[]{:S(2)}) collective-permute-start(bf16[256,704]{1,0:T(8,128)(2,1)S(1)} %get-tuple-element.120), channel_id=1, source_target_pairs={{4,8},{8,4},{5,9},{9,5},{6,10},{10,6},{7,11},{11,7},{20,24},{24,20... | collective-permute-start | bytes 1081352 | tf_op jit(solution)/shard_map/ppermute | solution.py:436
  89.8 21.0 %collective-permute-start.19 = (bf16[256,1024]{1,0:T(8,128)(2,1)}, bf16[256,1024]{1,0:T(8,128)(2,1)}, u32[]{:S(2)}, u32[]{:S(2)}) collective-permute-start(bf16[256,1024]{1,0:T(8,128)(2,1)} %get-tuple-element.123.refs_2_), channel_id=1, source_target_pairs={{4,0},{8,12},{5,1},{9,13},{6,2},{10,14},{7,3},{11,15},{20,16},{24,... | collective-permute-start | bytes 1572872 | tf_op jit(solution)/shard_map/ppermute | solution.py:437
  105.1 14.9 %collective-permute-start.20 = (bf16[256,704]{1,0:T(8,128)(2,1)}, bf16[256,704]{1,0:T(8,128)(2,1)}, u32[]{:S(2)}, u32[]{:S(2)}) collective-permute-start(bf16[256,704]{1,0:T(8,128)(2,1)} %get-tuple-element.127.refs_2_), channel_id=1, source_target_pairs={{4,0},{8,12},{5,1},{9,13},{6,2},{10,14},{7,3},{11,15},{20,16},{24,... | collective-permute-start | bytes 1081352 | tf_op jit(solution)/shard_map/ppermute | solution.py:437
  110.9 1.0 copy-start.6
  111.9 8.1 %copy-start.8 = (bf16[256,704]{1,0:T(8,128)(2,1)S(1)}, bf16[256,704]{1,0:T(8,128)(2,1)}, u32[]{:S(2)}) copy-start(bf16[256,704]{1,0:T(8,128)(2,1)} %copy-done.7) | copy-start | bytes 1081348
  127.0 2.1 %collective-permute-start.21 = (f32[4,16]{1,0:T(4,128)S(1)}, f32[4,16]{1,0:T(4,128)S(1)}, u32[]{:S(2)}, u32[]{:S(2)}) collective-permute-start(f32[4,16]{1,0:T(4,128)S(1)} %maximum_select_fusion), channel_id=1, source_target_pairs={{0,1},{1,0},{2,3},{3,2},{4,5},{5,4},{6,7},{7,6},{8,9},{9,8},{10,11... | collective-permute-start | bytes 776 | tf_op jit(solution)/shard_map/ppermute | solution.py:414
  127.1 3.7 %collective-permute-start.22 = (f32[4,16]{1,0:T(4,128)S(1)}, f32[4,16]{1,0:T(4,128)S(1)}, u32[]{:S(2)}, u32[]{:S(2)}) collective-permute-start(f32[4,16]{1,0:T(4,128)S(1)} %maximum_select_fusion), channel_id=1, source_target_pairs={{0,2},{1,3},{2,0},{3,1},{4,6},{5,7},{6,4},{7,5},{8,10},{9,11},{10,... | collective-permute-start | bytes 776 | tf_op jit(solution)/shard_map/ppermute | solution.py:414
  129.1 3.0 %collective-permute-start.23 = (f32[4,16]{1,0:T(4,128)S(1)}, f32[4,16]{1,0:T(4,128)S(1)}, u32[]{:S(2)}, u32[]{:S(2)}) collective-permute-start(f32[4,16]{1,0:T(4,128)S(1)} %maximum_select_fusion), channel_id=1, source_target_pairs={{0,3},{1,2},{2,1},{3,0},{4,7},{5,6},{6,5},{7,4},{8,11},{9,10},{10,... | collective-permute-start | bytes 776 | tf_op jit(solution)/shard_map/ppermute | solution.py:414
  132.1 3.6 %collective-permute-start.24 = (f32[4,16]{1,0:T(4,128)S(1)}, f32[4,16]{1,0:T(4,128)S(1)}, u32[]{:S(2)}, u32[]{:S(2)}) collective-permute-start(f32[4,16]{1,0:T(4,128)S(1)} %add_add_fusion.1), channel_id=1, source_target_pairs={{0,4},{4,0},{8,12},{12,8},{1,5},{5,1},{9,13},{13,9},{2,6},{6,2},{1... | collective-permute-start | bytes 776 | tf_op jit(solution)/shard_map/ppermute | solution.py:410
  135.7 4.5 %collective-permute-start.25 = (f32[4,16]{1,0:T(4,128)S(1)}, f32[4,16]{1,0:T(4,128)S(1)}, u32[]{:S(2)}, u32[]{:S(2)}) collective-permute-start(f32[4,16]{1,0:T(4,128)S(1)} %add.38), channel_id=1, source_target_pairs={{0,8},{4,12},{8,0},{12,4},{1,9},{5,13},{9,1},{13,5},{2,10},{6,14},... | collective-permute-start | bytes 776 | tf_op jit(solution)/shard_map/ppermute | solution.py:410

commit v5 on v4

--- a/solution.py
+++ b/solution.py
@@ -46,20 +46,33 @@
     return functools.reduce(lambda a, b: a + b, values)
 
 
+def padded(width):
+    return -(-width // 128) * 128
+
+
+def clear_tail(ref, width, value):
+    if width < ref.shape[1]:
+        ref[:, ref.shape[1] - 128 :] = jnp.full((ref.shape[0], 128), value, ref.dtype)
+
+
 def column_tiles(width):
     return [(start, min(TILE, width - start)) for start in range(0, width, TILE)]
 
 
-def basis_copies(basis_hbm, basis_ref, sems, first):
+def basis_copies(basis_hbm, basis_ref, sems, first, width, ragged_ref=None):
     depth = basis_hbm.shape[0]
     upper = depth // 32 * 16
     copies = []
-    for n, (start, size) in enumerate(column_tiles(basis_ref.shape[1])):
+    for n, (start, size) in enumerate(column_tiles(width)):
         copies.append(
             [
                 pltpu.make_async_copy(
                     basis_hbm.at[top : top + rows, first + start : first + start + size],
-                    basis_ref.at[top : top + rows, start : start + size],
+                    (
+                        ragged_ref.at[top : top + rows, :]
+                        if size % 128
+                        else basis_ref.at[top : top + rows, start : start + size]
+                    ),
                     sems.at[n, half],
                 )
                 for half, (top, rows) in enumerate(((0, upper), (upper, depth - upper)))
@@ -78,9 +91,12 @@
         rows_ref, basis_hbm, wide_ref, send_ref, done_ref = refs[:5]
         scratch = refs[5:]
     basis_ref, sems = scratch[:2]
-    copies = basis_copies(basis_hbm, basis_ref, sems, first)
+    ragged_ref = scratch[-1]
+    width = wide_ref.shape[1]
+    clear_tail(basis_ref, width, 0)
+    copies = basis_copies(basis_hbm, basis_ref, sems, first, width, ragged_ref)
     if terms == 1:
-        taken, row_sems = scratch[2:]
+        taken, row_sems = scratch[2:4]
         row_copies = [
             pltpu.make_async_copy(a, taken.at[n], row_sems.at[n]) for n, a in enumerate(arrays)
         ]
@@ -102,12 +118,16 @@
         for pair in copies[1:]:
             for copy in pair:
                 copy.start()
-    for pair, (start, size) in zip(copies, column_tiles(basis_ref.shape[1])):
+    for pair, (start, size) in zip(copies, column_tiles(width)):
         for copy in pair:
             copy.wait()
+        if size % 128:
+            basis_ref[:, start : start + size] = ragged_ref[...]
         product = jnp.dot(
-            rows_ref[...], basis_ref[:, start : start + size], preferred_element_type=F32
-        )
+            rows_ref[...],
+            basis_ref[:, start : start + padded(size)],
+            preferred_element_type=F32,
+        )[:, :size]
         wide_ref[:, start : start + size] = product
         send_ref[:, start : start + size] = product.astype(send_ref.dtype)
     done_ref[...] = jnp.zeros_like(done_ref)
@@ -116,7 +136,7 @@
 def project(order, inputs, basis, start, width):
     depth = basis.shape[0]
     tiles = len(column_tiles(width))
-    scratch = [pltpu.VMEM((depth, width), basis.dtype), pltpu.SemaphoreType.DMA((tiles, 2))]
+    scratch = [pltpu.VMEM((depth, padded(width)), basis.dtype), pltpu.SemaphoreType.DMA((tiles, 2))]
     if isinstance(inputs, tuple):
         terms = len(inputs[0])
         arrays = list(inputs[0]) + list(inputs[1])
@@ -132,6 +152,9 @@
         arrays = [inputs]
         rows = inputs.shape[0]
         specs = [VMEM]
+    ragged = column_tiles(width)[-1][1]
+    if ragged % 128:
+        scratch.append(pltpu.VMEM((depth, ragged), basis.dtype))
     out_shape = [
         jax.ShapeDtypeStruct((rows, width), F32),
         jax.ShapeDtypeStruct((rows, width), BF16),
@@ -155,7 +178,7 @@
 
 def act_kernel(order_ref, cand_ref, query_ref, basis_hbm, share_ref, done_ref, basis_ref, sems):
     del order_ref
-    copies = basis_copies(basis_hbm, basis_ref, sems, 0)
+    copies = basis_copies(basis_hbm, basis_ref, sems, 0, share_ref.shape[1])
     for pair in copies:
         for copy in pair:
             copy.start()
@@ -328,7 +351,7 @@
     per_block = 2 if pick else 1
     parts = refs[: blocks * per_block]
     (
-        eig_hbm, split_ref, query_act_ref, out_ref, done_ref, eig_ref, weights_ref, sems
+        eig_hbm, split_ref, query_act_ref, out_ref, done_ref, eig_ref, weights_ref, sums_ref, sems
     ) = refs[blocks * per_block :]
     width = parts[0].shape[1]
     features = eig_ref.shape[1]
@@ -341,17 +364,22 @@
         )
         for n, (start, rows) in enumerate(row_pieces(width))
     ]
+    span = eig_ref.shape[0]
+    if width < span:
+        eig_ref[width:] = jnp.ones((span - width, features), F32)
     for copy in copies:
         copy.start()
-    sums = []
+    clear_tail(sums_ref, width, 0)
+    query_rows = parts[0].shape[0] - cand_rows
     for b in range(blocks):
-        here = parts[b * per_block]
+        total = parts[b * per_block][...]
         if pick:
-            sums.append(jnp.where(is_inner(), here[...], parts[b * per_block + 1][...]))
-        else:
-            sums.append(here[...])
-    cand = jnp.concatenate([s[:cand_rows] for s in sums], 0).T
-    query = jnp.concatenate([s[cand_rows:] for s in sums], 0).T.astype(F32)
+            total = jnp.where(is_inner(), total, parts[b * per_block + 1][...])
+        sums_ref[b * cand_rows : (b + 1) * cand_rows, :width] = total[:cand_rows]
+        place = blocks * cand_rows + b * query_rows
+        sums_ref[place : place + query_rows, :width] = total[cand_rows:]
+    cand = sums_ref[: blocks * cand_rows, :].T
+    query = sums_ref[blocks * cand_rows :, :].T.astype(F32)
 
     def outer_of(k):
         return jnp.dot(
@@ -367,7 +395,7 @@
     for k in range(examples):
         if k > 0:
             outer = outer_of(k)
-        weights_ref[k * width : (k + 1) * width, :] = (outer * eig_ref[...]).astype(BF16)
+        weights_ref[k * span : (k + 1) * span, :] = (outer * eig_ref[...]).astype(BF16)
     image = lax.dot_general(
         weights_ref[...],
         query_act_ref[...],
@@ -376,7 +404,7 @@
     )
     for k in range(examples):
         out_ref[k : k + 1, :] = jnp.sum(
-            image[k * width : (k + 1) * width] * query, axis=0, keepdims=True
+            image[k * span : (k + 1) * span] * query, axis=0, keepdims=True
         )
     done_ref[...] = jnp.zeros_like(done_ref)
 
@@ -391,11 +419,12 @@
         out_specs=[VMEM, VMEM],
         out_shape=[jax.ShapeDtypeStruct((examples, query_acts.shape[0]), F32), ORDER],
         scratch_shapes=[
-            pltpu.VMEM((width, features), F32),
-            pltpu.VMEM((examples * width, features), BF16),
+            pltpu.VMEM((padded(width), features), F32),
+            pltpu.VMEM((examples * padded(width), features), BF16),
+            pltpu.VMEM((len(blocks) * parts[0].shape[0], padded(width)), BF16),
             pltpu.SemaphoreType.DMA((len(row_pieces(width)),)),
         ],
-        compiler_params=params(42),
+        compiler_params=params(36),
         cost_estimate=QUICK,
         name="score",
     )(order, *parts, eigvals, split, query_acts)

time: 141 us -> 142 us (level)
  no operation moved by 1% of the time
where the time goes in v5:
time: 142 us; the launch traced here: 141 us
  Pallas kernels  54.6 us (38%)
  starting transfers between devices  43.4 us (31%)
  waiting for transfers between devices  36.9 us (26%)
  local copies, waits for them, and re-layouts  5.03 us (4%)
    pallas_call x6, Pallas kernels, project(): pl.pallas_call(functools.partial(project_kernel, terms, start), in_specs=...  26.6 us
    pallas_call x3, Pallas kernels, score_chunk(): pl.pallas_call(functools.partial(score_kernel, len(blocks), pick, cand_ro...  22.1 us
    ppermute x3, starting transfers between devices, token_scores_paired(): inward = lambda a: lax.ppermute(a, 'hid', [(0, 1), (3, 2)])  12.2 us
    ppermute x3, waiting for transfers between devices, token_scores_paired(): beside = lambda a: lax.ppermute(a, 'hid', [(0, 1), (1, 0), (2, 3), (3, 2)])  11.3 us
    ppermute x3, waiting for transfers between devices, token_scores_paired(): outward = lambda a: lax.ppermute(a, 'hid', [(1, 0), (2, 3)])  10.4 us
    ppermute x5, waiting for transfers between devices, small_sum(): lax.ppermute(value, axes, [(i, i ^ other) for i in range(size)])  8.07 us
    ppermute x3, waiting for transfers between devices, token_scores_paired(): inward = lambda a: lax.ppermute(a, 'hid', [(0, 1), (3, 2)])  7.08 us
    ppermute x3, starting transfers between devices, token_scores_paired(): beside = lambda a: lax.ppermute(a, 'hid', [(0, 1), (1, 0), (2, 3), (3, 2)])  6.83 us
  transfers between devices with their start and end apart: 26, of which 11 were waited for; matrix products, arithmetic and copies ran while one was open for 0% of the time, Pallas kernels for 34%

profile of v5, /device:TPU:0, one launch (start us, length us, event | category | flops | bytes accessed | tf_op | source)
XLA Modules:
  0.0 141.2 jit_solution(2978902647845094553)
XLA Ops:
  0.0 4.8 %collective-permute-start = (bf16[128,2752]{0,1:T(8,128)(2,1)}, bf16[128,2752]{0,1:T(8,128)(2,1)S(1)}, u32[]{:S(2)}, u32[]{:S(2)}) collective-permute-start(bf16[128,2752]{0,1:T(8,128)(2,1)} %param.10), channel_id=1, source_target_pairs={{0,2},{2,0},{4,6},{6,4},{8,10},{10,8},{12,14},{14,12},{16,18},{18,... | collective-permute-start | bytes 2113544 | tf_op jit(solution)/shard_map/ppermute | solution.py:469
  4.8 0.7 collective-permute-start.1
  6.2 6.2 %project.6 = (f32[256,1024]{1,0:T(8,128)}, bf16[256,1024]{1,0:T(8,128)(2,1)}, bf16[256,2752]{1,0:T(8,128)(2,1)}, f32[8,128]{1,0:T(8,128)}) custom-call(f32[8,128]{1,0:T(8,128)} %broadcast_in_dim.9.order_ref, bf16[2752,128]{1,0:T(8,128)(2,1)} %bitcast.10, bf16[2752,128]{1,0:T(8,128)(2,1)} %bitcast.11, bf16[2752,2752]{1,0:T(8,128)(2,1)} %refs_1_.7), custom_call_target="tpu_custom_call" | custom-call | flops 1024 | bytes 1024 | tf_op jit(solution)/shard_map/project/pallas_call | solution.py:164
  12.4 3.5 %collective-permute-start.2 = (bf16[256,1024]{1,0:T(8,128)(2,1)}, bf16[256,1024]{1,0:T(8,128)(2,1)S(1)}, u32[]{:S(2)}, u32[]{:S(2)}) collective-permute-start(bf16[256,1024]{1,0:T(8,128)(2,1)} %get-tuple-element.73), channel_id=1, source_target_pairs={{0,4},{12,8},{1,5},{13,9},{2,6},{14,10},{3,7},{15,11},{16,20},{28,... | collective-permute-start | bytes 1572872 | tf_op jit(solution)/shard_map/ppermute | solution.py:464
  15.9 1.4 copy-done
  17.9 3.8 %project.7 = (f32[256,1024]{1,0:T(8,128)S(1)}, bf16[256,1024]{1,0:T(8,128)(2,1)S(1)}, f32[8,128]{1,0:T(8,128)S(1)}) custom-call(f32[8,128]{1,0:T(8,128)S(1)} %copy-done.9, bf16[256,2752]{1,0:T(8,128)(2,1)S(1)} %copy-done, bf16[2752,2752]{1,0:T(8,128)(2,1)} %refs_1_.7), custom_call_target="tpu_custom_call" | custom-call | flops 1024 | bytes 1024 | tf_op jit(solution)/shard_map/project/pallas_call | solution.py:164
  22.1 2.1 %acts.1 = (f32[256,1024]{1,0:T(8,128)S(1)}, f32[8,128]{1,0:T(8,128)S(1)}) custom-call(f32[8,128]{1,0:T(8,128)S(1)} %get-tuple-element.69.order_ref, bf16[128,2048]{1,0:T(8,128)(2,1)S(1)} %copy-done.3, bf16[128,2048]{1,0:T(8,128)(2,1)S(1)} %copy-done.4, bf16[2048,1024]{1,0:T(8,128)(2,1)S(1)} %copy-done.2), custom_call_target="tpu_custom_call" | custom-call | flops 1024 | bytes 1024 | tf_op jit(solution)/shard_map/acts/pallas_call | solution.py:197
  24.2 1.3 collective-permute-start.4
  25.6 1.3 collective-permute-start.5
  26.9 1.5 %collective-permute-start.3 = (bf16[256,1024]{1,0:T(8,128)(2,1)S(1)}, bf16[256,1024]{1,0:T(8,128)(2,1)S(1)}, u32[]{:S(2)}, u32[]{:S(2)}) collective-permute-start(bf16[256,1024]{1,0:T(8,128)(2,1)S(1)} %get-tuple-element.77), channel_id=1, source_target_pairs={{0,4},{12,8},{1,5},{13,9},{2,6},{14,10},{3,7},{15,11},{16,20},{28,... | collective-permute-start | bytes 1572872 | tf_op jit(solution)/shard_map/ppermute | solution.py:464
  28.3 1.1 collective-permute-start.9
  29.5 0.7 collective-permute-start.6
  30.2 4.9 %project.8 = (f32[256,704]{1,0:T(8,128)S(1)}, bf16[256,704]{1,0:T(8,128)(2,1)}, f32[8,128]{1,0:T(8,128)S(1)}) custom-call(f32[8,128]{1,0:T(8,128)S(1)} %get-tuple-element.74.order_ref, bf16[256,2752]{1,0:T(8,128)(2,1)S(1)} %copy-done, bf16[2752,2752]{1,0:T(8,128)(2,1)} %refs_1_.7), custom_call_target="tpu_custom_call" | custom-call | flops 1024 | bytes 1024 | tf_op jit(solution)/shard_map/project/pallas_call | solution.py:164
  35.2 5.1 %collective-permute-done.3.refs_1_.in_ref = bf16[256,1024]{1,0:T(8,128)(2,1)S(1)} collective-permute-done((bf16[256,1024]{1,0:T(8,128)(2,1)S(1)}, bf16[256,1024]{1,0:T(8,128)(2,1)S(1)}, u32[]{:S(2)}, u32[]{:S(2)}) %collective-permute-start.3) | collective-permute-done | bytes 524320 | tf_op jit(solution)/shard_map/ppermute | solution.py:464
  40.4 0.7 collective-permute-start.8
  41.1 7.2 %collective-permute-start.7 = (bf16[256,704]{1,0:T(8,128)(2,1)}, bf16[256,704]{1,0:T(8,128)(2,1)S(1)}, u32[]{:S(2)}, u32[]{:S(2)}) collective-permute-start(bf16[256,704]{1,0:T(8,128)(2,1)} %get-tuple-element.88), channel_id=1, source_target_pairs={{0,4},{12,8},{1,5},{13,9},{2,6},{14,10},{3,7},{15,11},{16,20},{28,... | collective-permute-start | bytes 1081352 | tf_op jit(solution)/shard_map/ppermute | solution.py:464
  48.3 3.9 %project.9 = (f32[256,1024]{1,0:T(8,128)S(1)}, bf16[256,1024]{1,0:T(8,128)(2,1)S(1)}, bf16[256,2752]{1,0:T(8,128)(2,1)S(1)}, f32[8,128]{1,0:T(8,128)S(1)}) custom-call(f32[8,128]{1,0:T(8,128)S(1)} %get-tuple-element.78.order_ref, bf16[2752,128]{1,0:T(8,128)(2,1)S(1)} %get-tuple-element.79.refs_0_, bf16[2752,128]{1,0:T(8,128)(2,1)S(1)} %collective-permute-done.4.refs_1_, ...), custom_call_target="tpu_custom_call" | custom-call | flops 1024 | bytes 1024 | tf_op jit(solution)/shard_map/project/pallas_call | solution.py:164
  52.4 3.7 %project.10 = (f32[256,1024]{1,0:T(8,128)S(1)}, bf16[256,1024]{1,0:T(8,128)(2,1)S(1)}, f32[8,128]{1,0:T(8,128)S(1)}) custom-call(f32[8,128]{1,0:T(8,128)S(1)} %get-tuple-element.84.order_ref, bf16[256,2752]{1,0:T(8,128)(2,1)S(1)} %get-tuple-element.85.refs_0_, bf16[2752,2752]{1,0:T(8,128)(2,1)} %refs_1_.7), custom_call_target="tpu_custom_call" | custom-call | flops 1024 | bytes 1024 | tf_op jit(solution)/shard_map/project/pallas_call | solution.py:164
  56.1 2.0 %collective-permute-done.7.refs_1_.in_ref = bf16[256,704]{1,0:T(8,128)(2,1)S(1)} collective-permute-done((bf16[256,704]{1,0:T(8,128)(2,1)}, bf16[256,704]{1,0:T(8,128)(2,1)S(1)}, u32[]{:S(2)}, u32[]{:S(2)}) %collective-permute-start.7) | collective-permute-done | bytes 360480 | tf_op jit(solution)/shard_map/ppermute | solution.py:464
  58.2 0.8 copy-done.5
  59.0 2.5 %collective-permute-start.12 = (bf16[256,1024]{1,0:T(8,128)(2,1)S(1)}, bf16[256,1024]{1,0:T(8,128)(2,1)S(1)}, u32[]{:S(2)}, u32[]{:S(2)}) collective-permute-start(bf16[256,1024]{1,0:T(8,128)(2,1)S(1)} %get-tuple-element.103), channel_id=1, source_target_pairs={{0,4},{4,0},{8,12},{12,8},{1,5},{5,1},{9,13},{13,9},{2,6},{6,2},{1... | collective-permute-start | bytes 1572872 | tf_op jit(solution)/shard_map/ppermute | solution.py:467
  61.5 0.9 collective-permute-start.11
  62.6 4.2 %project.11 = (f32[256,704]{1,0:T(8,128)S(1)}, bf16[256,704]{1,0:T(8,128)(2,1)S(1)}, f32[8,128]{1,0:T(8,128)S(1)}) custom-call(f32[8,128]{1,0:T(8,128)S(1)} %get-tuple-element.94.order_ref, bf16[256,2752]{1,0:T(8,128)(2,1)S(1)} %get-tuple-element.85.refs_0_, bf16[2752,2752]{1,0:T(8,128)(2,1)} %refs_1_.7), custom_call_target="tpu_custom_call" | custom-call | flops 1024 | bytes 1024 | tf_op jit(solution)/shard_map/project/pallas_call | solution.py:164
  66.8 2.3 %collective-permute-done.10.refs_1_ = bf16[256,1024]{1,0:T(8,128)(2,1)S(1)} collective-permute-done((bf16[256,1024]{1,0:T(8,128)(2,1)S(1)}, bf16[256,1024]{1,0:T(8,128)(2,1)S(1)}, u32[]{:S(2)}, u32[]{:S(2)}) %collective-permute-start.10) | collective-permute-done | bytes 524320 | tf_op jit(solution)/shard_map/ppermute | solution.py:467
  69.3 0.7 collective-permute-start.13
  70.0 1.7 %collective-permute-start.14 = (bf16[256,1024]{1,0:T(8,128)(2,1)S(1)}, bf16[256,1024]{1,0:T(8,128)(2,1)S(1)}, u32[]{:S(2)}, u32[]{:S(2)}) collective-permute-start(bf16[256,1024]{1,0:T(8,128)(2,1)S(1)} %get-tuple-element.107.own), channel_id=1, source_target_pairs={{0,2},{2,0},{1,3},{3,1},{4,6},{6,4},{5,7},{7,5},{8,10},{10,8},{9,1... | collective-permute-start | bytes 1572872 | tf_op jit(solution)/shard_map/ppermute | solution.py:463
  71.7 4.3 %collective-permute-start.15 = (bf16[256,704]{1,0:T(8,128)(2,1)S(1)}, bf16[256,704]{1,0:T(8,128)(2,1)S(1)}, u32[]{:S(2)}, u32[]{:S(2)}) collective-permute-start(bf16[256,704]{1,0:T(8,128)(2,1)S(1)} %get-tuple-element.110), channel_id=1, source_target_pairs={{0,4},{4,0},{8,12},{12,8},{1,5},{5,1},{9,13},{13,9},{2,6},{6,2},{1... | collective-permute-start | bytes 1081352 | tf_op jit(solution)/shard_map/ppermute | solution.py:467
  76.0 4.4 %collective-permute-done.12.refs_1_ = bf16[256,1024]{1,0:T(8,128)(2,1)S(1)} collective-permute-done((bf16[256,1024]{1,0:T(8,128)(2,1)S(1)}, bf16[256,1024]{1,0:T(8,128)(2,1)S(1)}, u32[]{:S(2)}, u32[]{:S(2)}) %collective-permute-start.12) | collective-permute-done | bytes 524320 | tf_op jit(solution)/shard_map/ppermute | solution.py:467
  81.4 1.3 collective-permute-start.17
  82.7 0.8 split_acts.1
  83.5 4.6 %collective-permute-done.15.refs_1_ = bf16[256,704]{1,0:T(8,128)(2,1)S(1)} collective-permute-done((bf16[256,704]{1,0:T(8,128)(2,1)S(1)}, bf16[256,704]{1,0:T(8,128)(2,1)S(1)}, u32[]{:S(2)}, u32[]{:S(2)}) %collective-permute-start.15) | collective-permute-done | bytes 360480 | tf_op jit(solution)/shard_map/ppermute | solution.py:467
  88.9 1.0 add.53
  89.8 1.3 collective-permute-start.19
  91.1 6.1 %collective-permute-done.17.refs_3_ = bf16[256,1024]{1,0:T(8,128)(2,1)S(1)} collective-permute-done((bf16[256,1024]{1,0:T(8,128)(2,1)S(1)}, bf16[256,1024]{1,0:T(8,128)(2,1)S(1)}, u32[]{:S(2)}, u32[]{:S(2)}) %collective-permute-start.17) | collective-permute-done | bytes 524320 | tf_op jit(solution)/shard_map/ppermute | solution.py:466
  97.3 6.9 %score.3 = (f32[4,256]{1,0:T(4,128)S(1)}, f32[8,128]{1,0:T(8,128)S(1)}) custom-call(f32[8,128]{1,0:T(8,128)S(1)} %get-tuple-element.113.order_ref, bf16[256,1024]{1,0:T(8,128)(2,1)S(1)} %get-tuple-element.114.refs_0_, bf16[256,1024]{1,0:T(8,128)(2,1)S(1)} %collective-permute-done.10.refs_1_, bf16[256,1024]{1,0:T(8,128)(2,1)S(1)} %get-tuple-element.115.refs_2_, ...), custom_call_target="tpu_custom_call" | custom-call | flops 1024 | bytes 1024 | tf_op jit(solution)/shard_map/score/pallas_call | solution.py:416
  104.2 0.9 add.54
  105.1 1.5 %collective-permute-start.20 = (bf16[256,704]{1,0:T(8,128)(2,1)}, bf16[256,704]{1,0:T(8,128)(2,1)}, u32[]{:S(2)}, u32[]{:S(2)}) collective-permute-start(bf16[256,704]{1,0:T(8,128)(2,1)} %get-tuple-element.127.refs_2_), channel_id=1, source_target_pairs={{4,0},{8,12},{5,1},{9,13},{6,2},{10,14},{7,3},{11,15},{20,16},{24,... | collective-permute-start | bytes 1081352 | tf_op jit(solution)/shard_map/ppermute | solution.py:466
  106.6 4.2 %collective-permute-done.19.refs_3_ = bf16[256,1024]{1,0:T(8,128)(2,1)} collective-permute-done((bf16[256,1024]{1,0:T(8,128)(2,1)}, bf16[256,1024]{1,0:T(8,128)(2,1)}, u32[]{:S(2)}, u32[]{:S(2)}) %collective-permute-start.19) | collective-permute-done | bytes 524320 | tf_op jit(solution)/shard_map/ppermute | solution.py:466
  110.9 1.0 copy-done.6
  111.9 8.1 %score.4 = (f32[4,256]{1,0:T(4,128)S(1)}, f32[8,128]{1,0:T(8,128)S(1)}) custom-call(f32[8,128]{1,0:T(8,128)S(1)} %get-tuple-element.121.order_ref, bf16[256,1024]{1,0:T(8,128)(2,1)S(1)} %copy-done.6, bf16[256,1024]{1,0:T(8,128)(2,1)S(1)} %collective-permute-done.12.refs_1_, bf16[256,1024]{1,0:T(8,128)(2,1)} %get-tuple-element.123.refs_2_, ...), custom_call_target="tpu_custom_call" | custom-call | flops 1024 | bytes 1024 | tf_op jit(solution)/shard_map/score/pallas_call | solution.py:416
  120.0 7.1 %score.5 = (f32[4,256]{1,0:T(4,128)S(1)}, f32[8,128]{1,0:T(8,128)}) custom-call(f32[8,128]{1,0:T(8,128)S(1)} %get-tuple-element.125.order_ref, bf16[256,704]{1,0:T(8,128)(2,1)S(1)} %copy-done.8, bf16[256,704]{1,0:T(8,128)(2,1)S(1)} %collective-permute-done.15.refs_1_, bf16[256,704]{1,0:T(8,128)(2,1)} %get-tuple-element.127.refs_2_, ...), custom_call_target="tpu_custom_call" | custom-call | flops 1024 | bytes 1024 | tf_op jit(solution)/shard_map/score/pallas_call | solution.py:416
  127.5 2.0 %collective-permute-start.22 = (f32[4,16]{1,0:T(4,128)S(1)}, f32[4,16]{1,0:T(4,128)S(1)}, u32[]{:S(2)}, u32[]{:S(2)}) collective-permute-start(f32[4,16]{1,0:T(4,128)S(1)} %maximum_select_fusion), channel_id=1, source_target_pairs={{0,2},{1,3},{2,0},{3,1},{4,6},{5,7},{6,4},{7,5},{8,10},{9,11},{10,... | collective-permute-start | bytes 776 | tf_op jit(solution)/shard_map/ppermute | solution.py:443
  129.6 1.5 %collective-permute-done.22 = f32[4,16]{1,0:T(4,128)S(1)} collective-permute-done((f32[4,16]{1,0:T(4,128)S(1)}, f32[4,16]{1,0:T(4,128)S(1)}, u32[]{:S(2)}, u32[]{:S(2)}) %collective-permute-start.22) | collective-permute-done | bytes 288 | tf_op jit(solution)/shard_map/ppermute | solution.py:443
  131.1 1.4 collective-permute-done.23
  132.5 1.5 %collective-permute-start.24 = (f32[4,16]{1,0:T(4,128)S(1)}, f32[4,16]{1,0:T(4,128)S(1)}, u32[]{:S(2)}, u32[]{:S(2)}) collective-permute-start(f32[4,16]{1,0:T(4,128)S(1)} %add_add_fusion.1), channel_id=1, source_target_pairs={{0,4},{4,0},{8,12},{12,8},{1,5},{5,1},{9,13},{13,9},{2,6},{6,2},{1... | collective-permute-start | bytes 776 | tf_op jit(solution)/shard_map/ppermute | solution.py:439
  134.0 2.1 %collective-permute-done.24 = f32[4,16]{1,0:T(4,128)S(1)} collective-permute-done((f32[4,16]{1,0:T(4,128)S(1)}, f32[4,16]{1,0:T(4,128)S(1)}, u32[]{:S(2)}, u32[]{:S(2)}) %collective-permute-start.24) | collective-permute-done | bytes 288 | tf_op jit(solution)/shard_map/ppermute | solution.py:439
  136.1 1.4 collective-permute-start.25
  137.5 3.1 %collective-permute-done.25 = f32[4,16]{1,0:T(4,128)S(1)} collective-permute-done((f32[4,16]{1,0:T(4,128)S(1)}, f32[4,16]{1,0:T(4,128)S(1)}, u32[]{:S(2)}, u32[]{:S(2)}) %collective-permute-start.25) | collective-permute-done | bytes 288 | tf_op jit(solution)/shard_map/ppermute | solution.py:439
  (65 shorter events, 5.4 us)
Async XLA Ops:
  0.0 24.2 %collective-permute-start = (bf16[128,2752]{0,1:T(8,128)(2,1)}, bf16[128,2752]{0,1:T(8,128)(2,1)S(1)}, u32[]{:S(2)}, u32[]{:S(2)}) collective-permute-start(bf16[128,2752]{0,1:T(8,128)(2,1)} %param.10), channel_id=1, source_target_pairs={{0,2},{2,0},{4,6},{6,4},{8,10},{10,8},{12,14},{14,12},{16,18},{18,... | collective-permute-start | bytes 2113544 | tf_op jit(solution)/shard_map/ppermute | solution.py:469
  4.8 19.4 %collective-permute-start.1 = (bf16[128,2752]{0,1:T(8,128)(2,1)}, bf16[128,2752]{0,1:T(8,128)(2,1)S(1)}, u32[]{:S(2)}, u32[]{:S(2)}) collective-permute-start(bf16[128,2752]{0,1:T(8,128)(2,1)} %param.11), channel_id=1, source_target_pairs={{1,3},{3,1},{5,7},{7,5},{9,11},{11,9},{13,15},{15,13},{17,19},{19,... | collective-permute-start | bytes 2113544 | tf_op jit(solution)/shard_map/ppermute | solution.py:470
  12.4 17.1 %collective-permute-start.2 = (bf16[256,1024]{1,0:T(8,128)(2,1)}, bf16[256,1024]{1,0:T(8,128)(2,1)S(1)}, u32[]{:S(2)}, u32[]{:S(2)}) collective-permute-start(bf16[256,1024]{1,0:T(8,128)(2,1)} %get-tuple-element.73), channel_id=1, source_target_pairs={{0,4},{12,8},{1,5},{13,9},{2,6},{14,10},{3,7},{15,11},{16,20},{28,... | collective-permute-start | bytes 1572872 | tf_op jit(solution)/shard_map/ppermute | solution.py:464
  15.9 1.4 copy-start
  17.2 0.7 copy-start.9
  17.9 3.9 %copy-start.2 = (bf16[2048,1024]{1,0:T(8,128)(2,1)S(1)}, bf16[2048,1024]{1,0:T(8,128)(2,1)}, u32[]{:S(2)}) copy-start(bf16[2048,1024]{1,0:T(8,128)(2,1)} %basis_hbm.1) | copy-start | bytes 12582916
  17.9 4.0 %copy-start.3 = (bf16[128,2048]{1,0:T(8,128)(2,1)S(1)}, bf16[128,2048]{1,0:T(8,128)(2,1)}, u32[]{:S(2)}) copy-start(bf16[128,2048]{1,0:T(8,128)(2,1)} %cand_ref.1) | copy-start | bytes 1572868
  17.9 4.2 %copy-start.4 = (bf16[128,2048]{1,0:T(8,128)(2,1)S(1)}, bf16[128,2048]{1,0:T(8,128)(2,1)}, u32[]{:S(2)}) copy-start(bf16[128,2048]{1,0:T(8,128)(2,1)} %query_ref.1) | copy-start | bytes 1572868
  21.7 7.7 %copy-start.1 = (f32[256,1024]{1,0:T(8,128)S(1)}, f32[256,1024]{1,0:T(8,128)}, u32[]{:S(2)}) copy-start(f32[256,1024]{1,0:T(8,128)} %get-tuple-element.72.refs_0_.wide_ref) | copy-start | bytes 3145732
  24.2 16.8 %collective-permute-start.4 = (bf16[2752,128]{1,0:T(8,128)(2,1)S(1)}, bf16[2752,128]{1,0:T(8,128)(2,1)S(1)}, u32[]{:S(2)}, u32[]{:S(2)}) collective-permute-start(bf16[2752,128]{1,0:T(8,128)(2,1)S(1)} %get-tuple-element.79.refs_0_), channel_id=1, source_target_pairs={{0,1},{2,3},{4,5},{6,7},{8,9},{10,11},{12,13},{14,15},{16,17},{18,... | collective-permute-start | bytes 2113544 | tf_op jit(solution)/shard_map/ppermute | solution.py:487
  25.6 22.7 %collective-permute-start.5 = (bf16[2752,128]{1,0:T(8,128)(2,1)S(1)}, bf16[2752,128]{1,0:T(8,128)(2,1)S(1)}, u32[]{:S(2)}, u32[]{:S(2)}) collective-permute-start(bf16[2752,128]{1,0:T(8,128)(2,1)S(1)} %get-tuple-element.80.refs_2_), channel_id=1, source_target_pairs={{1,0},{3,2},{5,4},{7,6},{9,8},{11,10},{13,12},{15,14},{17,16},{19,... | collective-permute-start | bytes 2113544 | tf_op jit(solution)/shard_map/ppermute | solution.py:488
  26.9 13.4 %collective-permute-start.3 = (bf16[256,1024]{1,0:T(8,128)(2,1)S(1)}, bf16[256,1024]{1,0:T(8,128)(2,1)S(1)}, u32[]{:S(2)}, u32[]{:S(2)}) collective-permute-start(bf16[256,1024]{1,0:T(8,128)(2,1)S(1)} %get-tuple-element.77), channel_id=1, source_target_pairs={{0,4},{12,8},{1,5},{13,9},{2,6},{14,10},{3,7},{15,11},{16,20},{28,... | collective-permute-start | bytes 1572872 | tf_op jit(solution)/shard_map/ppermute | solution.py:464
  28.3 34.0 %collective-permute-start.9 = (f32[256,1024]{1,0:T(8,128)S(1)}, f32[256,1024]{1,0:T(8,128)S(1)}, u32[]{:S(2)}, u32[]{:S(2)}) collective-permute-start(f32[256,1024]{1,0:T(8,128)S(1)} %get-tuple-element.93.share_ref), channel_id=1, source_target_pairs={{0,1},{1,0},{2,3},{3,2},{4,5},{5,4},{6,7},{7,6},{8,9},{9,8},{10,11... | collective-permute-start | bytes 3145736 | tf_op jit(solution)/shard_map/ppermute | solution.py:463
  29.5 22.6 %collective-permute-start.6 = (bf16[256,1024]{1,0:T(8,128)(2,1)S(1)}, bf16[256,1024]{1,0:T(8,128)(2,1)S(1)}, u32[]{:S(2)}, u32[]{:S(2)}) collective-permute-start(bf16[256,1024]{1,0:T(8,128)(2,1)S(1)} %get-tuple-element.82), channel_id=1, source_target_pairs={{4,8},{8,4},{5,9},{9,5},{6,10},{10,6},{7,11},{11,7},{20,24},{24,20... | collective-permute-start | bytes 1572872 | tf_op jit(solution)/shard_map/ppermute | solution.py:465
  40.4 17.7 %collective-permute-start.8 = (bf16[256,1024]{1,0:T(8,128)(2,1)S(1)}, bf16[256,1024]{1,0:T(8,128)(2,1)S(1)}, u32[]{:S(2)}, u32[]{:S(2)}) collective-permute-start(bf16[256,1024]{1,0:T(8,128)(2,1)S(1)} %get-tuple-element.90), channel_id=1, source_target_pairs={{4,8},{8,4},{5,9},{9,5},{6,10},{10,6},{7,11},{11,7},{20,24},{24,20... | collective-permute-start | bytes 1572872 | tf_op jit(solution)/shard_map/ppermute | solution.py:465
  41.1 17.0 %collective-permute-start.7 = (bf16[256,704]{1,0:T(8,128)(2,1)}, bf16[256,704]{1,0:T(8,128)(2,1)S(1)}, u32[]{:S(2)}, u32[]{:S(2)}) collective-permute-start(bf16[256,704]{1,0:T(8,128)(2,1)} %get-tuple-element.88), channel_id=1, source_target_pairs={{0,4},{12,8},{1,5},{13,9},{2,6},{14,10},{3,7},{15,11},{16,20},{28,... | collective-permute-start | bytes 1081352 | tf_op jit(solution)/shard_map/ppermute | solution.py:464
  52.3 16.9 %collective-permute-start.10 = (bf16[256,1024]{1,0:T(8,128)(2,1)S(1)}, bf16[256,1024]{1,0:T(8,128)(2,1)S(1)}, u32[]{:S(2)}, u32[]{:S(2)}) collective-permute-start(bf16[256,1024]{1,0:T(8,128)(2,1)S(1)} %get-tuple-element.97), channel_id=1, source_target_pairs={{0,4},{4,0},{8,12},{12,8},{1,5},{5,1},{9,13},{13,9},{2,6},{6,2},{1... | collective-permute-start | bytes 1572872 | tf_op jit(solution)/shard_map/ppermute | solution.py:467
  52.3 10.0 %copy-start.11 = (s32[128]{0:T(128)S(1)}, s32[128]{0:T(128)}, u32[]{:S(2)}) copy-start(s32[128]{0:T(128)} %param.14) | copy-start | bytes 1540
  52.4 10.0 %copy-start.12 = (s32[128]{0:T(128)S(1)}, s32[128]{0:T(128)}, u32[]{:S(2)}) copy-start(s32[128]{0:T(128)} %param.15) | copy-start | bytes 1540
  58.2 0.8 copy-start.5
  59.0 21.4 %collective-permute-start.12 = (bf16[256,1024]{1,0:T(8,128)(2,1)S(1)}, bf16[256,1024]{1,0:T(8,128)(2,1)S(1)}, u32[]{:S(2)}, u32[]{:S(2)}) collective-permute-start(bf16[256,1024]{1,0:T(8,128)(2,1)S(1)} %get-tuple-element.103), channel_id=1, source_target_pairs={{0,4},{4,0},{8,12},{12,8},{1,5},{5,1},{9,13},{13,9},{2,6},{6,2},{1... | collective-permute-start | bytes 1572872 | tf_op jit(solution)/shard_map/ppermute | solution.py:467
  61.5 10.2 %collective-permute-start.11 = (bf16[256,704]{1,0:T(8,128)(2,1)S(1)}, bf16[256,704]{1,0:T(8,128)(2,1)S(1)}, u32[]{:S(2)}, u32[]{:S(2)}) collective-permute-start(bf16[256,704]{1,0:T(8,128)(2,1)S(1)} %get-tuple-element.99), channel_id=1, source_target_pairs={{4,8},{8,4},{5,9},{9,5},{6,10},{10,6},{7,11},{11,7},{20,24},{24,20... | collective-permute-start | bytes 1081352 | tf_op jit(solution)/shard_map/ppermute | solution.py:465
  66.8 15.9 %copy-start.10 = (s32[4]{0:T(128)S(1)}, s32[4]{0:T(128)}, u32[]{:S(2)}) copy-start(s32[4]{0:T(128)} %offsets_ref.1) | copy-start | bytes 52
  69.3 11.9 %collective-permute-start.13 = (bf16[256,1024]{1,0:T(8,128)(2,1)S(1)}, bf16[256,1024]{1,0:T(8,128)(2,1)S(1)}, u32[]{:S(2)}, u32[]{:S(2)}) collective-permute-start(bf16[256,1024]{1,0:T(8,128)(2,1)S(1)} %get-tuple-element.105), channel_id=1, source_target_pairs={{4,8},{8,4},{5,9},{9,5},{6,10},{10,6},{7,11},{11,7},{20,24},{24,20... | collective-permute-start | bytes 1572872 | tf_op jit(solution)/shard_map/ppermute | solution.py:465
  70.0 12.7 %collective-permute-start.14 = (bf16[256,1024]{1,0:T(8,128)(2,1)S(1)}, bf16[256,1024]{1,0:T(8,128)(2,1)S(1)}, u32[]{:S(2)}, u32[]{:S(2)}) collective-permute-start(bf16[256,1024]{1,0:T(8,128)(2,1)S(1)} %get-tuple-element.107.own), channel_id=1, source_target_pairs={{0,2},{2,0},{1,3},{3,1},{4,6},{6,4},{5,7},{7,5},{8,10},{10,8},{9,1... | collective-permute-start | bytes 1572872 | tf_op jit(solution)/shard_map/ppermute | solution.py:463
  71.7 9.5 %copy-start.7 = (bf16[256,704]{1,0:T(8,128)(2,1)}, bf16[256,704]{1,0:T(8,128)(2,1)S(1)}, u32[]{:S(2)}) copy-start(bf16[256,704]{1,0:T(8,128)(2,1)S(1)} %get-tuple-element.126.refs_0_) | copy-start | bytes 1081348
  71.7 16.3 %collective-permute-start.15 = (bf16[256,704]{1,0:T(8,128)(2,1)S(1)}, bf16[256,704]{1,0:T(8,128)(2,1)S(1)}, u32[]{:S(2)}, u32[]{:S(2)}) collective-permute-start(bf16[256,704]{1,0:T(8,128)(2,1)S(1)} %get-tuple-element.110), channel_id=1, source_target_pairs={{0,4},{4,0},{8,12},{12,8},{1,5},{5,1},{9,13},{13,9},{2,6},{6,2},{1... | collective-permute-start | bytes 1081352 | tf_op jit(solution)/shard_map/ppermute | solution.py:467
  80.5 8.4 %collective-permute-start.16 = (bf16[256,1024]{1,0:T(8,128)(2,1)S(1)}, bf16[256,1024]{1,0:T(8,128)(2,1)S(1)}, u32[]{:S(2)}, u32[]{:S(2)}) collective-permute-start(bf16[256,1024]{1,0:T(8,128)(2,1)S(1)} %get-tuple-element.112), channel_id=1, source_target_pairs={{4,8},{8,4},{5,9},{9,5},{6,10},{10,6},{7,11},{11,7},{20,24},{24,20... | collective-permute-start | bytes 1572872 | tf_op jit(solution)/shard_map/ppermute | solution.py:465
  81.4 15.9 %collective-permute-start.17 = (bf16[256,1024]{1,0:T(8,128)(2,1)S(1)}, bf16[256,1024]{1,0:T(8,128)(2,1)S(1)}, u32[]{:S(2)}, u32[]{:S(2)}) collective-permute-start(bf16[256,1024]{1,0:T(8,128)(2,1)S(1)} %get-tuple-element.115.refs_2_), channel_id=1, source_target_pairs={{4,0},{8,12},{5,1},{9,13},{6,2},{10,14},{7,3},{11,15},{20,16},{24,... | collective-permute-start | bytes 1572872 | tf_op jit(solution)/shard_map/ppermute | solution.py:466
  88.1 16.1 %collective-permute-start.18 = (bf16[256,704]{1,0:T(8,128)(2,1)S(1)}, bf16[256,704]{1,0:T(8,128)(2,1)S(1)}, u32[]{:S(2)}, u32[]{:S(2)}) collective-permute-start(bf16[256,704]{1,0:T(8,128)(2,1)S(1)} %get-tuple-element.120), channel_id=1, source_target_pairs={{4,8},{8,4},{5,9},{9,5},{6,10},{10,6},{7,11},{11,7},{20,24},{24,20... | collective-permute-start | bytes 1081352 | tf_op jit(solution)/shard_map/ppermute | solution.py:465
  89.8 21.0 %collective-permute-start.19 = (bf16[256,1024]{1,0:T(8,128)(2,1)}, bf16[256,1024]{1,0:T(8,128)(2,1)}, u32[]{:S(2)}, u32[]{:S(2)}) collective-permute-start(bf16[256,1024]{1,0:T(8,128)(2,1)} %get-tuple-element.123.refs_2_), channel_id=1, source_target_pairs={{4,0},{8,12},{5,1},{9,13},{6,2},{10,14},{7,3},{11,15},{20,16},{24,... | collective-permute-start | bytes 1572872 | tf_op jit(solution)/shard_map/ppermute | solution.py:466
  105.1 14.9 %collective-permute-start.20 = (bf16[256,704]{1,0:T(8,128)(2,1)}, bf16[256,704]{1,0:T(8,128)(2,1)}, u32[]{:S(2)}, u32[]{:S(2)}) collective-permute-start(bf16[256,704]{1,0:T(8,128)(2,1)} %get-tuple-element.127.refs_2_), channel_id=1, source_target_pairs={{4,0},{8,12},{5,1},{9,13},{6,2},{10,14},{7,3},{11,15},{20,16},{24,... | collective-permute-start | bytes 1081352 | tf_op jit(solution)/shard_map/ppermute | solution.py:466
  110.9 1.0 copy-start.6
  111.9 8.1 %copy-start.8 = (bf16[256,704]{1,0:T(8,128)(2,1)S(1)}, bf16[256,704]{1,0:T(8,128)(2,1)}, u32[]{:S(2)}) copy-start(bf16[256,704]{1,0:T(8,128)(2,1)} %copy-done.7) | copy-start | bytes 1081348
  127.5 2.1 %collective-permute-start.21 = (f32[4,16]{1,0:T(4,128)S(1)}, f32[4,16]{1,0:T(4,128)S(1)}, u32[]{:S(2)}, u32[]{:S(2)}) collective-permute-start(f32[4,16]{1,0:T(4,128)S(1)} %maximum_select_fusion), channel_id=1, source_target_pairs={{0,1},{1,0},{2,3},{3,2},{4,5},{5,4},{6,7},{7,6},{8,9},{9,8},{10,11... | collective-permute-start | bytes 776 | tf_op jit(solution)/shard_map/ppermute | solution.py:443
  127.5 3.7 %collective-permute-start.22 = (f32[4,16]{1,0:T(4,128)S(1)}, f32[4,16]{1,0:T(4,128)S(1)}, u32[]{:S(2)}, u32[]{:S(2)}) collective-permute-start(f32[4,16]{1,0:T(4,128)S(1)} %maximum_select_fusion), channel_id=1, source_target_pairs={{0,2},{1,3},{2,0},{3,1},{4,6},{5,7},{6,4},{7,5},{8,10},{9,11},{10,... | collective-permute-start | bytes 776 | tf_op jit(solution)/shard_map/ppermute | solution.py:443
  129.5 3.0 %collective-permute-start.23 = (f32[4,16]{1,0:T(4,128)S(1)}, f32[4,16]{1,0:T(4,128)S(1)}, u32[]{:S(2)}, u32[]{:S(2)}) collective-permute-start(f32[4,16]{1,0:T(4,128)S(1)} %maximum_select_fusion), channel_id=1, source_target_pairs={{0,3},{1,2},{2,1},{3,0},{4,7},{5,6},{6,5},{7,4},{8,11},{9,10},{10,... | collective-permute-start | bytes 776 | tf_op jit(solution)/shard_map/ppermute | solution.py:443
  132.5 3.6 %collective-permute-start.24 = (f32[4,16]{1,0:T(4,128)S(1)}, f32[4,16]{1,0:T(4,128)S(1)}, u32[]{:S(2)}, u32[]{:S(2)}) collective-permute-start(f32[4,16]{1,0:T(4,128)S(1)} %add_add_fusion.1), channel_id=1, source_target_pairs={{0,4},{4,0},{8,12},{12,8},{1,5},{5,1},{9,13},{13,9},{2,6},{6,2},{1... | collective-permute-start | bytes 776 | tf_op jit(solution)/shard_map/ppermute | solution.py:439
  136.1 4.5 %collective-permute-start.25 = (f32[4,16]{1,0:T(4,128)S(1)}, f32[4,16]{1,0:T(4,128)S(1)}, u32[]{:S(2)}, u32[]{:S(2)}) collective-permute-start(f32[4,16]{1,0:T(4,128)S(1)} %add.38), channel_id=1, source_target_pairs={{0,8},{4,12},{8,0},{12,4},{1,9},{5,13},{9,1},{13,5},{2,10},{6,14},... | collective-permute-start | bytes 776 | tf_op jit(solution)/shard_map/ppermute | solution.py:439
